TPU v7x, 32 devices: a whole 2x2x4 slice. The times are simulated.
32 devices in a mesh: grp: 4 (over y, core), ep: 8 (over z, x).
Axes of the slice: x: 2, y: 2, z: 4, core: 2. Of those that a mesh axis runs over, the one named last changes fastest.
Arguments:
- hidden_in: bfloat16 [4096, 2048], P(('grp', 'ep')), may hold values from -6 to 6
- segments: int32 [4096], P('grp'), may hold values from 0 to 71, as said below
- routes: int32 [4096, 4], P('grp'), may hold values from 0 to 7, all different within a row; in each aligned block of 128 rows (0 to 127, 128 to 255, ...) at most 128 rows name the same one
- cotangent: bfloat16 [4096, 2048], P(('grp', 'ep')), may hold values from -6 to 6
- norm1_gain: float32 [2048], replicated, may hold values from 0.5 to 1.5
- w_qkv: bfloat16 [2048, 16, 384], P(None, 'ep'), may hold values from -0.125 to 0.125
- b_qkv: float32 [16, 384], P('ep'), may hold values from -1.75 to 1.75
- w_out: bfloat16 [16, 128, 2048], P('ep'), may hold values from -1 to 1
- norm2_gain: float32 [2048], replicated, may hold values from 0.5 to 1.5
- router: bfloat16 [2048, 8], replicated, may hold values from -0.0625 to 0.0625
- shared_gate_up: bfloat16 [2, 2048, 5632], P(None, None, 'ep'), may hold values from -0.125 to 0.125
- shared_down: bfloat16 [5632, 2048], P('ep'), may hold values from -0.15625 to 0.15625
- shared_gate: bfloat16 [2048], replicated, may hold values from -0.125 to 0.125
- expert_gate_up: bfloat16 [8, 2, 2048, 1408], P('ep'), may hold values from -0.125 to 0.125
- expert_down: bfloat16 [8, 1408, 2048], P('ep'), may hold values from -0.625 to 0.625
Outputs:
- layer_out: bfloat16 [4096, 2048], P(('grp', 'ep'))
- grad_x: float32 [4096, 2048], P(('grp', 'ep'))
- grad_norm1_gain: float32 [2048], replicated
- grad_w_qkv: float32 [2048, 16, 384], P('grp', 'ep')
- grad_b_qkv: float32 [16, 384], P('ep', 'grp')
- grad_w_out: float32 [16, 128, 2048], P('ep', None, 'grp')
- grad_norm2_gain: float32 [2048], replicated
- grad_router: float32 [2048, 8], replicated
- grad_shared_gate_up: float32 [2, 2048, 5632], P(None, 'grp', 'ep')
- grad_shared_down: float32 [5632, 2048], P('ep', 'grp')
- grad_shared_gate: float32 [2048], replicated
- grad_expert_gate_up: float32 [8, 2, 2048, 1408], P('ep', None, 'grp')
- grad_expert_down: float32 [8, 1408, 2048], P('ep', None, 'grp')
Inputs may be any that keep to these rules, and one draw needn't show every extreme that they name: `routes`: each row names 4 different experts. In the rows of one device (aligned blocks of 128 rows) no expert is named by more than 128 rows, a bound that some block reaches of some device in every draw. `segments`: segment numbers never fall. Each sequence of 1024 tokens (those of one index of grp) begins a new document, and its first document has exactly 800 tokens; the others have 60 to 800, but the last of a sequence may be cut shorter. Sequence s numbers its last document (s + 1) * 18 - 1.
All inputs are finite; a program needn't handle non-finite values.
Results may differ from a plain program's by a relative error of at most 0.019.
Values may be sent and summed in bfloat16 or wider, within the bound.
A program may use at most 320 MiB of HBM per device.

v0:
```python
import math

import jax
import jax.numpy as jnp
from jax import lax
from jax.sharding import PartitionSpec as P

EPS = 1e-06
THETA = 1000000.0
NEGATIVE = -1e30
HIGHEST = lax.Precision.HIGHEST


def rms_parts(values):
    factor = lax.rsqrt(jnp.mean(values * values, -1, keepdims=True) + EPS)
    return (values * factor, factor)


def norm_back(grad_out, normal, factor, gain):
    scaled = grad_out * gain
    grad_in = factor * (scaled - normal * jnp.mean(scaled * normal, -1, keepdims=True))
    return (grad_in, jnp.sum(grad_out * normal, 0))


def rope_tables(segment_ids, head_dim):
    token_count = segment_ids.shape[0]
    position = jnp.arange(token_count, dtype=jnp.int32)
    change = jnp.concatenate([jnp.ones((1,), dtype=bool), segment_ids[1:] != segment_ids[:-1]])
    starts = lax.cummax(jnp.where(change, position, 0), axis=0)
    offset = (position - starts).astype(jnp.float32)
    half_dim = head_dim // 2
    inverse = THETA ** (-2.0 * jnp.arange(half_dim, dtype=jnp.float32) / head_dim)
    angles = offset[:, None] * inverse[None, :]
    angles = jnp.concatenate([angles, angles], 1)
    return (jnp.cos(angles), jnp.sin(angles))


def rotate(values, cosine, sine):
    half_dim = values.shape[-1] // 2
    turned = jnp.concatenate([-values[..., half_dim:], values[..., :half_dim]], -1)
    return values * cosine[:, None, :] + turned * sine[:, None, :]


def rotate_back(grads, cosine, sine):
    half_dim = grads.shape[-1] // 2
    sined = grads * sine[:, None, :]
    turned = jnp.concatenate([sined[..., half_dim:], -sined[..., :half_dim]], -1)
    return grads * cosine[:, None, :] + turned


def silu_back(pre_act, grad_act, axis):
    gate_part = jnp.take(pre_act, 0, axis=axis)
    up_part = jnp.take(pre_act, 1, axis=axis)
    sigma = jax.nn.sigmoid(gate_part)
    d_gate = grad_act * up_part * sigma * (1.0 + gate_part * (1.0 - sigma))
    d_up = grad_act * gate_part * sigma
    return jnp.stack([d_gate, d_up], axis)


def expert_forward(expert_input, gate_up, down_proj):
    expert_pre = jnp.einsum(
        "rd,kdf->rkf", expert_input, gate_up, preferred_element_type=jnp.float32
    )
    expert_act = (jax.nn.silu(expert_pre[:, 0]) * expert_pre[:, 1]).astype(jnp.bfloat16)
    return (
        jnp.dot(expert_act, down_proj, preferred_element_type=jnp.float32).astype(jnp.bfloat16),
        expert_pre,
    )


def expert_backward(expert_input, expert_pre, gate_up, down_proj, grad_out):
    expert_act = (jax.nn.silu(expert_pre[:, 0]) * expert_pre[:, 1]).astype(jnp.bfloat16)
    grad_act = jnp.einsum("rd,fd->rf", grad_out, down_proj, preferred_element_type=jnp.float32)
    grad_pre = silu_back(expert_pre, grad_act, 1).astype(jnp.bfloat16)
    grad_down = jnp.einsum("rf,rd->fd", expert_act, grad_out, preferred_element_type=jnp.float32)
    grad_gate_up = jnp.einsum(
        "rd,rkf->kdf", expert_input, grad_pre, preferred_element_type=jnp.float32
    )
    grad_input = jnp.einsum(
        "rkf,kdf->rd", grad_pre, gate_up, preferred_element_type=jnp.float32
    ).astype(jnp.bfloat16)
    return (grad_gate_up, grad_down, grad_input)


def attend_forward(queries, key_rows, values, segment_ids, score_scale):
    seq_length, head_count, head_dim = queries.shape
    block_rows = min(512, seq_length)
    block_count = seq_length // block_rows
    position = jnp.arange(seq_length, dtype=jnp.int32)

    def one_block(pieces):
        query_block, segment_block, position_block = pieces
        scores = (
            jnp.einsum("qhc,khc->hqk", query_block, key_rows, preferred_element_type=jnp.float32)
            * score_scale
        )
        allowed = (segment_block[:, None] == segment_ids[None, :]) & (
            position[None, :] <= position_block[:, None]
        )
        scores = jnp.where(allowed[None], scores, NEGATIVE)
        highest = jnp.max(scores, -1, keepdims=True)
        expo = jnp.exp(scores - highest)
        totals = jnp.sum(expo, -1, keepdims=True)
        weights = (expo / totals).astype(jnp.bfloat16)
        block_out = jnp.einsum(
            "hqk,khc->qhc", weights, values, preferred_element_type=jnp.float32
        ).astype(jnp.bfloat16)
        return (block_out, highest[..., 0] + jnp.log(totals[..., 0]))

    outputs, log_totals = lax.map(
        one_block,
        (
            queries.reshape(block_count, block_rows, head_count, head_dim),
            segment_ids.reshape(block_count, block_rows),
            position.reshape(block_count, block_rows),
        ),
    )
    return (outputs.reshape(seq_length, head_count, head_dim), log_totals)


def attend_backward(queries, key_rows, values, segment_ids, log_totals, grad_attended, score_scale):
    seq_length, head_count, head_dim = queries.shape
    block_rows = min(512, seq_length)
    block_count = seq_length // block_rows
    position = jnp.arange(seq_length, dtype=jnp.int32)

    def one_block(carried, pieces):
        query_block, segment_block, position_block, total_block, grad_block = pieces
        scores = (
            jnp.einsum("qhc,khc->hqk", query_block, key_rows, preferred_element_type=jnp.float32)
            * score_scale
        )
        allowed = (segment_block[:, None] == segment_ids[None, :]) & (
            position[None, :] <= position_block[:, None]
        )
        scores = jnp.where(allowed[None], scores, NEGATIVE)
        weights = jnp.exp(scores - total_block[..., None])
        grad_weights = jnp.einsum(
            "qhc,khc->hqk", grad_block, values, preferred_element_type=jnp.float32
        )
        grad_scores = (
            weights * (grad_weights - jnp.sum(weights * grad_weights, -1, keepdims=True))
        ).astype(jnp.bfloat16)
        grad_query = (
            jnp.einsum("hqk,khc->qhc", grad_scores, key_rows, preferred_element_type=jnp.float32)
            * score_scale
        )
        grad_keys = (
            carried[0]
            + jnp.einsum(
                "hqk,qhc->khc", grad_scores, query_block, preferred_element_type=jnp.float32
            )
            * score_scale
        )
        grad_values = carried[1] + jnp.einsum(
            "hqk,qhc->khc",
            weights.astype(jnp.bfloat16),
            grad_block,
            preferred_element_type=jnp.float32,
        )
        return ((grad_keys, grad_values), grad_query)

    zero_state = jnp.zeros((seq_length, head_count, head_dim), jnp.float32)
    carried, grad_queries = lax.scan(
        one_block,
        (zero_state, zero_state),
        (
            queries.reshape(block_count, block_rows, head_count, head_dim),
            segment_ids.reshape(block_count, block_rows),
            position.reshape(block_count, block_rows),
            log_totals,
            grad_attended.reshape(block_count, block_rows, head_count, head_dim),
        ),
    )
    return (grad_queries.reshape(seq_length, head_count, head_dim), carried[0], carried[1])


def local(
    hidden_in,
    segments,
    routes,
    cotangent,
    norm1_gain,
    w_qkv,
    b_qkv,
    w_out,
    norm2_gain,
    router,
    shared_gate_up,
    shared_down,
    shared_gate,
    expert_gate_up,
    expert_down,
):
    tokens_here, width = hidden_in.shape
    ep_count = lax.axis_size("ep")
    my_index = lax.axis_index("ep")
    top_count = routes.shape[1]
    expert_count = router.shape[1]
    capacity = 2 * tokens_here * top_count // ep_count
    head_dim = b_qkv.shape[1] // 3
    score_scale = 1.0 / math.sqrt(head_dim)
    cosine, sine = rope_tables(segments, head_dim)
    local_gate_up = expert_gate_up[0]
    local_down = expert_down[0]
    expert_width = local_down.shape[0]
    input_f32 = hidden_in.astype(jnp.float32)
    normal_one, factor_one = rms_parts(input_f32)
    normed_one = (normal_one * norm1_gain).astype(jnp.bfloat16)
    group_one = lax.all_gather(normed_one, "ep", axis=0, tiled=True)
    projected = (
        jnp.einsum("td,dhc->thc", group_one, w_qkv, preferred_element_type=jnp.float32) + b_qkv
    )
    queries = rotate(projected[..., :head_dim], cosine, sine).astype(jnp.bfloat16)
    key_rows = rotate(projected[..., head_dim : 2 * head_dim], cosine, sine).astype(jnp.bfloat16)
    values = projected[..., 2 * head_dim :].astype(jnp.bfloat16)
    attended, log_totals = attend_forward(queries, key_rows, values, segments, score_scale)
    piece = attended
    attn_branch = lax.psum_scatter(
        jnp.einsum("thc,hcd->td", piece, w_out, preferred_element_type=jnp.float32),
        "ep",
        scatter_dimension=0,
        tiled=True,
    )
    residual = input_f32 + attn_branch
    normal_two, factor_two = rms_parts(residual)
    normed_two = (normal_two * norm2_gain).astype(jnp.bfloat16)
    group_two = lax.all_gather(normed_two, "ep", axis=0, tiled=True)
    route_probs = jax.nn.softmax(
        jnp.dot(group_two, router, preferred_element_type=jnp.float32), axis=-1
    )
    gate_values = jnp.take_along_axis(route_probs, routes, 1)
    shared_weight = jax.nn.sigmoid(
        jnp.dot(group_two, shared_gate, preferred_element_type=jnp.float32)
    )
    shared_pre = jnp.einsum(
        "td,kdf->ktf", group_two, shared_gate_up, preferred_element_type=jnp.float32
    )
    shared_act = (jax.nn.silu(shared_pre[0]) * shared_pre[1]).astype(jnp.bfloat16)
    shared_part = jnp.dot(shared_act, shared_down, preferred_element_type=jnp.float32)
    flat_routes = routes.reshape(ep_count, tokens_here * top_count)
    one_hot = (flat_routes[..., None] == jnp.arange(expert_count, dtype=jnp.int32)).astype(
        jnp.int32
    )
    ranks = jnp.sum(one_hot * (jnp.cumsum(one_hot, 1) - 1), -1)
    own_routes = lax.dynamic_index_in_dim(flat_routes, my_index, 0, keepdims=False)
    own_ranks = lax.dynamic_index_in_dim(ranks, my_index, 0, keepdims=False)
    targets = own_routes * capacity + own_ranks
    entry_index = jnp.arange(tokens_here * top_count, dtype=jnp.int32)
    send_token = (
        jnp.zeros((expert_count * capacity,), jnp.int32).at[targets].set(entry_index // top_count)
    )
    send_valid = jnp.zeros((expert_count * capacity,), dtype=bool).at[targets].set(True)
    outgoing = jnp.where(
        send_valid[:, None], normed_two[send_token], jnp.zeros((), jnp.bfloat16)
    ).reshape(expert_count, capacity, width)
    piece = lax.all_to_all(outgoing, "ep", split_axis=0, concat_axis=0, tiled=True)
    sources = piece.shape[0]
    slots = piece.shape[1]
    expert_out, expert_pre = expert_forward(piece.reshape(-1, width), local_gate_up, local_down)
    expert_out, expert_pre, arrived = (
        expert_out.reshape(sources, slots, width),
        expert_pre.reshape(sources, slots, 2, expert_width),
        piece,
    )
    returned = lax.all_to_all(expert_out, "ep", split_axis=0, concat_axis=0, tiled=True)
    routed = returned.reshape(-1, width)[targets].reshape(tokens_here, top_count, width)
    own_gates = lax.dynamic_slice_in_dim(gate_values, my_index * tokens_here, tokens_here, 0)
    expert_sum = jnp.sum(own_gates[..., None] * routed.astype(jnp.float32), 1)
    total_part = shared_weight[:, None] * shared_part
    combined = lax.psum_scatter(
        total_part.astype(jnp.bfloat16), "ep", scatter_dimension=0, tiled=True
    ).astype(jnp.float32)
    layer_out = (residual + combined + expert_sum).astype(jnp.bfloat16)
    grad_y = cotangent.astype(jnp.float32)
    group_grad = lax.all_gather(cotangent, "ep", axis=0, tiled=True)
    group_grad_f32 = group_grad.astype(jnp.float32)
    inner = jnp.sum(group_grad_f32 * shared_part, -1)
    grad_share = shared_weight * (1.0 - shared_weight) * inner
    grad_shared_out = (shared_weight[:, None] * group_grad_f32).astype(jnp.bfloat16)
    grad_shared_act = jnp.einsum(
        "td,fd->tf", grad_shared_out, shared_down, preferred_element_type=jnp.float32
    )
    grad_shared_pre = silu_back(shared_pre, grad_shared_act, 0).astype(jnp.bfloat16)
    grad_shared_down = jnp.einsum(
        "tf,td->fd", shared_act, grad_shared_out, preferred_element_type=jnp.float32
    )
    grad_shared_gate_up = jnp.einsum(
        "td,ktf->kdf", group_two, grad_shared_pre, preferred_element_type=jnp.float32
    )
    grad_shared_gate = jnp.dot(grad_share, group_two.astype(jnp.float32), precision=HIGHEST)
    extra_part = grad_share[:, None] * shared_gate.astype(jnp.float32)[None, :]
    router_f32 = router.astype(jnp.float32)
    own_probs = lax.dynamic_slice_in_dim(route_probs, my_index * tokens_here, tokens_here, 0)
    grad_gates = jnp.sum(routed.astype(jnp.float32) * grad_y[:, None, :], -1)
    grad_expert = (
        (own_gates[..., None] * grad_y[:, None, :])
        .astype(jnp.bfloat16)
        .reshape(tokens_here * top_count, width)
    )
    send_grad = (
        jnp.zeros((expert_count * capacity, width), jnp.bfloat16)
        .at[targets]
        .set(grad_expert)
        .reshape(expert_count, capacity, width)
    )
    arrived_grad = lax.all_to_all(send_grad, "ep", split_axis=0, concat_axis=0, tiled=True)
    grad_gate_up, grad_down, grad_input = expert_backward(
        arrived.reshape(-1, width),
        expert_pre.reshape(-1, 2, expert_width),
        local_gate_up,
        local_down,
        arrived_grad.reshape(-1, width),
    )
    returned_grad = lax.all_to_all(
        grad_input.reshape(ep_count, capacity, width), "ep", split_axis=0, concat_axis=0, tiled=True
    )
    expert_grad_in = jnp.sum(
        returned_grad.reshape(-1, width)[targets]
        .reshape(tokens_here, top_count, width)
        .astype(jnp.float32),
        1,
    )
    own_hot = (
        own_routes.reshape(tokens_here, top_count)[..., None]
        == jnp.arange(expert_count, dtype=jnp.int32)
    ).astype(jnp.float32)
    dense_grad = jnp.sum(own_hot * grad_gates[..., None], 1)
    grad_logits = own_probs * (dense_grad - jnp.sum(own_probs * dense_grad, -1, keepdims=True))
    router_grad_in = jnp.dot(grad_logits, router_f32.T, precision=HIGHEST)
    grad_router = jnp.dot(normed_two.astype(jnp.float32).T, grad_logits, precision=HIGHEST)
    piece = grad_shared_pre
    grad_normed_two = lax.psum_scatter(
        (
            jnp.einsum("ktf,kdf->td", piece, shared_gate_up, preferred_element_type=jnp.float32)
            + extra_part
        ).astype(jnp.bfloat16),
        "ep",
        scatter_dimension=0,
        tiled=True,
    ).astype(jnp.float32)
    grad_normed_two = grad_normed_two + expert_grad_in + router_grad_in
    grad_residual_norm, grad_norm2 = norm_back(grad_normed_two, normal_two, factor_two, norm2_gain)
    grad_residual = grad_y + grad_residual_norm
    group_attn_grad = lax.all_gather(grad_residual.astype(jnp.bfloat16), "ep", axis=0, tiled=True)
    grad_w_out = jnp.einsum(
        "thc,td->hcd", attended, group_attn_grad, preferred_element_type=jnp.float32
    )
    grad_attended = jnp.einsum(
        "td,hcd->thc", group_attn_grad, w_out, preferred_element_type=jnp.float32
    ).astype(jnp.bfloat16)
    grad_queries, grad_keys, grad_values = attend_backward(
        queries, key_rows, values, segments, log_totals, grad_attended, score_scale
    )
    grad_qkv = jnp.concatenate(
        [
            rotate_back(grad_queries, cosine, sine),
            rotate_back(grad_keys, cosine, sine),
            grad_values,
        ],
        -1,
    ).astype(jnp.bfloat16)
    grad_b_qkv = jnp.sum(grad_qkv.astype(jnp.float32), 0)
    grad_w_qkv = jnp.einsum("td,thc->dhc", group_one, grad_qkv, preferred_element_type=jnp.float32)
    piece = grad_qkv
    grad_normed_one = lax.psum_scatter(
        jnp.einsum("thc,dhc->td", piece, w_qkv, preferred_element_type=jnp.float32).astype(
            jnp.bfloat16
        ),
        "ep",
        scatter_dimension=0,
        tiled=True,
    ).astype(jnp.float32)
    grad_input_norm, grad_norm1 = norm_back(grad_normed_one, normal_one, factor_one, norm1_gain)
    grad_x = grad_residual + grad_input_norm
    shards = (
        lax.psum_scatter(
            grad_gate_up[None].astype(jnp.bfloat16), "grp", scatter_dimension=2, tiled=True
        ).astype(jnp.float32),
        lax.psum_scatter(
            grad_down[None].astype(jnp.bfloat16), "grp", scatter_dimension=2, tiled=True
        ).astype(jnp.float32),
        lax.psum_scatter(
            grad_w_qkv.astype(jnp.bfloat16), "grp", scatter_dimension=0, tiled=True
        ).astype(jnp.float32),
        lax.psum_scatter(
            grad_b_qkv.astype(jnp.bfloat16), "grp", scatter_dimension=1, tiled=True
        ).astype(jnp.float32),
        lax.psum_scatter(
            grad_w_out.astype(jnp.bfloat16), "grp", scatter_dimension=2, tiled=True
        ).astype(jnp.float32),
        lax.psum_scatter(
            grad_shared_gate_up.astype(jnp.bfloat16), "grp", scatter_dimension=1, tiled=True
        ).astype(jnp.float32),
        lax.psum_scatter(
            grad_shared_down.astype(jnp.bfloat16), "grp", scatter_dimension=1, tiled=True
        ).astype(jnp.float32),
    )
    common = lax.psum((grad_norm1, grad_norm2, grad_router, grad_shared_gate), ("grp", "ep"))
    return (
        layer_out,
        grad_x,
        common[0],
        shards[2],
        shards[3],
        shards[4],
        common[1],
        common[2],
        shards[5],
        shards[6],
        common[3],
        shards[0],
        shards[1],
    )


def solution(mesh):
    in_specs = (
        P(("grp", "ep"), None),
        P("grp"),
        P("grp", None),
        P(("grp", "ep"), None),
        P(),
        P(None, "ep", None),
        P("ep", None),
        P("ep", None, None),
        P(),
        P(),
        P(None, None, "ep"),
        P("ep", None),
        P(),
        P("ep", None, None, None),
        P("ep", None, None),
    )
    out_specs = (
        P(("grp", "ep"), None),
        P(("grp", "ep"), None),
        P(),
        P("grp", "ep", None),
        P("ep", "grp"),
        P("ep", None, "grp"),
        P(),
        P(),
        P(None, "grp", "ep"),
        P("ep", "grp"),
        P(),
        P("ep", None, "grp", None),
        P("ep", None, "grp"),
    )
    return jax.shard_map(local, mesh=mesh, in_specs=in_specs, out_specs=out_specs, check_vma=False)
```

profile of v0, /device:TPU:0, one launch (start us, length us, event | category | flops | bytes accessed | tf_op | source)
XLA Modules:
  0.0 1594.2 jit_solution(2896442369933589407)
XLA Ops:
  15.8 71.2 %all-gather.5.cloned.1.call-done = bf16[1024,2048]{1,0:T(8,128)(2,1)} async-done(((bf16[128,2048]{1,0:T(8,128)(2,1)}), bf16[1024,2048]{1,0:T(8,128)(2,1)}) %all-gather.5.cloned.1.call-update) | async-done | bytes 4194320 | tf_op jit(solution)/shard_map/all_gather | solution.py:210
  87.0 5.3 fusion.108
  97.5 4.1 fusion.130
  107.9 13.3 while.32
  121.2 5.9 convolution_bitcast_fusion
  127.5 147.2 %reduce-scatter.14.cloned.1.call-done = f32[128,2048]{1,0:T(8,128)} async-done(((f32[1024,2048]{1,0:T(8,128)}), f32[128,2048]{1,0:T(8,128)}) %reduce-scatter.14.cloned.1.call-update) | async-done | bytes 1048592 | tf_op jit(solution)/shard_map/reduce_scatter | solution.py:219
  281.9 9.0 reduce-window.19
  296.5 9.9 gather_fusion
  306.4 4.6 broadcast_select_fusion
  311.0 4.7 all-to-all-start
  319.8 4.2 mul.396
  324.1 5.3 mul.397
  330.0 53.5 %all-gather.7.cloned.1.call-done = bf16[1024,2048]{1,0:T(8,128)(2,1)} async-done(((bf16[128,2048]{1,0:T(8,128)(2,1)}), bf16[1024,2048]{1,0:T(8,128)(2,1)}) %all-gather.7.cloned.1.call-update) | async-done | bytes 4194320 | tf_op jit(solution)/shard_map/all_gather | solution.py:228
  383.5 3.4 fusion.163
  387.0 24.5 %gather_fusion.3 = f32[4096]{0:T(1024)S(1)} fusion(f32[1024,8]{0,1:T(8,128)S(1)} %fusion.139, s32[4096]{0:T(1024)S(1)} %reshape.569), kind=kCustom, calls=%fused_computation.3 | custom fusion | bytes 65536 | tf_op jit(solution)/shard_map/jit(take_along_axis)/gather | solution.py:232
  414.7 7.9 scatter_custom_fusion.2
  422.6 3.5 fusion.168
  426.2 9.8 fusion.99
  436.0 18.6 %all-to-all-done = bf16[8,128,2048]{2,1,0:T(8,128)(2,1)} async-done(((bf16[8,128,2048]{2,1,0:T(8,128)(2,1)}), bf16[8,128,2048]{2,1,0:T(8,128)(2,1)}, u32[]{:S(2)}, u32[]{:S(2)}) %all-to-all-start) | async-done | bytes 4194336 | tf_op jit(solution)/shard_map/all_to_all | solution.py:257
  454.6 14.2 all-to-all-start.2
  468.8 58.6 %all-gather.9.cloned.1.call-done = bf16[1024,2048]{1,0:T(8,128)(2,1)} async-done(((bf16[128,2048]{1,0:T(8,128)(2,1)}), bf16[1024,2048]{1,0:T(8,128)(2,1)}) %all-gather.9.cloned.1.call-update) | async-done | bytes 4194320 | tf_op jit(solution)/shard_map/all_gather | solution.py:276
  527.4 10.7 fusion.118
  538.1 5.9 fusion.55
  544.1 17.3 %fusion.52 = f32[1024,2,1408]{2,0,1:T(8,128)S(1)} fusion(bf16[1024,2048,1]{1,0,2:T(8,128)(2,1)} %bitcast.19, bf16[1,2,2048,1408]{3,2,1,0:T(8,128)(2,1)} %param.40), kind=kOutput, calls=%fused_computation.68 | convolution fusion | flops 11811160064 | bytes 27262976 | tf_op jit(solution)/shard_map/rd,kdf->rkf/dot_general | solution.py:61
  567.3 8.2 fusion.84
  575.5 8.7 all-to-all-done.2
  584.2 15.9 all-to-all-start.1
  600.1 11.9 fusion.56
  612.0 14.1 fusion.93
  628.7 16.3 %bitcast_convert_fusion.1 = bf16[1024,2048]{1,0:T(8,128)(2,1)} fusion(bf16[1,2,2048,1408]{3,2,1,0:T(8,128)(2,1)} %param.40, bf16[1024,1,1408]{2,0,1:T(8,128)(2,1)S(1)} %get-tuple-element.515, bf16[1024,1,1408]{2,0,1:T(8,128)(2,1)S(1)} %get-tuple-element.514), kind=kOutput, calls=%fused_computation.76 | convolution fusion | flops 11816140800 | bytes 21495808 | tf_op jit(solution)/shard_map/rkf,kdf->rd/dot_general | solution.py:79
  645.0 82.3 %all-to-all-done.1 = bf16[8,128,2048]{2,1,0:T(8,128)(2,1)} async-done(((bf16[8,128,2048]{2,1,0:T(8,128)(2,1)}), bf16[8,128,2048]{2,1,0:T(8,128)(2,1)}, u32[]{:S(2)}, u32[]{:S(2)}) %all-to-all-start.1) | async-done | bytes 4194336 | tf_op jit(solution)/shard_map/all_to_all | solution.py:266
  727.3 4.5 all-to-all-start.3
  734.9 8.1 gather_fusion.1
  743.1 4.7 reshape.541
  747.8 6.8 multiply_reduce_fusion.1
  754.7 86.6 %all-to-all-done.3 = bf16[8,128,2048]{2,1,0:T(8,128)(2,1)} async-done(((bf16[8,128,2048]{2,1,0:T(8,128)(2,1)}), bf16[8,128,2048]{2,1,0:T(8,128)(2,1)}, u32[]{:S(2)}, u32[]{:S(2)}) %all-to-all-start.3) | async-done | bytes 4194336 | tf_op jit(solution)/shard_map/all_to_all | solution.py:315
  841.3 8.0 gather_fusion.2
  849.2 4.7 reshape.542
  853.9 5.8 reduce_sum.162
  866.7 7.5 convolution_convert_fusion.1
  874.2 10.6 convert_bitcast_fusion.1
  884.9 10.5 fusion.57
  895.9 43.0 %all-gather.11.cloned.1.call-done = bf16[1024,2048]{1,0:T(8,128)(2,1)} async-done(((bf16[128,2048]{1,0:T(8,128)(2,1)}), bf16[1024,2048]{1,0:T(8,128)(2,1)}) %all-gather.11.cloned.1.call-update) | async-done | bytes 4194320 | tf_op jit(solution)/shard_map/all_gather | solution.py:345
  938.9 4.6 fusion.119
  943.5 49.3 %while.33 = (s32[]{:T(128)}, f32[1024,2,128]{0,2,1:T(8,128)}, f32[1024,2,128]{0,2,1:T(8,128)}, f32[2,512,2,128]{1,0,3,2:T(2,128)}, bf16[2,512,2,128]{3,1,2,0:T(8...) while((s32[]{:T(128)}, f32[1024,2,128]{0,2,1:T(8,128)}, ...), condition=%wide.region_28.33_spmd.clone, body=%wide.region_26.32_spmd.clone.sunk | while | flops 1360919552 | bytes 51425568 | solution.py:164
  956.5 10.4 dynamic_update_slice.22
  969.4 3.6 fusion.237
  982.3 10.5 dynamic_update_slice.22
  1003.9 4.6 fusion.96
  1008.7 7.9 fusion.87
  1016.7 6.7 bitcast_convert_fusion
  1024.1 18.3 %convert_bitcast_fusion = bf16[1,2,2048,1408]{2,3,1,0:T(8,128)(2,1)} fusion(bf16[1024,2048,1]{1,0,2:T(8,128)(2,1)} %bitcast.19, bf16[1024,1,1408]{2,0,1:T(8,128)(2,1)} %copy-done.51, bf16[1024,1,1408]{2,0,1:T(8,128)(2,1)} %copy-done.50), kind=kOutput, calls=%fused_computation.70 | convolution fusion | flops 11819810816 | bytes 21495808 | tf_op jit(solution)/shard_map/rd,rkf->kdf/dot_general | solution.py:76
  1043.1 4.0 fusion.169
  1055.2 37.1 %reduce-scatter.32.cloned.1.call-done = bf16[1,1408,512]{2,1,0:T(8,128)(2,1)} async-done(((bf16[1,1408,2048]{2,1,0:T(8,128)(2,1)}), bf16[1,1408,512]{2,1,0:T(8,128)(2,1)}) %reduce-scatter.32.cloned.1.call-update) | async-done | bytes 1441808 | tf_op jit(solution)/shard_map/reduce_scatter | solution.py:380
  1095.6 18.6 %reduce-scatter.34.cloned.1.call-done = bf16[96,2]{1,0:T(8,128)(2,1)} async-done(((bf16[384,2]{1,0:T(8,128)(2,1)}), bf16[96,2]{1,0:T(8,128)(2,1)}) %reduce-scatter.34.cloned.1.call-update) | async-done | bytes 400
  1115.6 26.8 %reduce-scatter.24.cloned.1.call-done = bf16[2,128,512]{2,1,0:T(8,128)(2,1)} async-done(((bf16[2,128,2048]{2,1,0:T(8,128)(2,1)}), bf16[2,128,512]{2,1,0:T(8,128)(2,1)}) %reduce-scatter.24.cloned.1.call-update) | async-done | bytes 262160 | tf_op jit(solution)/shard_map/reduce_scatter | solution.py:389
  1144.3 38.6 %reduce-scatter.22.cloned.1.call-done = bf16[512,2,384]{2,0,1:T(8,128)(2,1)} async-done(((bf16[2048,2,384]{2,0,1:T(8,128)(2,1)}), bf16[512,2,384]{2,0,1:T(8,128)(2,1)}) %reduce-scatter.22.cloned.1.call-update) | async-done | bytes 786448 | tf_op jit(solution)/shard_map/reduce_scatter | solution.py:383
  1185.9 88.9 %reduce-scatter.20.cloned.1.call-done = bf16[128,2048]{1,0:T(8,128)(2,1)} async-done(((bf16[1024,2048]{1,0:T(8,128)(2,1)}), bf16[128,2048]{1,0:T(8,128)(2,1)}) %reduce-scatter.20.cloned.1.call-update) | async-done | bytes 524304 | tf_op jit(solution)/shard_map/reduce_scatter | solution.py:366
  1276.5 89.7 %reduce-scatter.16.cloned.1.call-done = bf16[128,2048]{1,0:T(8,128)(2,1)} async-done(((bf16[1024,2048]{1,0:T(8,128)(2,1)}), bf16[128,2048]{1,0:T(8,128)(2,1)}) %reduce-scatter.16.cloned.1.call-update) | async-done | bytes 524304 | tf_op jit(solution)/shard_map/reduce_scatter | solution.py:271
  1366.2 4.1 fusion.124
  1370.3 41.2 %all-reduce = (f32[2048]{0:T(1024)}, f32[2048]{0:T(1024)}, f32[2048]{0:T(1024)}) all-reduce(f32[2048]{0:T(1024)S(1)} %get-tuple-element.457, f32[2048]{0:T(1024)S(1)} %copy-done.35, f32[2048]{0:T(1024)S(1)} %bitcast.316), channel_id=1, replica_groups=mesh['grp'=4,'ep'=8] {'grp','ep'}, use_global_device_ids=true, to_apply=%region_32.37 | all-reduce | flops 6144 | bytes 49152 | tf_op jit(solution)/shard_map/psum | solution.py:399
  1411.5 50.0 %reduce-scatter.30.cloned.1.call-done = bf16[1,2,512,1408]{2,3,1,0:T(8,128)(2,1)} async-done(((bf16[1,2,2048,1408]{2,3,1,0:T(8,128)(2,1)}), bf16[1,2,512,1408]{2,3,1,0:T(8,128)(2,1)}) %reduce-scatter.30.cloned.1.call-update) | async-done | bytes 2883600 | tf_op jit(solution)/shard_map/reduce_scatter | solution.py:377
  1461.5 5.1 copy.196
  1466.6 119.4 %all-reduce.3.cloned.1.call-done = f32[2048,8]{0,1:T(8,128)} async-done(((f32[2048,8]{0,1:T(8,128)}), f32[2048,8]{0,1:T(8,128)}) %all-reduce.3.cloned.1.call-update) | async-done | bytes 65552 | tf_op jit(solution)/shard_map/psum | solution.py:399
  (280 shorter events, 131.3 us)
Async XLA Ops:
  7.2 79.8 %copy-start = (bf16[2048,2,384]{2,1,0:T(2,128)(2,1)S(1)}, bf16[2048,2,384]{2,1,0:T(2,128)(2,1)}, u32[]{:S(2)}) copy-start(bf16[2048,2,384]{2,1,0:T(2,128)(2,1)} %param.32) | copy-start | bytes 9437188
  7.2 79.8 %all-gather.5.cloned.1.call-start = ((), (), s32[]{:S(2)}) async-start(), calls=%async_computation.15 | async-start | bytes 4718592 | tf_op jit(solution)/shard_map/all_gather | solution.py:210
  8.6 4.0 copy-start.45
  10.7 263.9 %reduce-scatter.14.cloned.1.call-start = ((), (), s32[]{:S(2)}) async-start(), calls=%async_computation.16 | async-start | bytes 9437184 | tf_op jit(solution)/shard_map/reduce_scatter | solution.py:219
  97.5 10.4 copy-start.20
  108.5 3.5 copy-start.6
  108.5 3.5 copy-start.15
  115.2 3.5 copy-start.6
  115.2 3.5 copy-start.15
  121.2 5.9 copy-start.22
  121.2 5.9 copy-start.24
  121.2 5.9 copy-start.33
  127.1 150.1 %copy-start.29 = (f32[2048]{0:T(1024)S(1)}, f32[2048]{0:T(1024)}, u32[]{:S(2)}) copy-start(f32[2048]{0:T(1024)} %param.35) | copy-start | bytes 24580
  127.1 151.0 %copy-start.26 = (s32[1024,4]{0,1:T(4,128)S(1)}, s32[1024,4]{0,1:T(4,128)}, u32[]{:S(2)}) copy-start(s32[1024,4]{0,1:T(4,128)} %param.29) | copy-start | bytes 49156
  127.1 256.4 %all-gather.7.cloned.1.call-start = ((), (), s32[]{:S(2)}) async-start(), calls=%async_computation.17 | async-start | bytes 4718592 | tf_op jit(solution)/shard_map/all_gather | solution.py:228
  280.5 25.9 %copy-start.31 = (s32[8,512]{1,0:T(8,128)}, s32[8,512]{1,0:T(8,128)S(1)}, u32[]{:S(2)}) copy-start(s32[8,512]{1,0:T(8,128)S(1)} %reshape.444) | copy-start | bytes 49156
  291.5 2.5 copy-start.42
  311.0 5.3 copy-start.39
  311.0 143.6 %all-to-all-start = ((bf16[8,128,2048]{2,1,0:T(8,128)(2,1)}), bf16[8,128,2048]{2,1,0:T(8,128)(2,1)}, u32[]{:S(2)}, u32[]{:S(2)}) async-start(bf16[8,128,2048]{2,1,0:T(8,128)(2,1)} %broadcast_select_fusion), calls=%async_computation.2 | async-start | bytes 8388608 | tf_op jit(solution)/shard_map/all_to_all | solution.py:257
  315.7 211.7 %all-gather.9.cloned.1.call-start = ((), (), s32[]{:S(2)}) async-start(), calls=%async_computation.19 | async-start | bytes 4718592 | tf_op jit(solution)/shard_map/all_gather | solution.py:276
  324.1 59.5 %copy-start.27 = (bf16[2048,8]{0,1:T(8,128)(2,1)S(1)}, bf16[2048,8]{0,1:T(8,128)(2,1)}, u32[]{:S(2)}) copy-start(bf16[2048,8]{0,1:T(8,128)(2,1)} %param.36) | copy-start | bytes 98308
  387.0 27.7 %copy-start.43 = (s32[512,1]{0,1:T(1,128)S(1)}, s32[512,1]{0,1:T(1,128)}, u32[]{:S(2)}) copy-start(s32[512,1]{0,1:T(1,128)} %copy-done.42) | copy-start | bytes 6148
  414.7 8.0 copy-start.36
  422.6 3.5 copy-start.2
  454.6 129.6 %all-to-all-start.2 = ((bf16[8,128,2048]{2,1,0:T(8,128)(2,1)}), bf16[8,128,2048]{2,1,0:T(8,128)(2,1)}, u32[]{:S(2)}, u32[]{:S(2)}) async-start(bf16[8,128,2048]{2,1,0:T(8,128)(2,1)} %bitcast.303), calls=%async_computation.5 | async-start | bytes 8388608 | tf_op jit(solution)/shard_map/all_to_all | solution.py:307
  527.4 10.7 copy-start.47
  527.4 10.7 copy-start.48
  538.1 6.0 copy-start.49
  538.1 29.2 %slice-start = ((s8[5767168]{0:T(1024)(128)(4,1)}), s8[4194304]{0:T(1024)(128)(4,1)S(1)}, s32[]{:S(2)}) async-start(s8[5767168]{0:T(1024)(128)(4,1)} %bitcast.324), calls=%async_computation.31 | async-start | bytes 8388608
  544.1 56.0 %copy-start.37 = (f32[1024]{0:T(1024)}, f32[1024]{0:T(1024)S(1)}, u32[]{:S(2)}) copy-start(f32[1024]{0:T(1024)S(1)} %fusion.143) | copy-start | bytes 12292
  544.1 23.2 %slice-start.1 = ((s8[5767168]{0:T(1024)(128)(4,1)}), s8[1572864]{0:T(1024)(128)(4,1)S(1)}, s32[]{:S(2)}) async-start(s8[5767168]{0:T(1024)(128)(4,1)} %bitcast.324), calls=%async_computation.32 | async-start | bytes 3145728
  561.4 4.3 copy-start.8
  584.2 15.9 copy-start.44
  584.2 143.1 %all-to-all-start.1 = ((bf16[8,128,2048]{2,1,0:T(8,128)(2,1)}), bf16[8,128,2048]{2,1,0:T(8,128)(2,1)}, u32[]{:S(2)}, u32[]{:S(2)}) async-start(bf16[8,128,2048]{2,1,0:T(8,128)(2,1)} %bitcast.305), calls=%async_computation.3 | async-start | bytes 8388608 | tf_op jit(solution)/shard_map/all_to_all | solution.py:266
  600.0 259.7 %reduce-scatter.18.cloned.1.call-start = ((), (), s32[]{:S(2)}) async-start(), calls=%async_computation.20 | async-start | bytes 4718592 | tf_op jit(solution)/shard_map/reduce_scatter | solution.py:333
  626.1 2.5 copy-start.51
  727.3 114.0 %all-to-all-start.3 = ((bf16[8,128,2048]{2,1,0:T(8,128)(2,1)}), bf16[8,128,2048]{2,1,0:T(8,128)(2,1)}, u32[]{:S(2)}, u32[]{:S(2)}) async-start(bf16[8,128,2048]{2,1,0:T(8,128)(2,1)} %bitcast.304), calls=%async_computation.6 | async-start | bytes 8388608 | tf_op jit(solution)/shard_map/all_to_all | solution.py:315
  731.8 207.1 %all-gather.11.cloned.1.call-start = ((), (), s32[]{:S(2)}) async-start(), calls=%async_computation.21 | async-start | bytes 4718592 | tf_op jit(solution)/shard_map/all_gather | solution.py:345
  853.9 5.8 copy-start.28
  853.9 5.8 copy-start.30
  853.9 5.8 copy-start.41
  859.8 4.4 copy-start.5
  866.4 180.7 %reduce-scatter.28.cloned.1.call-start = ((), (), s32[]{:S(2)}) async-start(), calls=%async_computation.27 | async-start | bytes 3604480 | tf_op jit(solution)/shard_map/reduce_scatter | solution.py:395
  874.1 177.7 %reduce-scatter.26.cloned.1.call-start = ((), (), s32[]{:S(2)}) async-start(), calls=%async_computation.26 | async-start | bytes 7208960 | tf_op jit(solution)/shard_map/reduce_scatter | solution.py:392
  884.8 207.5 %reduce-scatter.32.cloned.1.call-start = ((), (), s32[]{:S(2)}) async-start(), calls=%async_computation.29 | async-start | bytes 7208960 | tf_op jit(solution)/shard_map/reduce_scatter | solution.py:380
  895.4 218.8 %reduce-scatter.34.cloned.1.call-start = ((), (), s32[]{:S(2)}) async-start(), calls=%async_computation.30 | async-start | bytes 122880
  895.9 47.6 %copy-start.21 = (s32[1024]{0:T(1024)S(1)}, s32[1024]{0:T(1024)}, u32[]{:S(2)}) copy-start(s32[1024]{0:T(1024)} %param.28) | copy-start | bytes 12292
  895.9 47.6 %copy-start.23 = (s32[2,512]{1,0:T(2,128)S(1)}, s32[2,512]{1,0:T(2,128)}, u32[]{:S(2)}) copy-start(s32[2,512]{1,0:T(2,128)} %copy-done.22) | copy-start | bytes 12292
  895.9 47.6 %copy-start.25 = (s32[2,512]{1,0:T(2,128)S(1)}, s32[2,512]{1,0:T(2,128)}, u32[]{:S(2)}) copy-start(s32[2,512]{1,0:T(2,128)} %copy-done.24) | copy-start | bytes 12292
  895.9 47.6 %copy-start.34 = (f32[2,2,512]{2,1,0:T(2,128)S(1)}, f32[2,2,512]{2,1,0:T(2,128)}, u32[]{:S(2)}) copy-start(f32[2,2,512]{2,1,0:T(2,128)} %copy-done.33) | copy-start | bytes 24580
  943.5 2.5 copy-start.13
  950.1 2.9 copy-start.3
  969.4 3.7 copy-start.7
  974.8 2.9 copy-start.3
  997.3 4.5 copy-start.17
  1003.9 138.6 %reduce-scatter.24.cloned.1.call-start = ((), (), s32[]{:S(2)}) async-start(), calls=%async_computation.24 | async-start | bytes 1310720 | tf_op jit(solution)/shard_map/reduce_scatter | solution.py:389
  1008.5 174.3 %reduce-scatter.22.cloned.1.call-start = ((), (), s32[]{:S(2)}) async-start(), calls=%async_computation.23 | async-start | bytes 3932160 | tf_op jit(solution)/shard_map/reduce_scatter | solution.py:383
  1016.7 258.1 %reduce-scatter.20.cloned.1.call-start = ((), (), s32[]{:S(2)}) async-start(), calls=%async_computation.22 | async-start | bytes 4718592 | tf_op jit(solution)/shard_map/reduce_scatter | solution.py:366
  1023.5 342.7 %reduce-scatter.16.cloned.1.call-start = ((), (), s32[]{:S(2)}) async-start(), calls=%async_computation.18 | async-start | bytes 4718592 | tf_op jit(solution)/shard_map/reduce_scatter | solution.py:271
  1024.0 437.5 %reduce-scatter.30.cloned.1.call-start = ((), (), s32[]{:S(2)}) async-start(), calls=%async_computation.28 | async-start | bytes 14417920 | tf_op jit(solution)/shard_map/reduce_scatter | solution.py:377
  1042.4 543.6 %all-reduce.3.cloned.1.call-start = ((), (), s32[]{:S(2)}) async-start(), calls=%async_computation.25 | async-start | bytes 131072 | tf_op jit(solution)/shard_map/psum | solution.py:399
  1055.2 219.6 %copy-start.32 = (f32[2048]{0:T(1024)S(1)}, f32[2048]{0:T(1024)}, u32[]{:S(2)}) copy-start(f32[2048]{0:T(1024)} %param.31) | copy-start | bytes 24580
  1055.2 219.6 %copy-start.46 = (f32[128]{0:T(128)S(1)}, f32[128]{0:T(128)}, u32[]{:S(2)}) copy-start(f32[128]{0:T(128)} %copy-done.45) | copy-start | bytes 1540
  1185.9 184.4 %copy-start.35 = (f32[2048]{0:T(1024)S(1)}, f32[2048]{0:T(1024)}, u32[]{:S(2)}) copy-start(f32[2048]{0:T(1024)} %get-tuple-element.455) | copy-start | bytes 24580
  (17 other events, 25.2 us)
Sparse Core Ops, SparseCore 0:
  10.8 76.1 all-gather.4
  127.3 147.3 reduce-scatter.13
  278.2 105.2 all-gather.6
  385.7 141.6 all-gather.8
  612.2 168.4 reduce-scatter.17
  866.5 72.3 all-gather.10
  942.0 34.6 reduce-scatter.27
  980.0 54.8 reduce-scatter.25
  1037.4 54.8 reduce-scatter.31
  1094.7 19.5 reduce-scatter.33
  1117.5 24.8 reduce-scatter.23
  1144.8 37.9 reduce-scatter.21
  1186.9 87.8 reduce-scatter.19
  1278.3 87.8 reduce-scatter.15
  1368.8 92.6 reduce-scatter.29
  1468.4 117.5 all-reduce.2
where the time goes:
time: 1610 us; the launch traced here: 1590 us
  waiting for transfers between devices  1040 us (65%)
  matrix products  221 us (14%)
  local copies, waits for them, and re-layouts  147 us (9%)
  other arithmetic  88.9 us (6%)
  starting transfers between devices  41.3 us (3%)
  blocking collectives  41.2 us (3%)
    reduce_scatter x1, waiting for transfers between devices, local(): lax.psum_scatter(jnp.einsum('thc,hcd->td', piece, w_out, preferred_elemen...  147 us
    psum x1, waiting for transfers between devices, local(): lax.psum((grad_norm1, grad_norm2, grad_router, grad_shared_gate), ('grp',...  119 us
    reduce_scatter x1, waiting for transfers between devices, local(): lax.psum_scatter(total_part.astype(jnp.bfloat16), 'ep', scatter_dimension...  89.7 us
    reduce_scatter x1, waiting for transfers between devices, local(): lax.psum_scatter(jnp.einsum('thc,dhc->td', piece, w_qkv, preferred_elemen...  88.9 us
    all_to_all x1, waiting for transfers between devices, local(): lax.all_to_all(grad_input.reshape(ep_count, capacity, width), 'ep', split...  86.6 us
    all_to_all x1, waiting for transfers between devices, local(): lax.all_to_all(expert_out, 'ep', split_axis=0, concat_axis=0, tiled=True)  82.3 us
    all_gather x1, waiting for transfers between devices, local(): group_one = lax.all_gather(normed_one, 'ep', axis=0, tiled=True)  71.2 us
    all_gather x1, waiting for transfers between devices, local(): group_grad = lax.all_gather(cotangent, 'ep', axis=0, tiled=True)  58.6 us
  transfers between devices with their start and end apart: 20, of which 17 were waited for; matrix products, arithmetic and copies ran while one was open for 25% of the time, Pallas kernels for 0%

commit v1 on v0

v1 whole, which is shorter than its diff:
```python
import functools
import math

import jax
import jax.numpy as jnp
from jax import lax
from jax.experimental import pallas as pl
from jax.experimental.pallas import tpu as pltpu
from jax.sharding import PartitionSpec as P

EPS = 1e-06
THETA = 1000000.0
NEGATIVE = -1e30
BF16 = jnp.bfloat16
F32 = jnp.float32
LANES = 128
MIB = 1024 * 1024
KERNEL_COST = pl.CostEstimate(flops=10**6, bytes_accessed=10**5, transcendentals=0)


def dot(lhs, rhs):
    return jnp.dot(lhs, rhs, preferred_element_type=F32)


def dot_nt(lhs, rhs):
    return lax.dot_general(lhs, rhs, (((1,), (1,)), ((), ())), preferred_element_type=F32)


def dot_tn(lhs, rhs):
    return lax.dot_general(lhs, rhs, (((0,), (0,)), ((), ())), preferred_element_type=F32)


def tied(*arrays):
    return lax.optimization_barrier(arrays)


def sum_all(value, axes):
    for axis in axes:
        size = lax.axis_size(axis)
        step = 1
        while step < size:
            value = value + lax.ppermute(value, axis, [(i, i ^ step) for i in range(size)])
            step *= 2
    return value


class GrpReduce:
    def __init__(self, rows, produce):
        self.rows, self.produce = rows, produce
        self.size = lax.axis_size("grp")
        self.planes = self.size // 2
        mine = lax.axis_index("grp")
        self.core, self.plane = mine % 2, mine // 2
        self.far = [(self.plane + k) % self.planes for k in range(1, self.planes)]

    def after(self, token):
        self.rows = tied(self.rows, token)[0]

    def to_partner(self, value):
        return lax.ppermute(value, "grp", [(i, i ^ 1) for i in range(self.size)])

    def away(self):
        return [
            self.produce(self.rows, 2 * plane + 1 - self.core).astype(BF16) for plane in self.far
        ]

    def pass_on(self, arrived):
        return [
            (self.produce(self.rows, 2 * plane + self.core) + value.astype(F32)).astype(BF16)
            for plane, value in zip(self.far, arrived)
        ]

    def to_planes(self, values):
        sent = []
        for k, value in enumerate(values):
            shift = 2 * (k + 1)
            pairs = [(j, (j + shift) % self.size) for j in range(self.size)]
            sent.append(lax.ppermute(value, "grp", pairs))
        return sent

    def own(self):
        away = self.produce(self.rows, 2 * self.plane + 1 - self.core).astype(BF16)
        kept = self.produce(self.rows, 2 * self.plane + self.core)
        return kept + self.to_partner(away).astype(F32)


def add_all(value, others):
    for other in others:
        value = value + other.astype(F32)
    return value


def flat_tied(first, groups):
    flat = [value for group in groups for value in group]
    first, *flat = tied(first, *flat)
    result = []
    for group in groups:
        result.append(flat[: len(group)])
        flat = flat[len(group) :]
    return first, result


def columns_of(array, member):
    size = array.shape[1] // lax.axis_size("grp")
    return lax.dynamic_slice_in_dim(array, member * size, size, 1)


MESH = pl.DeviceIdType.MESH


def ring_places(count):
    here = lax.axis_index("ep")
    if count != 8:
        return here, lambda spot: spot
    x, z = here % 2, here // 2

    def index_at(spot):
        side = spot // 4
        return 2 * (spot + side * (7 - 2 * spot)) + side

    return z + x * (7 - 2 * z), index_at


def slot_index(count, slot):
    place, index_at = ring_places(count)
    offset = jnp.where(slot == count - 1, count // 2, (slot // 2 + 1) * (2 * (slot % 2) - 1))
    offset = jnp.where(slot == count - 2, 0, offset)
    return index_at((place + offset + count) % count)


def when(condition):
    if isinstance(condition, bool):
        return (lambda run: run()) if condition else (lambda run: None)
    return pl.when(condition)


def rows_at(slot, size):
    return pl.ds(pl.multiple_of(slot * size, size), size)


class KernelRing:
    def __init__(self, buffer, count, size, send_sems, recv_sems):
        place, index_at = ring_places(count)
        self.buffer, self.count, self.size = buffer, count, size
        self.half = count // 2
        self.send_sems, self.recv_sems = send_sems, recv_sems
        self.right = index_at((place + 1) % count)
        self.left = index_at((place + count - 1) % count)

    def own(self):
        return slice((self.count - 2) * self.size, (self.count - 1) * self.size)

    def copy(self, source, target, neighbour, step, way):
        return pltpu.make_async_remote_copy(
            src_ref=self.buffer.at[source],
            dst_ref=self.buffer.at[target],
            send_sem=self.send_sems.at[step, way],
            recv_sem=self.recv_sems.at[step, way],
            device_id={"ep": neighbour},
            device_id_type=MESH,
        )

    def sends(self, step):
        before = lax.rem(step + self.half - 1, self.half)
        copies = []
        for way, neighbour in enumerate((self.right, self.left)):
            source = jnp.where(step == 0, self.count - 2, 2 * before + way)
            copies.append(
                self.copy(
                    rows_at(source, self.size), rows_at(2 * step + way, self.size),
                    neighbour, step, way,
                )
            )
        return copies

    def last_sends(self):
        middle = self.size // 2
        copies = []
        for way, neighbour in enumerate((self.right, self.left)):
            source = (self.count - 4 + way) * self.size + way * middle
            target = (self.count - 1) * self.size + way * middle
            copies.append(
                self.copy(
                    pl.ds(source, middle), pl.ds(target, middle), neighbour, self.half - 1, way
                )
            )
        return copies

    def start(self):
        for copy in self.sends(0):
            copy.start()

    def arrive(self, i):
        @when(i < self.half - 1)
        def _():
            for copy in self.sends(i):
                copy.wait_recv()

        @when(i == self.half - 1)
        def _():
            for copy in self.last_sends():
                copy.wait_recv()

    def forward(self, i):
        @when(i < self.half - 2)
        def _():
            for copy in self.sends(i + 1):
                copy.start()

        @when(i == self.half - 2)
        def _():
            for copy in self.last_sends():
                copy.start()

    def finish(self):
        for step in range(self.half - 1):
            for copy in self.sends(step):
                copy.wait_send()
        for copy in self.last_sends():
            copy.wait_send()


class Exchange:
    def __init__(self, count, source_at, target_at, send_sems, recv_sems):
        self.count = count
        self.place, self.index_at = ring_places(count)
        self.source_at, self.target_at = source_at, target_at
        self.send_sems, self.recv_sems = send_sems, recv_sems

    def copy(self, slot):
        way = slot % 2
        far = slot // 2 + 1
        farthest = slot == self.count - 1
        offset = jnp.where(farthest, self.count // 2, far * (2 * way - 1))
        landing = jnp.where(farthest, slot, slot + 1 - 2 * way)
        return pltpu.make_async_remote_copy(
            src_ref=self.source_at(slot),
            dst_ref=self.target_at(landing),
            send_sem=self.send_sems.at[slot],
            recv_sem=self.recv_sems.at[landing],
            device_id={"ep": self.index_at((self.place + offset + self.count) % self.count)},
            device_id_type=MESH,
        )

    def arrived(self, slot):
        return pltpu.make_async_remote_copy(
            src_ref=self.source_at(slot),
            dst_ref=self.target_at(slot),
            send_sem=self.send_sems.at[slot],
            recv_sem=self.recv_sems.at[slot],
            device_id={"ep": self.index_at((self.place + 1) % self.count)},
            device_id_type=MESH,
        )

    def others(self):
        return [slot for slot in range(self.count) if slot != self.count - 2]


def greet(axis, count):
    barrier = pltpu.get_barrier_semaphore()
    here = lax.axis_index(axis)
    for step in range(1, count):
        pl.semaphore_signal(
            barrier, inc=1, device_id={axis: (here + step) % count}, device_id_type=MESH
        )


def block_rows_of(count):
    return 256 if count % 256 == 0 else 128


def attend_forward_kernel(
    count, grp_count, heads, scale, hidden, first_gain, gain, w, b, segments, row_segments, w_out,
    q_out, k_out, v_out, attended_out, log_out, residual_out, normed_out, cosine, sine, starts,
    x_out, w_all_out, row_positions, xs, w_all, received, x_send, x_recv, w_send, w_recv, plane_send, plane_recv, core_send,
    core_recv, hand_send, hand_recv, x_sems, w_sems, own_sem,
):
    size, width = hidden.shape
    half = count // 2
    rows = 2 * size
    dim = LANES
    inner_size = heads * dim
    planes = grp_count // 2
    mine = lax.axis_index("grp")
    core, plane = mine % 2, mine // 2
    part_width = width // grp_count

    own_columns = pl.ds(pl.multiple_of(mine * part_width, part_width), part_width)
    ring_x = KernelRing(xs, count, size, x_send, x_recv)
    ring_w = KernelRing(w_all.at[0], count, inner_size, w_send, w_recv)
    load = pltpu.make_async_copy(
        w_out.at[:, own_columns], w_all.at[0, ring_w.own()], own_sem.at[0]
    )
    load.start()
    greet("ep", count)
    greet("grp", grp_count)
    own_hidden = hidden[...].astype(F32)
    mean = jnp.sum(own_hidden * own_hidden, -1, keepdims=True) * (1.0 / width)
    xs[ring_x.own(), :] = (own_hidden * lax.rsqrt(mean + EPS) * first_gain[...]).astype(BF16)
    pl.semaphore_wait(pltpu.get_barrier_semaphore(), count - 1 + grp_count - 1)
    ring_x.start()
    load.wait()
    ring_w.start()

    for slot in range(count):
        row_positions[:, slot * size : (slot + 1) * size] = slot_index(
            count, slot
        ) * size + lax.broadcasted_iota(jnp.int32, (1, size), 1)
    lane = lax.broadcasted_iota(jnp.int32, (size, dim), 1)
    low_half = lane < dim // 2
    index = jnp.where(low_half, lane, lane - dim // 2).astype(F32)
    inverse = jnp.exp(index * (-2.0 * math.log(THETA) / dim))

    def tables(slot, carry):
        block = slot_index(count, slot)
        here, there = rows_at(slot, size), rows_at(block, size)
        before = jnp.where(row_segments[...] < segments[there, :], 1.0, 0.0)
        start = jnp.sum(before, -1, keepdims=True)
        starts[here, :] = start.astype(jnp.int32)
        position = (block * size + lax.broadcasted_iota(jnp.int32, (size, 1), 0)).astype(F32)
        angle = (position - start) * inverse
        cosine[here, :] = jnp.cos(angle)
        sine[here, :] = jnp.where(low_half, -jnp.sin(angle), jnp.sin(angle))
        return carry

    lax.fori_loop(0, count, tables, 0)

    def to_plane(step, i):
        here = rows_at(i, 2 * inner_size)
        landing = (planes - step) % planes
        return pltpu.make_async_remote_copy(
            src_ref=w_all.at[0, here],
            dst_ref=w_all.at[landing, here],
            send_sem=plane_send.at[step - 1, i],
            recv_sem=plane_recv.at[landing - 1, i],
            device_id={"grp": (mine + 2 * step) % grp_count},
            device_id_type=MESH,
        )

    def to_core(j):
        return pltpu.make_async_remote_copy(
            src_ref=w_all.at[j],
            dst_ref=w_all.at[planes + j],
            send_sem=core_send.at[j],
            recv_sem=core_recv.at[j],
            device_id={"grp": mine + 1 - 2 * core},
            device_id_type=MESH,
        )

    def store_x(i):
        here = rows_at(i, rows)
        return pltpu.make_async_copy(xs.at[here], x_out.at[here], x_sems.at[i])

    def store_w(j):
        return pltpu.make_async_copy(w_all.at[j], w_all_out.at[j], w_sems.at[j])

    def project(i, carry):
        here = rows_at(i, rows)
        ring_x.arrive(i)
        ring_x.forward(i)
        store_x(i).start()
        ring_w.arrive(i)
        ring_w.forward(i)
        for step in range(1, planes):
            to_plane(step, i).start()
        projected = dot(xs[here, :], w[...]) + b[...]
        cos, sin = cosine[here, :], sine[here, :]
        for h in range(heads):
            base = 3 * dim * h
            query = projected[:, base : base + dim]
            key = projected[:, base + dim : base + 2 * dim]
            q_out[h, here, :] = (query * cos + pltpu.roll(query, dim // 2, 1) * sin).astype(BF16)
            k_out[h, here, :] = (key * cos + pltpu.roll(key, dim // 2, 1) * sin).astype(BF16)
            v_out[h, here, :] = projected[:, base + 2 * dim : base + 3 * dim].astype(BF16)
        return carry

    lax.fori_loop(0, half, project, 0)
    to_core(0).start()
    store_w(0).start()

    exchange = Exchange(
        count,
        lambda slot: attended_out.at[rows_at(slot, size)],
        lambda slot: received.at[slot],
        hand_send,
        hand_recv,
    )

    def attend(step, carry):
        i = half - 1 - step
        here = rows_at(i, rows)
        count_up = lax.broadcasted_iota(jnp.int32, (size, 1), 0)
        own = jnp.concatenate(
            [slot_index(count, 2 * i + k) * size + count_up for k in range(2)], 0
        )
        start = starts[here, :]
        keys_at = row_positions[...]
        allowed = (keys_at <= own) & (keys_at >= start)
        for h in range(heads):
            scores = dot_nt(q_out[h, here, :], k_out[h]) * scale
            scores = jnp.where(allowed, scores, NEGATIVE)
            highest = jnp.max(scores, -1, keepdims=True)
            expo = jnp.exp(scores - highest)
            total = jnp.sum(expo, -1, keepdims=True)
            weights = (expo * (1.0 / total)).astype(BF16)
            attended_out[here, h * dim : (h + 1) * dim] = dot(weights, v_out[h]).astype(BF16)
            log_out[h, here, :] = highest + jnp.log(total)
        exchange.copy(2 * i + 1).start()

        @pl.when(i < half - 1)
        def _():
            exchange.copy(2 * i).start()

        return carry

    lax.fori_loop(0, half, attend, 0)
    received[count - 2] = attended_out[ring_x.own(), :]
    for j in range(1, planes):
        for i in range(half):
            to_plane((planes - j) % planes, i).wait_recv()
        to_core(j).start()
        store_w(j).start()
    for slot in exchange.others():
        exchange.arrived(slot).wait_recv()
    for j in range(planes):
        to_core(j).wait_recv()
        store_w(planes + j).start()
    mixed = jnp.concatenate([received[slot] for slot in range(count)], 1)
    square = jnp.zeros((size, 1), F32)
    for j in range(grp_count):
        member = 2 * ((plane + j % planes) % planes) + (core if j < planes else 1 - core)
        columns = pl.ds(pl.multiple_of(member * part_width, part_width), part_width)
        piece = hidden[:, columns].astype(F32) + dot(mixed, w_all[j])
        residual_out[:, columns] = piece
        square = square + jnp.sum(piece * piece, -1, keepdims=True)
    factor = lax.rsqrt(square * (1.0 / width) + EPS)
    normed_out[...] = (residual_out[...] * factor * gain[...]).astype(BF16)

    for i in range(half):
        store_x(i).wait()
        for step in range(1, planes):
            to_plane(step, i).wait_send()
    for j in range(grp_count):
        store_w(j).wait()
    for j in range(planes):
        to_core(j).wait_send()
    for slot in exchange.others():
        exchange.copy(slot).wait_send()
    ring_x.finish()
    ring_w.finish()


def attend_forward(
    count, grp_count, hidden, first_gain, gain, w, b, w_out, segments, scale
):
    size, width = hidden.shape
    tokens = size * count
    heads = w.shape[1] // (3 * LANES)
    half, planes = count // 2, grp_count // 2
    anywhere = pl.BlockSpec(memory_space=pl.ANY)
    whole = pl.BlockSpec(memory_space=pltpu.VMEM)
    shape = jax.ShapeDtypeStruct
    w_all_shape = (grp_count, count * heads * LANES, width // grp_count)
    dma = pltpu.SemaphoreType.DMA
    return pl.pallas_call(
        functools.partial(attend_forward_kernel, count, grp_count, heads, scale),
        in_specs=[whole] * 7 + [anywhere],
        out_specs=[whole] * 10 + [anywhere] * 2,
        out_shape=(
            shape((heads, tokens, LANES), BF16),
            shape((heads, tokens, LANES), BF16),
            shape((heads, tokens, LANES), BF16),
            shape((tokens, heads * LANES), BF16),
            shape((heads, tokens, 1), F32),
            shape((size, width), F32),
            shape((size, width), BF16),
            shape((tokens, LANES), F32),
            shape((tokens, LANES), F32),
            shape((tokens, 1), jnp.int32),
            shape((tokens, width), BF16),
            shape(w_all_shape, BF16),
        ),
        scratch_shapes=[
            pltpu.VMEM((1, tokens), jnp.int32),
            pltpu.VMEM((tokens, width), BF16),
            pltpu.VMEM(w_all_shape, BF16),
            pltpu.VMEM((count, size, heads * LANES), BF16),
            dma((half, 2)),
            dma((half, 2)),
            dma((half, 2)),
            dma((half, 2)),
            dma((max(planes - 1, 1), half)),
            dma((max(planes - 1, 1), half)),
            dma((planes,)),
            dma((planes,)),
            dma((count,)),
            dma((count,)),
            dma((half,)),
            dma((grp_count,)),
            dma((1,)),
        ],
        compiler_params=pltpu.CompilerParams(
            collective_id=1, has_side_effects=True, vmem_limit_bytes=56 * MIB
        ),
        cost_estimate=KERNEL_COST,
        name="attend_forward",
    )(hidden, first_gain[None, :], gain[None, :], w, b, segments[:, None], segments[None, :], w_out)


def attend_backward_kernel(
    count, grp_count, heads, scale, g_own, w_all, w, cosine, sine, q, k, v, row_logs, row_starts,
    g_out, bias_out, branch_out, group_out, row_positions, positions, g_att, dk, dv, outbox, gs,
    send_sems, recv_sems, ring_send, ring_recv, store_sems,
):
    size, width = g_own.shape
    tokens = size * count
    rows = block_rows_of(tokens)
    dim = LANES
    inner_size = heads * dim
    planes = grp_count // 2
    mine = lax.axis_index("grp")
    core, plane = mine % 2, mine // 2
    part_width = width // grp_count

    ring = KernelRing(gs, count, size, ring_send, ring_recv)

    def store(i):
        here = rows_at(i, 2 * size)
        return pltpu.make_async_copy(gs.at[here], group_out.at[here], store_sems.at[i])

    def next_pair(i):
        ring.arrive(i)
        ring.forward(i)
        store(i).start()

    greet("ep", count)
    gs[ring.own(), :] = g_own[...]
    for slot in range(count):
        first = slot_index(count, slot) * size
        row_positions[:, slot * size : (slot + 1) * size] = first + lax.broadcasted_iota(
            jnp.int32, (1, size), 1
        )
        positions[slot * size : (slot + 1) * size, :] = first + lax.broadcasted_iota(
            jnp.int32, (size, 1), 0
        )
    own_rows = None
    for j in range(grp_count):
        member = 2 * ((plane + j % planes) % planes) + (core if j < planes else 1 - core)
        columns = pl.ds(pl.multiple_of(member * part_width, part_width), part_width)
        piece = dot_nt(g_own[:, columns], w_all[j])
        own_rows = piece if own_rows is None else own_rows + piece
    own_rows = own_rows.astype(BF16)
    for slot in range(count):
        outbox[slot] = own_rows[:, slot * inner_size : (slot + 1) * inner_size]
    exchange = Exchange(
        count,
        lambda slot: outbox.at[slot],
        lambda slot: g_att.at[rows_at(slot, size)],
        send_sems,
        recv_sems,
    )
    pl.semaphore_wait(pltpu.get_barrier_semaphore(), count - 1)
    for slot in exchange.others():
        exchange.copy(slot).start()
    ring.start()
    g_att[(count - 2) * size : (count - 1) * size, :] = outbox[count - 2]
    dk[...] = jnp.zeros_like(dk)
    dv[...] = jnp.zeros_like(dv)
    for slot in exchange.others():
        exchange.arrived(slot).wait_recv()

    def scores_back(i, carry):
        here = rows_at(i, rows)
        own, start = row_positions[:, here], row_starts[:, here]
        keys_at = positions[...]
        allowed = (keys_at <= own) & (keys_at >= start)
        cos, sin = cosine[here, :], sine[here, :]
        for h in range(heads):
            query = q[h, here, :]
            g_block = g_att[here, h * dim : (h + 1) * dim]
            scores = dot_nt(k[h], query) * scale - row_logs[h, :, here]
            weights = jnp.exp(jnp.where(allowed, scores, NEGATIVE))
            g_weights = dot_nt(v[h], g_block)
            inner = jnp.sum(weights * g_weights, 0, keepdims=True)
            g_scores = (weights * (g_weights - inner)).astype(BF16)
            g_query = dot_tn(g_scores, k[h]) * scale
            g_query = g_query * cos - pltpu.roll(g_query, dim // 2, 1) * sin
            g_out[here, 3 * dim * h : 3 * dim * h + dim] = g_query.astype(BF16)
            dk[h] += dot(g_scores, query)
            dv[h] += dot(weights.astype(BF16), g_block)

        @pl.when(i == 1)
        def _():
            next_pair(0)

        return carry

    lax.fori_loop(0, tokens // rows, scores_back, 0)
    next_pair(1)
    bias_out[...] = jnp.zeros_like(bias_out)

    def finish(i, carry):
        here = rows_at(i, rows)
        cos, sin = cosine[here, :], sine[here, :]
        for h in range(heads):
            base = 3 * dim * h
            g_key = dk[h, here, :] * scale
            g_key = g_key * cos - pltpu.roll(g_key, dim // 2, 1) * sin
            g_out[here, base + dim : base + 2 * dim] = g_key.astype(BF16)
            g_out[here, base + 2 * dim : base + 3 * dim] = dv[h, here, :].astype(BF16)
        g_here = g_out[here, :]
        bias_out[...] += jnp.sum(g_here.astype(F32), 0, keepdims=True)
        branch_out[here, :] = dot_nt(g_here, w[...]).astype(BF16)
        return carry

    lax.fori_loop(0, tokens // rows, finish, 0)
    for i in range(2, count // 2):
        next_pair(i)
    for slot in exchange.others():
        exchange.copy(slot).wait_send()
    ring.finish()
    for i in range(count // 2):
        store(i).wait()


def attend_backward(
    count, grp_count, g_own, w_all, w, cosine, sine, q, k, v, logs, starts, scale
):
    size, width = g_own.shape
    heads, tokens, _ = q.shape
    whole = pl.BlockSpec(memory_space=pltpu.VMEM)
    shape = jax.ShapeDtypeStruct
    dma = pltpu.SemaphoreType.DMA
    return pl.pallas_call(
        functools.partial(attend_backward_kernel, count, grp_count, heads, scale),
        in_specs=[whole] * 10,
        out_specs=[whole] * 3 + [pl.BlockSpec(memory_space=pl.ANY)],
        out_shape=(
            shape((tokens, 3 * LANES * heads), BF16),
            shape((1, 3 * LANES * heads), F32),
            shape((tokens, width), BF16),
            shape((tokens, width), BF16),
        ),
        scratch_shapes=[
            pltpu.VMEM((1, tokens), jnp.int32),
            pltpu.VMEM((tokens, 1), jnp.int32),
            pltpu.VMEM((tokens, heads * LANES), BF16),
            pltpu.VMEM((heads, tokens, LANES), F32),
            pltpu.VMEM((heads, tokens, LANES), F32),
            pltpu.VMEM((count, size, heads * LANES), BF16),
            pltpu.VMEM((tokens, width), BF16),
            dma((count,)),
            dma((count,)),
            dma((count // 2, 2)),
            dma((count // 2, 2)),
            dma((count // 2,)),
        ],
        compiler_params=pltpu.CompilerParams(
            collective_id=2, has_side_effects=True, vmem_limit_bytes=56 * MIB
        ),
        cost_estimate=KERNEL_COST,
        name="attend_backward",
    )(
        g_own, w_all, w, cosine, sine, q, k, v,
        logs.reshape(heads, 1, tokens), starts.reshape(1, tokens),
    )


def reduce_kernel(count, number, *refs):
    parts, outs = refs[:number], refs[number : 2 * number]
    to_right = refs[2 * number : 3 * number]
    to_left = refs[3 * number : 4 * number]
    send_sems, recv_sems = refs[4 * number :]
    half = count // 2
    size = outs[0].shape[0]
    middle = size // 2
    place, index_at = ring_places(count)
    neighbours = (index_at((place + 1) % count), index_at((place + count - 1) % count))
    barrier = pltpu.get_barrier_semaphore()
    for neighbour in neighbours:
        pl.semaphore_signal(barrier, inc=1, device_id={"ep": neighbour}, device_id_type=MESH)
    pl.semaphore_wait(barrier, 2)

    def copy(a, step, way):
        held = (to_right, to_left)[way][a]
        if step == 0:
            cut = pl.ds(way * middle, middle)
            source = parts[a].at[pl.ds((count - 1) * size + way * middle, middle)]
            target = held.at[0, cut]
        else:
            source, target = held.at[step - 1], held.at[step]
        return pltpu.make_async_remote_copy(
            src_ref=source,
            dst_ref=target,
            send_sem=send_sems.at[a, step, way],
            recv_sem=recv_sems.at[a, step, way],
            device_id={"ep": neighbours[way]},
            device_id_type=MESH,
        )

    for a in range(number):
        for way in range(2):
            copy(a, 0, way).start()
    for step in range(1, half):
        far = half - step
        for a in range(number):
            for way in range(2):
                held = (to_right, to_left)[way][a]
                first = (2 * far - 1 - way) * size
                copy(a, step - 1, way).wait_recv()
                if step == 1:
                    here = slice(way * middle, (way + 1) * middle)
                    rest = slice((1 - way) * middle, (2 - way) * middle)
                    own = parts[a][first + way * middle : first + (way + 1) * middle, :]
                    held[0, here] = (own.astype(F32) + held[0, here].astype(F32)).astype(BF16)
                    held[0, rest] = parts[a][
                        first + (1 - way) * middle : first + (2 - way) * middle, :
                    ]
                else:
                    own = parts[a][first : first + size, :]
                    held[step - 1] = (own.astype(F32) + held[step - 1].astype(F32)).astype(BF16)
                copy(a, step, way).start()
    for a in range(number):
        own = parts[a][(count - 2) * size : (count - 1) * size, :].astype(F32)
        for way in range(2):
            copy(a, half - 1, way).wait_recv()
            own = own + (to_right, to_left)[way][a][half - 1].astype(F32)
        outs[a][...] = own
    for a in range(number):
        for step in range(half):
            for way in range(2):
                copy(a, step, way).wait_send()


def reduce_rows(count, call, *parts):
    tokens, width = parts[0].shape
    size, number, half = tokens // count, len(parts), count // 2
    return pl.pallas_call(
        functools.partial(reduce_kernel, count, number),
        in_specs=[pl.BlockSpec(memory_space=pltpu.VMEM)] * number,
        out_specs=[pl.BlockSpec(memory_space=pltpu.VMEM)] * number,
        out_shape=[jax.ShapeDtypeStruct((size, width), F32)] * number,
        scratch_shapes=[pltpu.VMEM((half, size, width), BF16)] * (2 * number)
        + [pltpu.SemaphoreType.DMA((number, half, 2))] * 2,
        compiler_params=pltpu.CompilerParams(
            collective_id=call, has_side_effects=True, vmem_limit_bytes=56 * MIB
        ),
        cost_estimate=KERNEL_COST,
        name="reduce_rows",
    )(*parts)


def tiles_of(width):
    tiles, start = [], 0
    while width - start > 384:
        tiles.append((start, 256))
        start += 256
    tiles.append((start, width - start))
    return tiles


def experts_kernel(
    count, expert_count, x_own, cot_own, routes, routes_w, gate_up_e, down_e, gate_up_s, down_s,
    act_e_out, grad_e_out, act_s_out, grad_s_out, part_out, branch_out, logits_out, x_out,
    cot_out,
    xs, cots, gate_e, up_e, held_e, gate_s, up_s, held_s, act_e, grad_e, act_s, grad_s, part,
    branch, logits_held, x_send, x_recv, cot_send, cot_recv, weight_sems, out_sems, x_sems,
):
    half = count // 2
    size = x_own.shape[0]
    rows = 2 * size
    ring_x = KernelRing(xs, count, size, x_send, x_recv)
    ring_cot = KernelRing(cots, count, size, cot_send, cot_recv)

    barrier = pltpu.get_barrier_semaphore()
    for neighbour in (ring_x.left, ring_x.right):
        pl.semaphore_signal(barrier, inc=1, device_id={"ep": neighbour}, device_id_type=MESH)
    loads = [
        pltpu.make_async_copy(source, target, weight_sems.at[i])
        for i, (source, target) in enumerate(
            [
                (gate_up_e.at[0, 0], gate_e),
                (gate_up_e.at[0, 1], up_e),
                (down_e.at[0], held_e),
                (gate_up_s.at[0], gate_s),
                (gate_up_s.at[1], up_s),
                (down_s, held_s),
            ]
        )
    ]
    for load in loads:
        load.start()
    xs[ring_x.own(), :] = x_own[...]
    cots[ring_x.own(), :] = cot_own[...]
    pl.semaphore_wait(barrier, 2)
    ring_x.start()
    ring_cot.start()

    def stores(i):
        here = rows_at(i, rows)
        slot = lax.rem(i, 2)
        pieces = [
            (act_e.at[slot], act_e_out.at[here]),
            (grad_e.at[slot, 0], grad_e_out.at[0, here]),
            (grad_e.at[slot, 1], grad_e_out.at[1, here]),
            (act_s.at[slot], act_s_out.at[here]),
            (grad_s.at[slot, 0], grad_s_out.at[0, here]),
            (grad_s.at[slot, 1], grad_s_out.at[1, here]),
            (part.at[slot], part_out.at[here]),
            (branch.at[slot], branch_out.at[here]),
            (logits_held.at[slot], logits_out.at[here]),
        ]
        return [
            pltpu.make_async_copy(source, target, out_sems.at[slot, k])
            for k, (source, target) in enumerate(pieces)
        ]

    def store_rows(i):
        here = rows_at(i, rows)
        return [
            pltpu.make_async_copy(xs.at[here], x_out.at[here], x_sems.at[0, i]),
            pltpu.make_async_copy(cots.at[here], cot_out.at[here], x_sems.at[1, i]),
        ]

    sections = (
        (gate_e, up_e, held_e, act_e, grad_e, dot, dot_nt),
        (gate_s, up_s, held_s, act_s, grad_s, dot_nt, dot),
    )
    mine = lax.axis_index("ep")
    onehot = (lax.broadcasted_iota(jnp.int32, (1, LANES), 1) == mine).astype(F32)

    def one_pair(i, carry):
        slot = lax.rem(i, 2)
        here = rows_at(i, rows)
        ring_x.arrive(i)
        ring_x.forward(i)
        ring_cot.arrive(i)
        ring_cot.forward(i)
        for copy in store_rows(i):
            copy.start()

        @pl.when(i == 0)
        def _():
            for load in loads:
                load.wait()

        @pl.when(i >= 2)
        def _():
            for copy in stores(i - 2):
                copy.wait()

        lane = lax.broadcasted_iota(jnp.int32, (rows, LANES), 1)
        inputs, cotangent = xs[here, :], cots[here, :]
        logits = dot(inputs, routes_w[...])
        routed = jnp.where(lane < expert_count, logits, NEGATIVE)
        expo = jnp.exp(routed - jnp.max(routed, -1, keepdims=True))
        probs = expo * (1.0 / jnp.sum(expo, -1, keepdims=True))
        named = jnp.concatenate(
            [routes[rows_at(slot_index(count, 2 * i + k), size), :] for k in range(2)], 0
        )
        hits = jnp.sum(jnp.where(named == mine, 1.0, 0.0), -1, keepdims=True)
        own_prob = jnp.sum(probs * onehot, -1, keepdims=True) * hits
        share_logit = jnp.sum(jnp.where(lane == expert_count, logits, 0.0), -1, keepdims=True)
        share = 1.0 / (1.0 + jnp.exp(-share_logit))

        inner = []
        total, out_total = None, None
        for s, (gate_w, up_w, down_w, act_out, grad_out, ahead, back_dot) in enumerate(sections):
            factor = own_prob if s == 0 else share
            dots = jnp.zeros((rows, 1), F32)
            for start, width in tiles_of(down_w.shape[0]):
                cut = pl.ds(start, width)
                piece = (slice(None), cut) if s == 0 else (cut, slice(None))
                gate = ahead(inputs, gate_w[piece])
                up = ahead(inputs, up_w[piece])
                grad = dot_nt(cotangent, down_w[cut, :])
                sigma = 0.5 * jnp.tanh(0.5 * gate) + 0.5
                silu = gate * sigma
                act = (silu * up).astype(BF16).astype(F32)
                dots = dots + jnp.sum(grad * act, -1, keepdims=True)
                scaled = grad * factor
                act_out[slot, :, cut] = (act * factor).astype(BF16)
                grad_out[slot, 0, :, cut] = (
                    scaled * up * (sigma + silu * (1.0 - sigma))
                ).astype(BF16)
                grad_out[slot, 1, :, cut] = (scaled * silu).astype(BF16)
            inner.append(dots)
            back = back_dot(grad_out[slot, 0], gate_w[...]) + back_dot(
                grad_out[slot, 1], up_w[...]
            )
            total = back if total is None else total + back
            out_piece = dot(act_out[slot], down_w[...])
            out_total = out_piece if out_total is None else out_total + out_piece
        branch[slot] = out_total.astype(BF16)
        grad_logits = own_prob * inner[0] * (onehot - probs)
        grad_share = share * (1.0 - share) * inner[1]
        grad_logits = grad_logits + jnp.where(lane == expert_count, grad_share, 0.0)
        high = grad_logits.astype(BF16)
        low = (grad_logits - high.astype(F32)).astype(BF16)
        total = total + dot_nt(high, routes_w[...]) + dot_nt(low, routes_w[...])
        logits_held[slot, :, :LANES] = high
        logits_held[slot, :, LANES:] = low
        part[slot] = total.astype(BF16)
        for copy in stores(i):
            copy.start()
        return carry

    lax.fori_loop(0, half, one_pair, 0)
    for i in range(half):
        for copy in store_rows(i):
            copy.wait()
    for i in range(max(half - 2, 0), half):
        for copy in stores(i):
            copy.wait()
    ring_x.finish()
    ring_cot.finish()


def experts(
    count, expert_count, x_own, cot_own, routes, routes_w, gate_up_e, down_e, gate_up_s, down_s
):
    size, width = x_own.shape
    tokens, rows, half = size * count, 2 * size, count // 2
    wide, narrow = down_e.shape[1], down_s.shape[0]
    anywhere = pl.BlockSpec(memory_space=pl.ANY)
    whole = pl.BlockSpec(memory_space=pltpu.VMEM)
    shape = jax.ShapeDtypeStruct
    dma = pltpu.SemaphoreType.DMA
    return pl.pallas_call(
        functools.partial(experts_kernel, count, expert_count),
        in_specs=[whole] * 4 + [anywhere] * 4,
        out_specs=[anywhere] * 9,
        out_shape=(
            shape((tokens, wide), BF16),
            shape((2, tokens, wide), BF16),
            shape((tokens, narrow), BF16),
            shape((2, tokens, narrow), BF16),
            shape((tokens, width), BF16),
            shape((tokens, width), BF16),
            shape((tokens, 2 * LANES), BF16),
            shape((tokens, width), BF16),
            shape((tokens, width), BF16),
        ),
        scratch_shapes=[
            pltpu.VMEM((tokens, width), BF16),
            pltpu.VMEM((tokens, width), BF16),
            pltpu.VMEM((width, wide), BF16),
            pltpu.VMEM((width, wide), BF16),
            pltpu.VMEM((wide, width), BF16),
            pltpu.VMEM((narrow, width), BF16),
            pltpu.VMEM((narrow, width), BF16),
            pltpu.VMEM((narrow, width), BF16),
            pltpu.VMEM((2, rows, wide), BF16),
            pltpu.VMEM((2, 2, rows, wide), BF16),
            pltpu.VMEM((2, rows, narrow), BF16),
            pltpu.VMEM((2, 2, rows, narrow), BF16),
            pltpu.VMEM((2, rows, width), BF16),
            pltpu.VMEM((2, rows, width), BF16),
            pltpu.VMEM((2, rows, 2 * LANES), BF16),
            dma((half, 2)),
            dma((half, 2)),
            dma((half, 2)),
            dma((half, 2)),
            dma((6,)),
            dma((2, 9)),
            dma((2, half)),
        ],
        compiler_params=pltpu.CompilerParams(
            collective_id=0, has_side_effects=True, vmem_limit_bytes=60 * MIB
        ),
        cost_estimate=KERNEL_COST,
        name="experts",
    )(x_own, cot_own, routes, routes_w, gate_up_e, down_e, gate_up_s, down_s)


def norm_of(values):
    factor = lax.rsqrt(jnp.mean(values * values, -1, keepdims=True) + EPS)
    return values * factor, factor


def norm_back(grad_out, normal, factor, gain):
    scaled = grad_out * gain
    return factor * (scaled - normal * jnp.mean(scaled * normal, -1, keepdims=True))


def local(
    hidden_in, segments, routes, cotangent, norm1_gain, w_qkv, b_qkv, w_out, norm2_gain, router,
    shared_gate_up, shared_down, shared_gate, expert_gate_up, expert_down,
):
    tokens_here, width = hidden_in.shape
    ep_count = lax.axis_size("ep")
    grp_count = lax.axis_size("grp")
    expert_count = router.shape[1]
    heads, qkv_dim = b_qkv.shape
    head_dim = qkv_dim // 3
    scale = 1.0 / math.sqrt(head_dim)
    slice_width = width // grp_count
    routes_w = jnp.concatenate(
        [router, shared_gate[:, None], jnp.zeros((width, LANES - 1 - expert_count), BF16)], 1
    )
    w_flat = w_qkv.reshape(width, heads * qkv_dim)
    b_flat = b_qkv.reshape(1, heads * qkv_dim)
    w_out_flat = w_out.reshape(heads * head_dim, width)

    (
        queries, key_rows, values, attended, logs, residual, normed_two, cosine, sine, starts,
        group_one, w_all,
    ) = attend_forward(
        ep_count, grp_count, hidden_in, norm1_gain, norm2_gain, w_flat, b_flat, w_out_flat,
        segments, scale,
    )

    (
        expert_act, expert_grad, shared_act, shared_grad, part, out_parts, grad_logits,
        group_two, group_cot,
    ) = experts(
        ep_count, expert_count, normed_two, cotangent, routes, routes_w,
        expert_gate_up, expert_down, jnp.swapaxes(shared_gate_up, 1, 2), shared_down,
    )

    def expert_gate_up_grad(rows, member):
        columns = columns_of(rows, member)
        return jnp.stack([dot_tn(columns, expert_grad[k]) for k in range(2)], 0)

    def shared_gate_up_grad(rows, member):
        columns = columns_of(rows, member)
        return jnp.stack([dot_tn(shared_grad[k], columns) for k in range(2)], 0)

    def down_grad(act):
        return lambda rows, member: dot_tn(act, columns_of(rows, member))

    sums = [
        GrpReduce(group_two, expert_gate_up_grad),
        GrpReduce(group_cot, down_grad(expert_act)),
        GrpReduce(group_two, shared_gate_up_grad),
        GrpReduce(group_cot, down_grad(shared_act)),
    ]
    part, aways = flat_tied(part, [item.away() for item in sums])
    arrived = [[item.to_partner(v) for v in values_] for item, values_ in zip(sums, aways)]
    (grad_normed_two,) = reduce_rows(ep_count, 3, part)
    normal_two, factor_two = norm_of(residual)
    grad_y = cotangent.astype(F32)
    grad_residual = grad_y + norm_back(grad_normed_two, normal_two, factor_two, norm2_gain)
    grad_norm2 = jnp.sum(grad_normed_two * normal_two, 0)
    for item in sums:
        item.after(grad_normed_two)
    own_attn, passed = flat_tied(
        grad_residual.astype(BF16),
        [item.pass_on(values_) for item, values_ in zip(sums, arrived)],
    )
    from_planes = [item.to_planes(values_) for item, values_ in zip(sums, passed)]

    grad_qkv, grad_bias, grad_branch, group_attn = attend_backward(
        ep_count, grp_count, own_attn, w_all, w_flat, cosine, sine, queries, key_rows, values,
        logs, starts, scale,
    )
    grad_norm1 = jnp.zeros((width,), F32)

    def w_qkv_grad(rows, member):
        nonlocal grad_norm1
        piece = dot_tn(columns_of(rows, member), grad_qkv)
        start = member * slice_width
        weights = lax.dynamic_slice_in_dim(w_flat, start, slice_width, 0).astype(F32)
        inner = jnp.sum(weights * piece, -1)
        grad_norm1 = lax.dynamic_update_slice_in_dim(grad_norm1, inner, start, 0)
        return piece

    more = [
        GrpReduce(group_one, w_qkv_grad),
        GrpReduce(group_attn, lambda rows, member: dot_tn(attended, columns_of(rows, member))),
    ]
    grad_branch, aways = flat_tied(grad_branch, [item.away() for item in more])
    arrived = [[item.to_partner(v) for v in values_] for item, values_ in zip(more, aways)]
    grad_normed_one, out_sum = reduce_rows(ep_count, 4, grad_branch, out_parts)
    layer_out = (residual + out_sum).astype(BF16)
    normal_one, factor_one = norm_of(hidden_in.astype(F32))
    grad_x = grad_residual + norm_back(grad_normed_one, normal_one, factor_one, norm1_gain)

    for item in more + sums:
        item.after(grad_normed_one)
    from_planes = [
        item.to_planes(item.pass_on(values_)) for item, values_ in zip(more, arrived)
    ] + from_planes
    (
        grad_w_qkv, grad_w_out, grad_expert_gate_up, grad_expert_down, grad_shared_gate_up,
        grad_shared_down,
    ) = [
        add_all(item.own(), values_) for item, values_ in zip(more + sums, from_planes)
    ]
    grad_routes = dot_tn(grad_logits, group_two)
    grad_routes = grad_routes[: expert_count + 1] + grad_routes[LANES : LANES + expert_count + 1]
    small = jnp.concatenate([grad_norm2[None], (grad_norm1 / norm1_gain)[None], grad_routes], 0)
    small = sum_all(small, ("ep", "grp"))
    bias_total = sum_all(grad_bias, ("grp",)).reshape(heads, grp_count, qkv_dim // grp_count)
    grad_b = lax.dynamic_index_in_dim(bias_total, lax.axis_index("grp"), 1, keepdims=False)
    grad_shared_gate_up = jnp.swapaxes(grad_shared_gate_up, 1, 2)

    return (
        layer_out,
        grad_x,
        small[1],
        grad_w_qkv.reshape(slice_width, heads, qkv_dim),
        grad_b,
        grad_w_out.reshape(heads, head_dim, slice_width),
        small[0],
        small[2 : expert_count + 2].T,
        grad_shared_gate_up,
        grad_shared_down,
        small[expert_count + 2],
        grad_expert_gate_up[None],
        grad_expert_down[None],
    )


def solution(mesh):
    in_specs = (
        P(("grp", "ep"), None),
        P("grp"),
        P("grp", None),
        P(("grp", "ep"), None),
        P(),
        P(None, "ep", None),
        P("ep", None),
        P("ep", None, None),
        P(),
        P(),
        P(None, None, "ep"),
        P("ep", None),
        P(),
        P("ep", None, None, None),
        P("ep", None, None),
    )
    out_specs = (
        P(("grp", "ep"), None),
        P(("grp", "ep"), None),
        P(),
        P("grp", "ep", None),
        P("ep", "grp"),
        P("ep", None, "grp"),
        P(),
        P(),
        P(None, "grp", "ep"),
        P("ep", "grp"),
        P(),
        P("ep", None, "grp", None),
        P("ep", None, "grp"),
    )
    return jax.shard_map(local, mesh=mesh, in_specs=in_specs, out_specs=out_specs, check_vma=False)
```

time: 1610 us -> 706 us (0.44)
  waiting for transfers between devices: 1040 us -> 140 us
  Pallas kernels: 0 us -> 395 us
  matrix products: 221 us -> 83.9 us
  local copies, waits for them, and re-layouts: 147 us -> 20.1 us
  other arithmetic: 88.9 us -> 43.7 us
  blocking collectives: 41.2 us -> 0 us
  starting transfers between devices: 41.3 us -> 16 us
    reduce_scatter x10 -> x0, waiting for transfers between devices: 478 us -> none  [the longest x1 147 us: local(): lax.psum_scatter(jnp.einsum('thc,hcd->td', piece, w_out, preferred_elemen...]
    pallas_call x0 -> x5, Pallas kernels: none -> 395 us  [the longest x2 134 us: reduce_rows(): pl.pallas_call(functools.partial(reduce_kernel, count, number), in_specs=...]
    all_gather x4 -> x0, waiting for transfers between devices: 226 us -> none  [the longest x1 71.2 us: local(): group_one = lax.all_gather(normed_one, 'ep', axis=0, tiled=True)]
    all_to_all x4 -> x0, waiting for transfers between devices: 196 us -> none  [the longest x1 86.6 us: local(): lax.all_to_all(grad_input.reshape(ep_count, capacity, width), 'ep', split...]
    ppermute x0 -> x25, waiting for transfers between devices: none -> 140 us  [the longest x6 131 us: to_planes(): sent.append(lax.ppermute(value, 'grp', pairs))]
    dot_general x37 -> x33, matrix products: 221 us -> 83.9 us  [dot_tn(): lax.dot_general(lhs, rhs, (((0,), (0,)), ((), ())), preferred_element_typ...]
    psum x1 -> x0, waiting for transfers between devices: 119 us -> none  [local(): lax.psum((grad_norm1, grad_norm2, grad_router, grad_shared_gate), ('grp',...]
    gather x7 -> x0, local copies, waits for them, and re-layouts: 54.2 us -> none  [the longest x4 28.2 us: local(): gate_values = jnp.take_along_axis(route_probs, routes, 1)]
  transfers between devices with their start and end apart: 20 -> 25, of which waited for: 17 -> 6; matrix products, arithmetic and copies ran while one was open for 25% -> 10% of each run, Pallas kernels for 0% -> 7%
where the time goes in v1:
time: 706 us; the launch traced here: 700 us
  Pallas kernels  395 us (56%)
  waiting for transfers between devices  140 us (20%)
  matrix products  83.9 us (12%)
  other arithmetic  43.7 us (6%)
  local copies, waits for them, and re-layouts  20.1 us (3%)
  starting transfers between devices  16 us (2%)
    pallas_call x2, Pallas kernels, reduce_rows(): pl.pallas_call(functools.partial(reduce_kernel, count, number), in_specs=...  134 us
    ppermute x6, waiting for transfers between devices, to_planes(): sent.append(lax.ppermute(value, 'grp', pairs))  131 us
    pallas_call x1, Pallas kernels, experts(): pl.pallas_call(functools.partial(experts_kernel, count, expert_count), in...  108 us
    pallas_call x1, Pallas kernels, attend_forward(): pl.pallas_call(functools.partial(attend_forward_kernel, count, grp_count,...  90.5 us
    dot_general x33, matrix products, dot_tn(): lax.dot_general(lhs, rhs, (((0,), (0,)), ((), ())), preferred_element_typ...  83.9 us
    pallas_call x1, Pallas kernels, attend_backward(): pl.pallas_call(functools.partial(attend_backward_kernel, count, grp_count...  62.5 us
  transfers between devices with their start and end apart: 25, of which 6 were waited for; matrix products, arithmetic and copies ran while one was open for 10% of the time, Pallas kernels for 7%

profile of v1, /device:TPU:0, one launch (start us, length us, event | category | flops | bytes accessed | tf_op | source)
XLA Modules:
  0.0 699.8 jit_solution(9261094001293752458)
XLA Ops:
  0.7 1.3 copy.36
  2.0 1.7 copy.33.routes
  5.8 1.7 copy.30.segments
  7.5 4.2 copy.35
  12.9 90.5 %attend_forward.1 = (bf16[2,1024,128]{2,1,0:T(8,128)(2,1)}, bf16[2,1024,128]{2,1,0:T(8,128)(2,1)}, bf16[2,1024,128]{2,1,0:T(8,128)(2,1)}, bf16[1024,256]{1,0:T(8...) custom-call(bf16[128,2048]{1,0:T(8,128)(2,1)} %hidden.1, ...), custom_call_target="tpu_custom_call" | custom-call | flops 1000000 | bytes 100000 | tf_op jit(solution)/shard_map/attend_forward/pallas_call | solution.py:465
  103.4 107.6 %experts.1 = (bf16[1024,1408]{1,0:T(8,128)(2,1)}, bf16[2,1024,1408]{2,1,0:T(8,128)(2,1)}, bf16[1024,704]{1,0:T(8,128)(2,1)}, bf16[2,1024,704]{2,1,0:T(8,128)(2,1...) custom-call(bf16[128,2048]{1,0:T(8,128)(2,1)} %get-tuple-element.60., ...), custom_call_target="tpu_custom_call" | custom-call | flops 1000000 | bytes 100000 | tf_op jit(solution)/shard_map/experts/pallas_call | solution.py:929
  211.0 2.8 fusion.83
  214.0 3.0 fusion.77
  217.1 1.9 fusion.17
  218.9 1.9 fusion.14
  221.1 1.8 convolution_convert_fusion.7
  222.9 2.8 convolution_convert_fusion.3
  225.7 1.2 pad_maximum_fusion.2
  227.0 1.8 pad_maximum_fusion
  228.8 1.8 collective-permute-start.3
  231.3 49.8 %reduce_rows.2 = f32[128,2048]{1,0:T(8,128)} custom-call(bf16[1024,2048]{1,0:T(8,128)(2,1)} %get-tuple-element.68.refs_0_), custom_call_target="tpu_custom_call" | custom-call | flops 1000000 | bytes 100000 | tf_op jit(solution)/shard_map/reduce_rows/pallas_call | solution.py:738
  281.1 3.9 fusion.50
  285.0 3.9 fusion.56
  288.9 3.4 convolution_bitcast_fusion.2
  292.4 3.6 convolution_bitcast_fusion.3
  296.0 1.3 fusion.185
  297.9 1.8 reduce.1
  299.8 1.6 reduce
  303.5 3.5 add_convert_fusion.2
  307.1 3.2 fusion.3
  310.3 4.7 add_convert_fusion
  315.0 3.9 fusion
  318.9 62.5 %attend_backward.1 = (bf16[1024,768]{1,0:T(8,128)(2,1)}, f32[1,768]{1,0:T(1,128)}, bf16[1024,2048]{1,0:T(8,128)(2,1)}, bf16[1024,2048]{1,0:T(8,128)(2,1)}) custom-call(bf16[128,2048]{1,0:T(8,128)(2,1)} %fusion.181.g_own, bf16[4,2048,512]{2,1,0:T(8,128)(2,1)} %get-tuple-element.76.w_all, bf16[2048,768]{1,0:T(8,128)(2,1)} %bitcast.146, ...), custom_call_target="tpu_custom_call" | custom-call | flops 1000000 | bytes 100000 | tf_op jit(solution)/shard_map/attend_backward/pallas_call | solution.py:634
  381.4 2.4 convolution_convert_fusion.9
  383.8 4.2 fusion.183
  387.9 84.3 %reduce_rows.3 = (f32[128,2048]{1,0:T(8,128)}, f32[128,2048]{1,0:T(8,128)}) custom-call(bf16[1024,2048]{1,0:T(8,128)(2,1)} %get-tuple-element.89.refs_0_, bf16[1024,2048]{1,0:T(8,128)(2,1)} %get-tuple-element.90.refs_1_), custom_call_target="tpu_custom_call" | custom-call | flops 1000000 | bytes 100000 | tf_op jit(solution)/shard_map/reduce_rows/pallas_call | solution.py:738
  472.3 3.4 fusion.74
  475.7 1.8 fusion.80
  478.2 1.8 convolution_convert_fusion.6
  480.0 2.0 fusion.119
  482.0 2.0 fusion.59
  484.1 2.1 fusion.53
  486.1 1.9 fusion.20
  488.0 1.9 fusion.23
  489.9 2.8 convolution_convert_fusion
  492.7 3.7 fusion.117
  498.6 3.5 convolution_bitcast_fusion.1
  505.0 1.8 pad_maximum_fusion.1
  506.8 3.4 convolution_bitcast_fusion
  512.4 1.6 fusion.91
  514.0 2.0 convolution_convert_fusion.8
  516.7 51.9 %collective-permute-done.11 = bf16[512,768]{1,0:T(8,128)(2,1)S(1)} collective-permute-done((bf16[512,768]{1,0:T(8,128)(2,1)S(1)}, bf16[512,768]{1,0:T(8,128)(2,1)S(1)}, u32[]{:S(2)}, u32[]{:S(2)}) %collective-permute-start.11) | collective-permute-done | bytes 786464 | tf_op jit(solution)/shard_map/ppermute | solution.py:78
  569.7 2.0 multiply_reduce_fusion
  573.1 1.7 add_convert_fusion.4
  575.3 2.4 collective-permute-done.4
  578.7 5.5 collective-permute-done.16
  584.9 1.1 collective-permute-start.5
  586.1 1.7 fusion.96
  587.9 2.0 collective-permute-done.5
  590.9 1.5 pad_maximum_fusion.3
  592.4 1.5 collective-permute-start.6
  595.0 4.8 collective-permute-done.6
  600.4 2.1 convert_add_fusion.2
  602.5 2.7 convert_add_fusion.1
  606.7 4.2 add_bitcast_fusion
  612.1 73.2 %collective-permute-done.18 = bf16[2,704,512]{2,1,0:T(8,128)(2,1)S(1)} collective-permute-done((bf16[2,704,512]{2,1,0:T(8,128)(2,1)}, bf16[2,704,512]{2,1,0:T(8,128)(2,1)S(1)}, u32[]{:S(2)}, u32[]{:S(2)}) %collective-permute-start.18) | collective-permute-done | bytes 1441824 | tf_op jit(solution)/shard_map/ppermute | solution.py:78
  685.3 2.2 fusion.5
  687.5 3.1 reshape.81
  692.8 6.8 fusion.2
  (170 shorter events, 28.1 us)
Async XLA Ops:
  211.0 3.0 copy-start.10
  211.0 6.0 copy-start.1
  217.1 3.8 copy-start.35
  218.9 2.2 copy-start.29
  220.8 2.1 copy-start.32
  227.0 4.1 copy-start.7
  228.8 74.3 %collective-permute-start.3 = (bf16[704,512]{1,0:T(8,128)(2,1)}, bf16[704,512]{1,0:T(8,128)(2,1)}, u32[]{:S(2)}, u32[]{:S(2)}) collective-permute-start(bf16[704,512]{1,0:T(8,128)(2,1)} %convolution_convert_fusion.7), channel_id=1, source_target_pairs={{0,8},{8,0},{16,24},{24,16},{1,9},{9,1},{17,25},{25,17},{2,10},{10... | collective-permute-start | bytes 2162696 | tf_op jit(solution)/shard_map/ppermute | solution.py:60
  230.6 79.7 %collective-permute-start.1 = (bf16[1408,512]{1,0:T(8,128)(2,1)}, bf16[1408,512]{1,0:T(8,128)(2,1)}, u32[]{:S(2)}, u32[]{:S(2)}) collective-permute-start(bf16[1408,512]{1,0:T(8,128)(2,1)} %convolution_convert_fusion.3), channel_id=1, source_target_pairs={{0,8},{8,0},{16,24},{24,16},{1,9},{9,1},{17,25},{25,17},{2,10},{10... | collective-permute-start | bytes 4325384 | tf_op jit(solution)/shard_map/ppermute | solution.py:60
  230.6 76.5 %collective-permute-start.2 = (bf16[2,704,512]{2,1,0:T(8,128)(2,1)}, bf16[2,704,512]{2,1,0:T(8,128)(2,1)}, u32[]{:S(2)}, u32[]{:S(2)}) collective-permute-start(bf16[2,704,512]{2,1,0:T(8,128)(2,1)} %pad_maximum_fusion.2), channel_id=1, source_target_pairs={{0,8},{8,0},{16,24},{24,16},{1,9},{9,1},{17,25},{25,17},{2,10},{10... | collective-permute-start | bytes 4325384 | tf_op jit(solution)/shard_map/ppermute | solution.py:60
  231.1 83.9 %collective-permute-start = (bf16[2,512,1408]{2,1,0:T(8,128)(2,1)}, bf16[2,512,1408]{2,1,0:T(8,128)(2,1)}, u32[]{:S(2)}, u32[]{:S(2)}) collective-permute-start(bf16[2,512,1408]{2,1,0:T(8,128)(2,1)} %pad_maximum_fusion), channel_id=1, source_target_pairs={{0,8},{8,0},{16,24},{24,16},{1,9},{9,1},{17,25},{25,17},{2,10},{10... | collective-permute-start | bytes 8650760 | tf_op jit(solution)/shard_map/ppermute | solution.py:60
  231.3 57.6 %slice-start = ((s8[5767168]{0:T(1024)(128)(4,1)}), s8[1572864]{0:T(1024)(128)(4,1)S(1)}, s32[]{:S(2)}) async-start(s8[5767168]{0:T(1024)(128)(4,1)} %bitcast.148), calls=%async_computation | async-start | bytes 3145728
  281.1 7.8 %slice-start.1 = ((s8[5767168]{0:T(1024)(128)(4,1)}), s8[4194304]{0:T(1024)(128)(4,1)S(1)}, s32[]{:S(2)}) async-start(s8[5767168]{0:T(1024)(128)(4,1)} %bitcast.148), calls=%async_computation.1 | async-start | bytes 8388608
  285.0 3.9 copy-start.11
  292.4 3.6 copy-start.40
  297.3 4.6 copy-start.8
  303.1 4.0 copy-start.18
  303.1 4.0 copy-start.19
  307.1 3.2 copy-start.33
  310.3 4.7 copy-start.5
  310.3 4.7 copy-start.6
  318.9 62.5 %copy-start.21 = (bf16[1024,256]{1,0:T(8,128)(2,1)S(1)}, bf16[1024,256]{1,0:T(8,128)(2,1)}, u32[]{:S(2)}) copy-start(bf16[1024,256]{1,0:T(8,128)(2,1)} %get-tuple-element.87) | copy-start | bytes 1572868
  387.9 84.3 %copy-start.12 = (bf16[1024,2048]{1,0:T(8,128)(2,1)S(1)}, bf16[1024,2048]{1,0:T(8,128)(2,1)}, u32[]{:S(2)}) copy-start(bf16[1024,2048]{1,0:T(8,128)(2,1)} %get-tuple-element.99) | copy-start | bytes 12582916
  472.3 3.4 copy-start.31
  472.3 5.2 copy-start.37
  475.7 2.4 copy-start.30
  480.0 6.2 slice-start.2
  482.0 4.1 slice-start.3
  492.7 3.7 copy-start.28
  492.7 3.7 copy-start.38
  498.6 3.5 copy-start.27
  498.6 5.5 copy-start.9
  498.6 5.5 copy-start.26
  498.6 5.8 copy-start.39
  502.1 14.0 %collective-permute-start.12 = (f32[1,768]{1,0:T(1,128)S(1)}, f32[1,768]{1,0:T(1,128)S(1)}, u32[]{:S(2)}, u32[]{:S(2)}) collective-permute-start(f32[1,768]{1,0:T(1,128)S(1)} %copy-done.27), channel_id=1, source_target_pairs={{0,8},{8,0},{16,24},{24,16},{1,9},{9,1},{17,25},{25,17},{2,10},{10... | collective-permute-start | bytes 9224 | tf_op jit(solution)/shard_map/ppermute | solution.py:42
  502.1 85.7 %collective-permute-start.20 = (bf16[704,512]{1,0:T(8,128)(2,1)}, bf16[704,512]{1,0:T(8,128)(2,1)}, u32[]{:S(2)}, u32[]{:S(2)}) collective-permute-start(bf16[704,512]{1,0:T(8,128)(2,1)} %add_convert_fusion.2), channel_id=1, source_target_pairs={{0,16},{8,24},{16,0},{24,8},{1,17},{9,25},{17,1},{25,9},{2,18},{10... | collective-permute-start | bytes 2162696 | tf_op jit(solution)/shard_map/ppermute | solution.py:78
  503.1 90.9 %collective-permute-start.24 = (bf16[1408,512]{1,0:T(8,128)(2,1)}, bf16[1408,512]{1,0:T(8,128)(2,1)}, u32[]{:S(2)}, u32[]{:S(2)}) collective-permute-start(bf16[1408,512]{1,0:T(8,128)(2,1)} %add_convert_fusion), channel_id=1, source_target_pairs={{0,16},{8,24},{16,0},{24,8},{1,17},{9,25},{17,1},{25,9},{2,18},{10... | collective-permute-start | bytes 4325384 | tf_op jit(solution)/shard_map/ppermute | solution.py:78
  504.4 5.8 collective-permute-start.10
  504.5 11.7 %collective-permute-start.9 = (bf16[512,768]{1,0:T(8,128)(2,1)S(1)}, bf16[512,768]{1,0:T(8,128)(2,1)S(1)}, u32[]{:S(2)}, u32[]{:S(2)}) collective-permute-start(bf16[512,768]{1,0:T(8,128)(2,1)S(1)} %get-tuple-element.121), channel_id=1, source_target_pairs={{0,8},{8,0},{16,24},{24,16},{1,9},{9,1},{17,25},{25,17},{2,10},{10... | collective-permute-start | bytes 2359304 | tf_op jit(solution)/shard_map/ppermute | solution.py:60
  510.2 2.2 copy-start.20
  511.3 57.3 %collective-permute-start.11 = (bf16[512,768]{1,0:T(8,128)(2,1)S(1)}, bf16[512,768]{1,0:T(8,128)(2,1)S(1)}, u32[]{:S(2)}, u32[]{:S(2)}) collective-permute-start(bf16[512,768]{1,0:T(8,128)(2,1)S(1)} %get-tuple-element.119), channel_id=1, source_target_pairs={{0,16},{8,24},{16,0},{24,8},{1,17},{9,25},{17,1},{25,9},{2,18},{10... | collective-permute-start | bytes 2359304 | tf_op jit(solution)/shard_map/ppermute | solution.py:78
  512.4 57.3 %copy-start = (bf16[256,8,2,384]{3,1,2,0:T(8,128)(2,1)S(1)}, bf16[256,8,2,384]{3,1,2,0:T(8,128)(2,1)}, u32[]{:S(2)}) copy-start(bf16[256,8,2,384]{3,1,2,0:T(8,128)(2,1)} %copy.35) | copy-start | bytes 9437188
  512.4 57.3 %copy-start.14 = (f32[512,768]{1,0:T(8,128)S(1)}, f32[512,768]{1,0:T(8,128)}, u32[]{:S(2)}) copy-start(f32[512,768]{1,0:T(8,128)} %get-tuple-element.118) | copy-start | bytes 4718596
  516.1 58.8 %collective-permute-start.14 = (bf16[256,512]{1,0:T(8,128)(2,1)S(1)}, bf16[256,512]{1,0:T(8,128)(2,1)S(1)}, u32[]{:S(2)}, u32[]{:S(2)}) collective-permute-start(bf16[256,512]{1,0:T(8,128)(2,1)S(1)} %convolution_convert_fusion.8), channel_id=1, source_target_pairs={{0,8},{8,0},{16,24},{24,16},{1,9},{9,1},{17,25},{25,17},{2,10},{10... | collective-permute-start | bytes 786440 | tf_op jit(solution)/shard_map/ppermute | solution.py:60
  516.2 56.5 %collective-permute-start.15 = (bf16[256,512]{1,0:T(8,128)(2,1)}, bf16[256,512]{1,0:T(8,128)(2,1)S(1)}, u32[]{:S(2)}, u32[]{:S(2)}) collective-permute-start(bf16[256,512]{1,0:T(8,128)(2,1)} %convolution_convert_fusion.9), channel_id=1, source_target_pairs={{0,8},{8,0},{16,24},{24,16},{1,9},{9,1},{17,25},{25,17},{2,10},{10... | collective-permute-start | bytes 786440 | tf_op jit(solution)/shard_map/ppermute | solution.py:60
  568.6 6.2 collective-permute-start.13
  569.6 3.4 copy-start.22
  572.7 5.0 collective-permute-start.4
  574.7 17.6 %collective-permute-start.19 = (bf16[704,512]{1,0:T(8,128)(2,1)}, bf16[704,512]{1,0:T(8,128)(2,1)}, u32[]{:S(2)}, u32[]{:S(2)}) collective-permute-start(bf16[704,512]{1,0:T(8,128)(2,1)} %convolution_convert_fusion.6), channel_id=1, source_target_pairs={{0,8},{8,0},{16,24},{24,16},{1,9},{9,1},{17,25},{25,17},{2,10},{10... | collective-permute-start | bytes 2162696 | tf_op jit(solution)/shard_map/ppermute | solution.py:60
  574.8 9.4 %copy-start.23 = (bf16[256,512]{1,0:T(8,128)(2,1)}, bf16[256,512]{1,0:T(8,128)(2,1)S(1)}, u32[]{:S(2)}) copy-start(bf16[256,512]{1,0:T(8,128)(2,1)S(1)} %collective-permute-done.14) | copy-start | bytes 786436
  574.8 31.3 %collective-permute-start.23 = (bf16[1408,512]{1,0:T(8,128)(2,1)}, bf16[1408,512]{1,0:T(8,128)(2,1)}, u32[]{:S(2)}, u32[]{:S(2)}) collective-permute-start(bf16[1408,512]{1,0:T(8,128)(2,1)} %convolution_convert_fusion), channel_id=1, source_target_pairs={{0,8},{8,0},{16,24},{24,16},{1,9},{9,1},{17,25},{25,17},{2,10},{10... | collective-permute-start | bytes 4325384 | tf_op jit(solution)/shard_map/ppermute | solution.py:60
  577.7 6.5 collective-permute-start.16
  584.9 5.0 collective-permute-start.5
  587.8 14.7 %copy-start.15 = (f32[704,512]{1,0:T(8,128)S(1)}, f32[704,512]{1,0:T(8,128)}, u32[]{:S(2)}) copy-start(f32[704,512]{1,0:T(8,128)} %fusion.119) | copy-start | bytes 4325380
  587.8 105.0 %collective-permute-start.21 = (bf16[2,512,1408]{2,1,0:T(8,128)(2,1)}, bf16[2,512,1408]{2,1,0:T(8,128)(2,1)}, u32[]{:S(2)}, u32[]{:S(2)}) collective-permute-start(bf16[2,512,1408]{2,1,0:T(8,128)(2,1)} %pad_maximum_fusion.1), channel_id=1, source_target_pairs={{0,8},{8,0},{16,24},{24,16},{1,9},{9,1},{17,25},{25,17},{2,10},{10... | collective-permute-start | bytes 8650760 | tf_op jit(solution)/shard_map/ppermute | solution.py:60
  589.9 102.8 %collective-permute-start.22 = (bf16[2,512,1408]{2,1,0:T(8,128)(2,1)}, bf16[2,512,1408]{2,1,0:T(8,128)(2,1)}, u32[]{:S(2)}, u32[]{:S(2)}) collective-permute-start(bf16[2,512,1408]{2,1,0:T(8,128)(2,1)} %fusion), channel_id=1, source_target_pairs={{0,16},{8,24},{16,0},{24,8},{1,17},{9,25},{17,1},{25,9},{2,18},{10... | collective-permute-start | bytes 8650760 | tf_op jit(solution)/shard_map/ppermute | solution.py:78
  592.4 7.4 %collective-permute-start.6 = (f32[11,2048]{1,0:T(8,128)S(1)}, f32[11,2048]{1,0:T(8,128)}, u32[]{:S(2)}, u32[]{:S(2)}) collective-permute-start(f32[11,2048]{1,0:T(8,128)S(1)} %add.227), channel_id=1, source_target_pairs={{0,4},{1,5},{2,6},{3,7},{4,0},{5,1},{6,2},{7,3},{8,12},{9,13},{10,... | collective-permute-start | bytes 270344 | tf_op jit(solution)/shard_map/ppermute | solution.py:42
  594.0 91.3 %collective-permute-start.18 = (bf16[2,704,512]{2,1,0:T(8,128)(2,1)}, bf16[2,704,512]{2,1,0:T(8,128)(2,1)S(1)}, u32[]{:S(2)}, u32[]{:S(2)}) collective-permute-start(bf16[2,704,512]{2,1,0:T(8,128)(2,1)} %fusion.3), channel_id=1, source_target_pairs={{0,16},{8,24},{16,0},{24,8},{1,17},{9,25},{17,1},{25,9},{2,18},{10... | collective-permute-start | bytes 4325384 | tf_op jit(solution)/shard_map/ppermute | solution.py:78
  599.8 85.4 %collective-permute-start.17 = (bf16[2,704,512]{2,1,0:T(8,128)(2,1)S(1)}, bf16[2,704,512]{2,1,0:T(8,128)(2,1)S(1)}, u32[]{:S(2)}, u32[]{:S(2)}) collective-permute-start(bf16[2,704,512]{2,1,0:T(8,128)(2,1)S(1)} %pad_maximum_fusion.3), channel_id=1, source_target_pairs={{0,8},{8,0},{16,24},{24,16},{1,9},{9,1},{17,25},{25,17},{2,10},{10... | collective-permute-start | bytes 4325384 | tf_op jit(solution)/shard_map/ppermute | solution.py:60
  600.4 6.3 copy-start.13
  606.1 79.2 %copy-start.16 = (f32[1,704,512]{2,1,0:T(8,128)S(1)}, f32[1,704,512]{2,1,0:T(8,128)}, u32[]{:S(2)}) copy-start(f32[1,704,512]{2,1,0:T(8,128)} %fusion.59) | copy-start | bytes 4325380
  606.1 79.2 %copy-start.17 = (f32[1,704,512]{2,1,0:T(8,128)S(1)}, f32[1,704,512]{2,1,0:T(8,128)}, u32[]{:S(2)}) copy-start(f32[1,704,512]{2,1,0:T(8,128)} %fusion.53) | copy-start | bytes 4325380
  606.1 4.8 collective-permute-start.7
  611.0 79.6 %collective-permute-start.8 = (f32[11,2048]{1,0:T(8,128)S(1)}, f32[11,2048]{1,0:T(8,128)}, u32[]{:S(2)}, u32[]{:S(2)}) collective-permute-start(f32[11,2048]{1,0:T(8,128)S(1)} %add.229), channel_id=1, source_target_pairs={{0,16},{8,24},{16,0},{24,8},{1,17},{9,25},{17,1},{25,9},{2,18},{10... | collective-permute-start | bytes 270344 | tf_op jit(solution)/shard_map/ppermute | solution.py:42
  687.5 5.3 copy-start.4
  (6 other events, 8.6 us)

commit v2 on v1

--- a/solution.py
+++ b/solution.py
@@ -34,16 +34,6 @@
     return lax.optimization_barrier(arrays)
 
 
-def sum_all(value, axes):
-    for axis in axes:
-        size = lax.axis_size(axis)
-        step = 1
-        while step < size:
-            value = value + lax.ppermute(value, axis, [(i, i ^ step) for i in range(size)])
-            step *= 2
-    return value
-
-
 class GrpReduce:
     def __init__(self, rows, produce):
         self.rows, self.produce = rows, produce
@@ -69,14 +59,6 @@
             (self.produce(self.rows, 2 * plane + self.core) + value.astype(F32)).astype(BF16)
             for plane, value in zip(self.far, arrived)
         ]
-
-    def to_planes(self, values):
-        sent = []
-        for k, value in enumerate(values):
-            shift = 2 * (k + 1)
-            pairs = [(j, (j + shift) % self.size) for j in range(self.size)]
-            sent.append(lax.ppermute(value, "grp", pairs))
-        return sent
 
     def own(self):
         away = self.produce(self.rows, 2 * self.plane + 1 - self.core).astype(BF16)
@@ -254,6 +236,32 @@
 
     def others(self):
         return [slot for slot in range(self.count) if slot != self.count - 2]
+
+
+class PlaneCopies:
+    def __init__(self, sources, targets, planes, sems):
+        mine, size = lax.axis_index("grp"), lax.axis_size("grp")
+        self.copies = []
+        for i, (source, target) in enumerate(zip(sources, targets)):
+            shift = 2 * (i % (planes - 1) + 1)
+            self.copies.append(
+                pltpu.make_async_remote_copy(
+                    src_ref=source,
+                    dst_ref=target,
+                    send_sem=sems.at[0, i],
+                    recv_sem=sems.at[1, i],
+                    device_id={"grp": (mine + shift) % size},
+                    device_id_type=MESH,
+                )
+            )
+
+    def start(self):
+        for copy in self.copies:
+            copy.start()
+
+    def finish(self):
+        for copy in self.copies:
+            copy.wait()
 
 
 def greet(axis, count):
@@ -299,8 +307,6 @@
     xs[ring_x.own(), :] = (own_hidden * lax.rsqrt(mean + EPS) * first_gain[...]).astype(BF16)
     pl.semaphore_wait(pltpu.get_barrier_semaphore(), count - 1 + grp_count - 1)
     ring_x.start()
-    load.wait()
-    ring_w.start()
 
     for slot in range(count):
         row_positions[:, slot * size : (slot + 1) * size] = slot_index(
@@ -359,10 +365,12 @@
         ring_x.arrive(i)
         ring_x.forward(i)
         store_x(i).start()
-        ring_w.arrive(i)
-        ring_w.forward(i)
-        for step in range(1, planes):
-            to_plane(step, i).start()
+
+        @pl.when(i == half - 2)
+        def _():
+            load.wait()
+            ring_w.start()
+
         projected = dot(xs[here, :], w[...]) + b[...]
         cos, sin = cosine[here, :], sine[here, :]
         for h in range(heads):
@@ -375,8 +383,6 @@
         return carry
 
     lax.fori_loop(0, half, project, 0)
-    to_core(0).start()
-    store_w(0).start()
 
     exchange = Exchange(
         count,
@@ -411,9 +417,15 @@
         def _():
             exchange.copy(2 * i).start()
 
+        ring_w.arrive(step)
+        ring_w.forward(step)
+        for k in range(1, planes):
+            to_plane(k, step).start()
         return carry
 
     lax.fori_loop(0, half, attend, 0)
+    to_core(0).start()
+    store_w(0).start()
     received[count - 2] = attended_out[ring_x.own(), :]
     for j in range(1, planes):
         for i in range(half):
@@ -509,9 +521,16 @@
 
 def attend_backward_kernel(
     count, grp_count, heads, scale, g_own, w_all, w, cosine, sine, q, k, v, row_logs, row_starts,
-    g_out, bias_out, branch_out, group_out, row_positions, positions, g_att, dk, dv, outbox, gs,
-    send_sems, recv_sems, ring_send, ring_recv, store_sems,
+    *refs,
 ):
+    number = (len(refs) - 17) // 2
+    bulk, refs = refs[:number], refs[number:]
+    g_out, bias_out, branch_out, group_out = refs[:4]
+    landed = refs[4 : 4 + number]
+    (
+        row_positions, positions, g_att, dk, dv, outbox, gs, send_sems, recv_sems, ring_send,
+        ring_recv, store_sems, plane_sems,
+    ) = refs[4 + number :]
     size, width = g_own.shape
     tokens = size * count
     rows = block_rows_of(tokens)
@@ -534,7 +553,12 @@
         store(i).start()
 
     greet("ep", count)
+    greet("grp", grp_count)
     gs[ring.own(), :] = g_own[...]
+    pl.semaphore_wait(pltpu.get_barrier_semaphore(), count - 1 + grp_count - 1)
+    plane_copies = PlaneCopies(bulk, landed, grp_count // 2, plane_sems)
+    ring.start()
+    plane_copies.start()
     for slot in range(count):
         first = slot_index(count, slot) * size
         row_positions[:, slot * size : (slot + 1) * size] = first + lax.broadcasted_iota(
@@ -559,10 +583,8 @@
         send_sems,
         recv_sems,
     )
-    pl.semaphore_wait(pltpu.get_barrier_semaphore(), count - 1)
     for slot in exchange.others():
         exchange.copy(slot).start()
-    ring.start()
     g_att[(count - 2) * size : (count - 1) * size, :] = outbox[count - 2]
     dk[...] = jnp.zeros_like(dk)
     dv[...] = jnp.zeros_like(dv)
@@ -589,14 +611,17 @@
             dk[h] += dot(g_scores, query)
             dv[h] += dot(weights.astype(BF16), g_block)
 
-        @pl.when(i == 1)
+        @pl.when(i == 0)
         def _():
             next_pair(0)
 
+        @pl.when(i == 2)
+        def _():
+            next_pair(1)
+
         return carry
 
     lax.fori_loop(0, tokens // rows, scores_back, 0)
-    next_pair(1)
     bias_out[...] = jnp.zeros_like(bias_out)
 
     def finish(i, carry):
@@ -621,25 +646,28 @@
     ring.finish()
     for i in range(count // 2):
         store(i).wait()
+    plane_copies.finish()
 
 
 def attend_backward(
-    count, grp_count, g_own, w_all, w, cosine, sine, q, k, v, logs, starts, scale
+    count, grp_count, g_own, w_all, w, cosine, sine, q, k, v, logs, starts, scale, bulk
 ):
     size, width = g_own.shape
     heads, tokens, _ = q.shape
+    anywhere = pl.BlockSpec(memory_space=pl.ANY)
     whole = pl.BlockSpec(memory_space=pltpu.VMEM)
     shape = jax.ShapeDtypeStruct
     dma = pltpu.SemaphoreType.DMA
     return pl.pallas_call(
         functools.partial(attend_backward_kernel, count, grp_count, heads, scale),
-        in_specs=[whole] * 10,
-        out_specs=[whole] * 3 + [pl.BlockSpec(memory_space=pl.ANY)],
+        in_specs=[whole] * 10 + [anywhere] * len(bulk),
+        out_specs=[whole] * 3 + [anywhere] * (1 + len(bulk)),
         out_shape=(
             shape((tokens, 3 * LANES * heads), BF16),
             shape((1, 3 * LANES * heads), F32),
             shape((tokens, width), BF16),
             shape((tokens, width), BF16),
+            *[shape(value.shape, value.dtype) for value in bulk],
         ),
         scratch_shapes=[
             pltpu.VMEM((1, tokens), jnp.int32),
@@ -654,6 +682,7 @@
             dma((count // 2, 2)),
             dma((count // 2, 2)),
             dma((count // 2,)),
+            dma((2, max(len(bulk), 1))),
         ],
         compiler_params=pltpu.CompilerParams(
             collective_id=2, has_side_effects=True, vmem_limit_bytes=56 * MIB
@@ -662,24 +691,83 @@
         name="attend_backward",
     )(
         g_own, w_all, w, cosine, sine, q, k, v,
-        logs.reshape(heads, 1, tokens), starts.reshape(1, tokens),
-    )
-
-
-def reduce_kernel(count, number, *refs):
-    parts, outs = refs[:number], refs[number : 2 * number]
-    to_right = refs[2 * number : 3 * number]
-    to_left = refs[3 * number : 4 * number]
-    send_sems, recv_sems = refs[4 * number :]
+        logs.reshape(heads, 1, tokens), starts.reshape(1, tokens), *bulk,
+    )
+
+
+def doubling_stages(axes):
+    stages = []
+    for axis in axes:
+        step = 1
+        while step < lax.axis_size(axis):
+            stages.append((axis, step))
+            step *= 2
+    return stages
+
+
+class Doubling:
+    def __init__(self, held, arrived, stages, sems):
+        self.held, self.arrived, self.stages, self.sems = held, arrived, stages, sems
+        self.place = 0
+
+    def copy(self, k):
+        axis, step = self.stages[k]
+        here = lax.axis_index(axis)
+        return pltpu.make_async_remote_copy(
+            src_ref=self.held.at[k],
+            dst_ref=self.arrived.at[k],
+            send_sem=self.sems.at[0, k],
+            recv_sem=self.sems.at[1, k],
+            device_id={axis: here + step * (1 - 2 * (here // step % 2))},
+            device_id_type=MESH,
+        )
+
+    def start(self):
+        self.copy(0).start()
+
+    def advance(self):
+        k = self.place
+        if k < len(self.stages):
+            self.copy(k).wait_recv()
+            self.held[k + 1] = self.held[k] + self.arrived[k]
+            if k + 1 < len(self.stages):
+                self.copy(k + 1).start()
+            self.place += 1
+
+    def finish(self):
+        while self.place < len(self.stages):
+            self.advance()
+        for k in range(len(self.stages)):
+            self.copy(k).wait_send()
+        return self.held[len(self.stages)]
+
+
+def reduce_kernel(count, grp_count, number, bulk_number, small_axes, *refs):
+    refs = list(refs)
+
+    def take(amount):
+        taken = refs[:amount]
+        del refs[:amount]
+        return taken
+
+    small_number = len(small_axes)
+    parts, smalls, bulk = take(number), take(small_number), take(bulk_number)
+    outs, small_outs, landed = take(number), take(small_number), take(bulk_number)
+    to_right, to_left = take(number), take(number)
+    small_held, small_arrived = take(small_number), take(small_number)
+    send_sems, recv_sems = take(2)
+    small_sems = take(small_number)
+    (plane_sems,) = take(1)
     half = count // 2
     size = outs[0].shape[0]
     middle = size // 2
     place, index_at = ring_places(count)
     neighbours = (index_at((place + 1) % count), index_at((place + count - 1) % count))
-    barrier = pltpu.get_barrier_semaphore()
-    for neighbour in neighbours:
-        pl.semaphore_signal(barrier, inc=1, device_id={"ep": neighbour}, device_id_type=MESH)
-    pl.semaphore_wait(barrier, 2)
+    greet("ep", count)
+    greet("grp", grp_count)
+    for held, small in zip(small_held, smalls):
+        held[0] = small[...]
+    pl.semaphore_wait(pltpu.get_barrier_semaphore(), count - 1 + grp_count - 1)
 
     def copy(a, step, way):
         held = (to_right, to_left)[way][a]
@@ -698,9 +786,17 @@
             device_id_type=MESH,
         )
 
+    sums = [
+        Doubling(held, arrived, doubling_stages(axes), sems)
+        for held, arrived, axes, sems in zip(small_held, small_arrived, small_axes, small_sems)
+    ]
     for a in range(number):
         for way in range(2):
             copy(a, 0, way).start()
+    for item in sums:
+        item.start()
+    plane_copies = PlaneCopies(bulk, landed, grp_count // 2, plane_sems)
+    plane_copies.start()
     for step in range(1, half):
         far = half - step
         for a in range(number):
@@ -720,34 +816,56 @@
                     own = parts[a][first : first + size, :]
                     held[step - 1] = (own.astype(F32) + held[step - 1].astype(F32)).astype(BF16)
                 copy(a, step, way).start()
+            for item in sums:
+                item.advance()
     for a in range(number):
         own = parts[a][(count - 2) * size : (count - 1) * size, :].astype(F32)
         for way in range(2):
             copy(a, half - 1, way).wait_recv()
             own = own + (to_right, to_left)[way][a][half - 1].astype(F32)
         outs[a][...] = own
+    for item, out in zip(sums, small_outs):
+        out[...] = item.finish()
     for a in range(number):
         for step in range(half):
             for way in range(2):
                 copy(a, step, way).wait_send()
-
-
-def reduce_rows(count, call, *parts):
+    plane_copies.finish()
+
+
+def reduce_rows(count, grp_count, call, parts, smalls=(), small_axes=(), bulk=()):
     tokens, width = parts[0].shape
     size, number, half = tokens // count, len(parts), count // 2
-    return pl.pallas_call(
-        functools.partial(reduce_kernel, count, number),
-        in_specs=[pl.BlockSpec(memory_space=pltpu.VMEM)] * number,
-        out_specs=[pl.BlockSpec(memory_space=pltpu.VMEM)] * number,
-        out_shape=[jax.ShapeDtypeStruct((size, width), F32)] * number,
+    stages = [len(doubling_stages(axes)) for axes in small_axes]
+    anywhere = pl.BlockSpec(memory_space=pl.ANY)
+    whole = pl.BlockSpec(memory_space=pltpu.VMEM)
+    shape = jax.ShapeDtypeStruct
+    dma = pltpu.SemaphoreType.DMA
+    results = pl.pallas_call(
+        functools.partial(
+            reduce_kernel, count, grp_count, number, len(bulk), tuple(small_axes)
+        ),
+        in_specs=[whole] * (number + len(smalls)) + [anywhere] * len(bulk),
+        out_specs=[whole] * (number + len(smalls)) + [anywhere] * len(bulk),
+        out_shape=[shape((size, width), F32)] * number
+        + [shape(value.shape, value.dtype) for value in (*smalls, *bulk)],
         scratch_shapes=[pltpu.VMEM((half, size, width), BF16)] * (2 * number)
-        + [pltpu.SemaphoreType.DMA((number, half, 2))] * 2,
+        + [pltpu.VMEM((k + 1, *value.shape), F32) for k, value in zip(stages, smalls)]
+        + [pltpu.VMEM((k, *value.shape), F32) for k, value in zip(stages, smalls)]
+        + [dma((number, half, 2))] * 2
+        + [dma((2, k)) for k in stages]
+        + [dma((2, max(len(bulk), 1)))],
         compiler_params=pltpu.CompilerParams(
             collective_id=call, has_side_effects=True, vmem_limit_bytes=56 * MIB
         ),
         cost_estimate=KERNEL_COST,
         name="reduce_rows",
-    )(*parts)
+    )(*parts, *smalls, *bulk)
+    return (
+        results[:number],
+        results[number : number + len(smalls)],
+        results[number + len(smalls) :],
+    )
 
 
 def tiles_of(width):
@@ -1037,7 +1155,7 @@
     ]
     part, aways = flat_tied(part, [item.away() for item in sums])
     arrived = [[item.to_partner(v) for v in values_] for item, values_ in zip(sums, aways)]
-    (grad_normed_two,) = reduce_rows(ep_count, 3, part)
+    (grad_normed_two,), _, _ = reduce_rows(ep_count, grp_count, 3, [part])
     normal_two, factor_two = norm_of(residual)
     grad_y = cotangent.astype(F32)
     grad_residual = grad_y + norm_back(grad_normed_two, normal_two, factor_two, norm2_gain)
@@ -1048,12 +1166,13 @@
         grad_residual.astype(BF16),
         [item.pass_on(values_) for item, values_ in zip(sums, arrived)],
     )
-    from_planes = [item.to_planes(values_) for item, values_ in zip(sums, passed)]
-
-    grad_qkv, grad_bias, grad_branch, group_attn = attend_backward(
+    each = grp_count // 2 - 1
+
+    grad_qkv, grad_bias, grad_branch, group_attn, *landed = attend_backward(
         ep_count, grp_count, own_attn, w_all, w_flat, cosine, sine, queries, key_rows, values,
-        logs, starts, scale,
-    )
+        logs, starts, scale, passed[0],
+    )
+    from_planes = [landed]
     grad_norm1 = jnp.zeros((width,), F32)
 
     def w_qkv_grad(rows, member):
@@ -1069,29 +1188,33 @@
         GrpReduce(group_one, w_qkv_grad),
         GrpReduce(group_attn, lambda rows, member: dot_tn(attended, columns_of(rows, member))),
     ]
-    grad_branch, aways = flat_tied(grad_branch, [item.away() for item in more])
+    aways = [item.away() for item in more]
     arrived = [[item.to_partner(v) for v in values_] for item, values_ in zip(more, aways)]
-    grad_normed_one, out_sum = reduce_rows(ep_count, 4, grad_branch, out_parts)
+    more_passed = [item.pass_on(values_) for item, values_ in zip(more, arrived)]
+    more_own = [item.own() for item in more]
+    grad_routes = dot_tn(grad_logits, group_two)
+    grad_routes = grad_routes[: expert_count + 1] + grad_routes[LANES : LANES + expert_count + 1]
+    small = jnp.concatenate([grad_norm2[None], (grad_norm1 / norm1_gain)[None], grad_routes], 0)
+    bulk = [value for values_ in passed[1:] for value in values_]
+    (grad_normed_one, out_sum), (small, bias_total), landed = reduce_rows(
+        ep_count, grp_count, 4, [grad_branch, out_parts], [small, grad_bias],
+        [("ep", "grp"), ("grp",)], bulk + [value for values_ in more_passed for value in values_],
+    )
+    from_planes += [landed[i * each : (i + 1) * each] for i in range(5)]
     layer_out = (residual + out_sum).astype(BF16)
     normal_one, factor_one = norm_of(hidden_in.astype(F32))
     grad_x = grad_residual + norm_back(grad_normed_one, normal_one, factor_one, norm1_gain)
 
-    for item in more + sums:
+    for item in sums:
         item.after(grad_normed_one)
-    from_planes = [
-        item.to_planes(item.pass_on(values_)) for item, values_ in zip(more, arrived)
-    ] + from_planes
     (
-        grad_w_qkv, grad_w_out, grad_expert_gate_up, grad_expert_down, grad_shared_gate_up,
-        grad_shared_down,
+        grad_expert_gate_up, grad_expert_down, grad_shared_gate_up, grad_shared_down,
+        grad_w_qkv, grad_w_out,
     ) = [
-        add_all(item.own(), values_) for item, values_ in zip(more + sums, from_planes)
+        add_all(own, values_)
+        for own, values_ in zip([item.own() for item in sums] + more_own, from_planes)
     ]
-    grad_routes = dot_tn(grad_logits, group_two)
-    grad_routes = grad_routes[: expert_count + 1] + grad_routes[LANES : LANES + expert_count + 1]
-    small = jnp.concatenate([grad_norm2[None], (grad_norm1 / norm1_gain)[None], grad_routes], 0)
-    small = sum_all(small, ("ep", "grp"))
-    bias_total = sum_all(grad_bias, ("grp",)).reshape(heads, grp_count, qkv_dim // grp_count)
+    bias_total = bias_total.reshape(heads, grp_count, qkv_dim // grp_count)
     grad_b = lax.dynamic_index_in_dim(bias_total, lax.axis_index("grp"), 1, keepdims=False)
     grad_shared_gate_up = jnp.swapaxes(grad_shared_gate_up, 1, 2)
 

time: 706 us -> 668 us (0.946)
  waiting for transfers between devices: 140 us -> 0.03 us
  Pallas kernels: 395 us -> 499 us
  starting transfers between devices: 16 us -> 4.7 us
  local copies, waits for them, and re-layouts: 20.1 us -> 30.1 us
    ppermute x13 -> x0, waiting for transfers between devices: 140 us -> none  [the longest x6 131 us: to_planes(): sent.append(lax.ppermute(value, 'grp', pairs))]
    pallas_call x2, Pallas kernels: 134 us -> 209 us  [reduce_rows(): pl.pallas_call(functools.partial(reduce_kernel, count, grp_count, number,...]
    pallas_call x1, Pallas kernels: 90.5 us -> 107 us  [attend_forward(): pl.pallas_call(functools.partial(attend_forward_kernel, count, grp_count,...]
    ppermute x13 -> x0, starting transfers between devices: 11.9 us -> none  [the longest x6 6.09 us: to_planes(): sent.append(lax.ppermute(value, 'grp', pairs))]
    pallas_call x1, Pallas kernels: 62.5 us -> 74.1 us  [attend_backward(): pl.pallas_call(functools.partial(attend_backward_kernel, count, grp_count...]
  transfers between devices with their start and end apart: 25 -> 12, of which waited for: 6 -> 0; matrix products, arithmetic and copies ran while one was open for 10% -> 16% of each run, Pallas kernels for 7% -> 32%
where the time goes in v2:
time: 668 us; the launch traced here: 661 us
  Pallas kernels  499 us (75%)
  matrix products  81.7 us (12%)
  other arithmetic  44.6 us (7%)
  local copies, waits for them, and re-layouts  30.1 us (5%)
    pallas_call x2, Pallas kernels, reduce_rows(): pl.pallas_call(functools.partial(reduce_kernel, count, grp_count, number,...  209 us
    pallas_call x1, Pallas kernels, experts(): pl.pallas_call(functools.partial(experts_kernel, count, expert_count), in...  109 us
    pallas_call x1, Pallas kernels, attend_forward(): pl.pallas_call(functools.partial(attend_forward_kernel, count, grp_count,...  107 us
    dot_general x33, matrix products, dot_tn(): lax.dot_general(lhs, rhs, (((0,), (0,)), ((), ())), preferred_element_typ...  81.7 us
    pallas_call x1, Pallas kernels, attend_backward(): pl.pallas_call(functools.partial(attend_backward_kernel, count, grp_count...  74.1 us
    unnamed x120, local copies, waits for them, and re-layouts  13.4 us
  transfers between devices with their start and end apart: 12, of which 0 were waited for; matrix products, arithmetic and copies ran while one was open for 16% of the time, Pallas kernels for 32%

profile of v2, /device:TPU:0, one launch (start us, length us, event | category | flops | bytes accessed | tf_op | source)
XLA Modules:
  0.0 661.4 jit_solution(8472420785830099719)
XLA Ops:
  0.7 1.3 copy.36
  2.0 1.7 copy.33.routes
  5.8 1.7 copy.30.segments
  7.5 4.2 copy.35
  12.9 106.8 %attend_forward.1 = (bf16[2,1024,128]{2,1,0:T(8,128)(2,1)}, bf16[2,1024,128]{2,1,0:T(8,128)(2,1)}, bf16[2,1024,128]{2,1,0:T(8,128)(2,1)}, bf16[1024,256]{1,0:T(8...) custom-call(bf16[128,2048]{1,0:T(8,128)(2,1)} %hidden.1, ...), custom_call_target="tpu_custom_call" | custom-call | flops 1000000 | bytes 100000 | tf_op jit(solution)/shard_map/attend_forward/pallas_call | solution.py:477
  119.7 108.6 %experts.1 = (bf16[1024,1408]{1,0:T(8,128)(2,1)}, bf16[2,1024,1408]{2,1,0:T(8,128)(2,1)}, bf16[1024,704]{1,0:T(8,128)(2,1)}, bf16[2,1024,704]{2,1,0:T(8,128)(2,1...) custom-call(bf16[128,2048]{1,0:T(8,128)(2,1)} %get-tuple-element.63., ...), custom_call_target="tpu_custom_call" | custom-call | flops 1000000 | bytes 100000 | tf_op jit(solution)/shard_map/experts/pallas_call | solution.py:1047
  228.3 2.8 fusion.83
  231.3 3.1 fusion.77
  234.4 1.9 fusion.17
  236.2 1.9 fusion.14
  238.4 1.8 convolution_convert_fusion.7
  240.2 2.8 convolution_convert_fusion.3
  243.0 1.2 pad_maximum_fusion.2
  244.3 1.9 pad_maximum_fusion
  246.2 2.4 collective-permute-start.3
  249.3 52.0 %reduce_rows.2 = f32[128,2048]{1,0:T(8,128)} custom-call(bf16[1024,2048]{1,0:T(8,128)(2,1)} %get-tuple-element.71.refs_0_), custom_call_target="tpu_custom_call" | custom-call | flops 1000000 | bytes 100000 | tf_op jit(solution)/shard_map/reduce_rows/pallas_call | solution.py:844
  301.3 3.9 fusion.50
  305.2 3.9 fusion.56
  309.2 3.4 convolution_bitcast_fusion.2
  312.6 3.6 convolution_bitcast_fusion.3
  316.8 1.3 fusion.184
  319.2 1.8 reduce.1
  321.0 1.6 reduce
  323.2 1.1 fusion.181.g_own
  324.8 3.5 add_convert_fusion.2.refs_6_
  328.3 3.2 fusion.3.refs_5_
  331.6 4.7 add_convert_fusion.refs_4_
  336.2 3.9 fusion.refs_0_
  340.2 74.1 %attend_backward.1 = (bf16[1024,768]{1,0:T(8,128)(2,1)}, f32[1,768]{1,0:T(1,128)}, bf16[1024,2048]{1,0:T(8,128)(2,1)}, bf16[1024,2048]{1,0:T(8,128)(2,1)}, bf16[2,512,1408]{2,1,0:T(8,128)(2,1)}) custom-call(bf16[128,2048]{1,0:T(8,128)(2,1)} %fusion.181.g_own, bf16[4,2048,512]{2,1,0:T(8,128)(2,1)} %get-tuple-element.79.w_all, bf16[2048,768]{1,0:T(8,128)(2,1)} %bitcast.146, ...), custom_call_target="tpu_custom_call" | custom-call | flops 1000000 | bytes 100000 | tf_op jit(solution)/shard_map/attend_backward/pallas_call | solution.py:661
  414.3 2.6 fusion.103
  418.0 1.2 copy-done.30
  421.4 1.2 convolution_convert_fusion.8
  422.6 1.3 fusion.94
  423.9 1.2 add_convert_fusion.4.refs_8_
  425.1 3.7 multiply_reduce_fusion
  429.4 1.4 dynamic_update_slice.12
  430.7 1.4 dynamic_update_slice.13
  432.1 1.5 dynamic_update_slice.14
  433.6 1.8 dynamic_update_slice.15
  436.1 1.4 pad_maximum_fusion.4.refs_2_
  437.5 157.2 %reduce_rows.3 = (f32[128,2048]{1,0:T(8,128)}, f32[128,2048]{1,0:T(8,128)}, f32[11,2048]{1,0:T(8,128)}, f32[1,768]{1,0:T(1,128)}, bf16[1408,512]{1,0:T(8,128)(2,...) custom-call(bf16[1024,2048]{1,0:T(8,128)(2,1)} %get-tuple-element.88, ...), custom_call_target="tpu_custom_call" | custom-call | flops 1000000 | bytes 100000 | tf_op jit(solution)/shard_map/reduce_rows/pallas_call | solution.py:844
  594.8 1.5 fusion.182
  596.3 1.5 slice_bitcast_fusion
  597.8 3.4 fusion.74
  601.2 1.8 fusion.80
  603.7 1.8 convolution_convert_fusion.6
  605.5 2.0 fusion.119
  607.5 2.1 fusion.59
  609.6 3.0 fusion.20
  612.6 3.0 fusion.23
  615.5 2.9 convolution_convert_fusion
  618.4 3.3 fusion.117
  621.7 3.6 convolution_bitcast_fusion.1
  626.4 3.7 pad_maximum_fusion.1
  630.6 1.7 fusion.91
  632.3 1.3 pad_maximum_fusion.3
  635.0 2.1 fusion.53
  638.7 1.9 convolution_bitcast_fusion
  640.6 1.4 convert_add_fusion.1
  642.7 1.4 convert_add_fusion
  644.1 2.9 reshape.81
  647.0 5.0 fusion.5
  652.1 3.7 add_bitcast_fusion
  655.8 5.3 fusion.2
  (165 shorter events, 17.7 us)
Async XLA Ops:
  228.3 3.0 copy-start.12
  228.3 6.0 copy-start.1
  234.4 3.8 copy-start.48
  236.2 2.2 copy-start.41
  238.1 2.1 copy-start.45
  244.3 4.8 copy-start.7
  246.2 78.2 %collective-permute-start.3 = (bf16[704,512]{1,0:T(8,128)(2,1)}, bf16[704,512]{1,0:T(8,128)(2,1)}, u32[]{:S(2)}, u32[]{:S(2)}) collective-permute-start(bf16[704,512]{1,0:T(8,128)(2,1)} %convolution_convert_fusion.7), channel_id=1, source_target_pairs={{0,8},{8,0},{16,24},{24,16},{1,9},{9,1},{17,25},{25,17},{2,10},{10... | collective-permute-start | bytes 2162696 | tf_op jit(solution)/shard_map/ppermute | solution.py:50
  248.6 83.0 %collective-permute-start.1 = (bf16[1408,512]{1,0:T(8,128)(2,1)}, bf16[1408,512]{1,0:T(8,128)(2,1)}, u32[]{:S(2)}, u32[]{:S(2)}) collective-permute-start(bf16[1408,512]{1,0:T(8,128)(2,1)} %convolution_convert_fusion.3), channel_id=1, source_target_pairs={{0,8},{8,0},{16,24},{24,16},{1,9},{9,1},{17,25},{25,17},{2,10},{10... | collective-permute-start | bytes 4325384 | tf_op jit(solution)/shard_map/ppermute | solution.py:50
  248.6 79.7 %collective-permute-start.2 = (bf16[2,704,512]{2,1,0:T(8,128)(2,1)}, bf16[2,704,512]{2,1,0:T(8,128)(2,1)}, u32[]{:S(2)}, u32[]{:S(2)}) collective-permute-start(bf16[2,704,512]{2,1,0:T(8,128)(2,1)} %pad_maximum_fusion.2), channel_id=1, source_target_pairs={{0,8},{8,0},{16,24},{24,16},{1,9},{9,1},{17,25},{25,17},{2,10},{10... | collective-permute-start | bytes 4325384 | tf_op jit(solution)/shard_map/ppermute | solution.py:50
  249.1 87.1 %collective-permute-start = (bf16[2,512,1408]{2,1,0:T(8,128)(2,1)}, bf16[2,512,1408]{2,1,0:T(8,128)(2,1)}, u32[]{:S(2)}, u32[]{:S(2)}) collective-permute-start(bf16[2,512,1408]{2,1,0:T(8,128)(2,1)} %pad_maximum_fusion), channel_id=1, source_target_pairs={{0,8},{8,0},{16,24},{24,16},{1,9},{9,1},{17,25},{25,17},{2,10},{10... | collective-permute-start | bytes 8650760 | tf_op jit(solution)/shard_map/ppermute | solution.py:50
  249.3 59.8 %slice-start = ((s8[5767168]{0:T(1024)(128)(4,1)}), s8[1572864]{0:T(1024)(128)(4,1)S(1)}, s32[]{:S(2)}) async-start(s8[5767168]{0:T(1024)(128)(4,1)} %bitcast.148), calls=%async_computation | async-start | bytes 3145728
  301.3 7.8 %slice-start.1 = ((s8[5767168]{0:T(1024)(128)(4,1)}), s8[4194304]{0:T(1024)(128)(4,1)S(1)}, s32[]{:S(2)}) async-start(s8[5767168]{0:T(1024)(128)(4,1)} %bitcast.148), calls=%async_computation.1 | async-start | bytes 8388608
  305.2 3.9 copy-start.13
  312.6 4.2 copy-start.51
  318.1 5.2 copy-start.9
  318.3 6.0 copy-start.35
  323.2 5.1 copy-start.39
  324.4 4.0 copy-start.22
  324.4 4.0 copy-start.23
  328.3 3.2 copy-start.46
  331.5 4.7 copy-start.5
  331.5 4.7 copy-start.6
  340.2 74.2 %copy-start.32 = (bf16[1024,2048]{1,0:T(8,128)(2,1)S(1)}, bf16[1024,2048]{1,0:T(8,128)(2,1)}, u32[]{:S(2)}) copy-start(bf16[1024,2048]{1,0:T(8,128)(2,1)} %get-tuple-element.90) | copy-start | bytes 12582916
  414.3 2.6 copy-start.19
  416.9 2.3 copy-start.30
  419.7 4.2 collective-permute-start.5
  419.8 5.3 collective-permute-start.4
  421.4 3.7 copy-start
  422.6 214.5 %collective-permute-start.7 = (bf16[256,512]{1,0:T(8,128)(2,1)}, bf16[256,512]{1,0:T(8,128)(2,1)S(1)}, u32[]{:S(2)}, u32[]{:S(2)}) collective-permute-start(bf16[256,512]{1,0:T(8,128)(2,1)} %convolution_convert_fusion.8), channel_id=1, source_target_pairs={{0,8},{8,0},{16,24},{24,16},{1,9},{9,1},{17,25},{25,17},{2,10},{10... | collective-permute-start | bytes 786440 | tf_op jit(solution)/shard_map/ppermute | solution.py:50
  425.1 10.3 %copy-start.34 = (f32[2048]{0:T(1024)S(1)}, f32[2048]{0:T(1024)}, u32[]{:S(2)}) copy-start(f32[2048]{0:T(1024)} %param.19) | copy-start | bytes 24580
  437.5 160.3 %copy-start.14 = (bf16[1024,2048]{1,0:T(8,128)(2,1)S(1)}, bf16[1024,2048]{1,0:T(8,128)(2,1)}, u32[]{:S(2)}) copy-start(bf16[1024,2048]{1,0:T(8,128)(2,1)} %get-tuple-element.105) | copy-start | bytes 12582916
  597.8 3.4 copy-start.43
  597.8 5.2 copy-start.50
  601.2 2.4 copy-start.42
  603.7 5.9 slice-start.2
  605.5 4.1 slice-start.3
  612.6 3.0 copy-start.47
  621.7 3.6 copy-start.10
  621.7 3.6 copy-start.38
  621.7 4.0 copy-start.37
  625.8 14.8 %collective-permute-start.9 = (bf16[704,512]{1,0:T(8,128)(2,1)}, bf16[704,512]{1,0:T(8,128)(2,1)S(1)}, u32[]{:S(2)}, u32[]{:S(2)}) collective-permute-start(bf16[704,512]{1,0:T(8,128)(2,1)} %convolution_convert_fusion.6), channel_id=1, source_target_pairs={{0,8},{8,0},{16,24},{24,16},{1,9},{9,1},{17,25},{25,17},{2,10},{10... | collective-permute-start | bytes 2162696 | tf_op jit(solution)/shard_map/ppermute | solution.py:50
  625.8 4.8 copy-start.11
  625.8 4.8 copy-start.24
  625.8 4.8 copy-start.36
  625.8 4.8 copy-start.40
  625.8 16.2 %collective-permute-start.6 = (bf16[512,768]{1,0:T(8,128)(2,1)}, bf16[512,768]{1,0:T(8,128)(2,1)S(1)}, u32[]{:S(2)}, u32[]{:S(2)}) collective-permute-start(bf16[512,768]{1,0:T(8,128)(2,1)} %get-tuple-element.117), channel_id=1, source_target_pairs={{0,8},{8,0},{16,24},{24,16},{1,9},{9,1},{17,25},{25,17},{2,10},{10... | collective-permute-start | bytes 2359304 | tf_op jit(solution)/shard_map/ppermute | solution.py:50
  626.3 25.7 %collective-permute-start.11 = (bf16[1408,512]{1,0:T(8,128)(2,1)}, bf16[1408,512]{1,0:T(8,128)(2,1)}, u32[]{:S(2)}, u32[]{:S(2)}) collective-permute-start(bf16[1408,512]{1,0:T(8,128)(2,1)} %convolution_convert_fusion), channel_id=1, source_target_pairs={{0,8},{8,0},{16,24},{24,16},{1,9},{9,1},{17,25},{25,17},{2,10},{10... | collective-permute-start | bytes 4325384 | tf_op jit(solution)/shard_map/ppermute | solution.py:50
  626.4 5.9 copy-start.28
  630.1 25.7 %collective-permute-start.10 = (bf16[2,512,1408]{2,1,0:T(8,128)(2,1)}, bf16[2,512,1408]{2,1,0:T(8,128)(2,1)}, u32[]{:S(2)}, u32[]{:S(2)}) collective-permute-start(bf16[2,512,1408]{2,1,0:T(8,128)(2,1)} %pad_maximum_fusion.1), channel_id=1, source_target_pairs={{0,8},{8,0},{16,24},{24,16},{1,9},{9,1},{17,25},{25,17},{2,10},{10... | collective-permute-start | bytes 8650760 | tf_op jit(solution)/shard_map/ppermute | solution.py:50
  630.6 1.7 copy-start.27
  630.6 3.4 copy-start.15
  630.6 4.5 copy-start.44
  630.6 8.1 %slice-start.4 = ((s8[5767168]{0:T(1024)(128)(4,1)}), s8[1572864]{0:T(1024)(128)(4,1)S(1)}, s32[]{:S(2)}) async-start(s8[5767168]{0:T(1024)(128)(4,1)} %bitcast.152), calls=%async_computation.4 | async-start | bytes 3145728
  632.3 6.4 slice-start.5
  635.0 2.2 copy-start.18
  635.0 2.2 copy-start.31
  637.1 9.9 %collective-permute-start.8 = (bf16[2,704,512]{2,1,0:T(8,128)(2,1)}, bf16[2,704,512]{2,1,0:T(8,128)(2,1)}, u32[]{:S(2)}, u32[]{:S(2)}) collective-permute-start(bf16[2,704,512]{2,1,0:T(8,128)(2,1)} %pad_maximum_fusion.3), channel_id=1, source_target_pairs={{0,8},{8,0},{16,24},{24,16},{1,9},{9,1},{17,25},{25,17},{2,10},{10... | collective-permute-start | bytes 4325384 | tf_op jit(solution)/shard_map/ppermute | solution.py:50
  638.7 1.9 copy-start.20
  638.7 1.9 copy-start.26
  640.6 2.1 copy-start.25
  647.0 5.0 copy-start.16
  647.0 5.0 copy-start.21
  652.1 3.8 copy-start.4
  652.1 3.8 copy-start.17
  (6 other events, 8.8 us)

commit v3 on v2

--- a/solution.py
+++ b/solution.py
@@ -30,10 +30,6 @@
     return lax.dot_general(lhs, rhs, (((0,), (0,)), ((), ())), preferred_element_type=F32)
 
 
-def tied(*arrays):
-    return lax.optimization_barrier(arrays)
-
-
 class GrpReduce:
     def __init__(self, rows, produce):
         self.rows, self.produce = rows, produce
@@ -43,9 +39,6 @@
         self.core, self.plane = mine % 2, mine // 2
         self.far = [(self.plane + k) % self.planes for k in range(1, self.planes)]
 
-    def after(self, token):
-        self.rows = tied(self.rows, token)[0]
-
     def to_partner(self, value):
         return lax.ppermute(value, "grp", [(i, i ^ 1) for i in range(self.size)])
 
@@ -67,19 +60,10 @@
 
 
 def add_all(value, others):
+    value = value.astype(F32)
     for other in others:
         value = value + other.astype(F32)
     return value
-
-
-def flat_tied(first, groups):
-    flat = [value for group in groups for value in group]
-    first, *flat = tied(first, *flat)
-    result = []
-    for group in groups:
-        result.append(flat[: len(group)])
-        flat = flat[len(group) :]
-    return first, result
 
 
 def columns_of(array, member):
@@ -279,8 +263,8 @@
 
 def attend_forward_kernel(
     count, grp_count, heads, scale, hidden, first_gain, gain, w, b, segments, row_segments, w_out,
-    q_out, k_out, v_out, attended_out, log_out, residual_out, normed_out, cosine, sine, starts,
-    x_out, w_all_out, row_positions, xs, w_all, received, x_send, x_recv, w_send, w_recv, plane_send, plane_recv, core_send,
+    q_out, k_out, v_out, attended_out, log_out, residual_out, normed_out, cosine, sine, row_starts,
+    x_out, w_all_out, row_positions, starts, xs, w_all, received, x_send, x_recv, w_send, w_recv, plane_send, plane_recv, core_send,
     core_recv, hand_send, hand_recv, x_sems, w_sems, own_sem,
 ):
     size, width = hidden.shape
@@ -306,6 +290,8 @@
     mean = jnp.sum(own_hidden * own_hidden, -1, keepdims=True) * (1.0 / width)
     xs[ring_x.own(), :] = (own_hidden * lax.rsqrt(mean + EPS) * first_gain[...]).astype(BF16)
     pl.semaphore_wait(pltpu.get_barrier_semaphore(), count - 1 + grp_count - 1)
+    load.wait()
+    ring_w.start()
     ring_x.start()
 
     for slot in range(count):
@@ -323,6 +309,9 @@
         before = jnp.where(row_segments[...] < segments[there, :], 1.0, 0.0)
         start = jnp.sum(before, -1, keepdims=True)
         starts[here, :] = start.astype(jnp.int32)
+        own_row = row_segments[:, there]
+        before = jnp.where(segments[...] < own_row, 1.0, 0.0)
+        row_starts[:, here] = jnp.sum(before, 0, keepdims=True).astype(jnp.int32)
         position = (block * size + lax.broadcasted_iota(jnp.int32, (size, 1), 0)).astype(F32)
         angle = (position - start) * inverse
         cosine[here, :] = jnp.cos(angle)
@@ -362,15 +351,13 @@
 
     def project(i, carry):
         here = rows_at(i, rows)
+        ring_w.arrive(i)
+        ring_w.forward(i)
+        for step in range(1, planes):
+            to_plane(step, i).start()
         ring_x.arrive(i)
         ring_x.forward(i)
         store_x(i).start()
-
-        @pl.when(i == half - 2)
-        def _():
-            load.wait()
-            ring_w.start()
-
         projected = dot(xs[here, :], w[...]) + b[...]
         cos, sin = cosine[here, :], sine[here, :]
         for h in range(heads):
@@ -383,6 +370,8 @@
         return carry
 
     lax.fori_loop(0, half, project, 0)
+    to_core(0).start()
+    store_w(0).start()
 
     exchange = Exchange(
         count,
@@ -410,22 +399,17 @@
             total = jnp.sum(expo, -1, keepdims=True)
             weights = (expo * (1.0 / total)).astype(BF16)
             attended_out[here, h * dim : (h + 1) * dim] = dot(weights, v_out[h]).astype(BF16)
-            log_out[h, here, :] = highest + jnp.log(total)
+            logs = jnp.broadcast_to(highest + jnp.log(total), (rows, LANES))
+            log_out[h, :, here] = jnp.transpose(logs)[:1, :]
         exchange.copy(2 * i + 1).start()
 
         @pl.when(i < half - 1)
         def _():
             exchange.copy(2 * i).start()
 
-        ring_w.arrive(step)
-        ring_w.forward(step)
-        for k in range(1, planes):
-            to_plane(k, step).start()
         return carry
 
     lax.fori_loop(0, half, attend, 0)
-    to_core(0).start()
-    store_w(0).start()
     received[count - 2] = attended_out[ring_x.own(), :]
     for j in range(1, planes):
         for i in range(half):
@@ -483,17 +467,18 @@
             shape((heads, tokens, LANES), BF16),
             shape((heads, tokens, LANES), BF16),
             shape((tokens, heads * LANES), BF16),
-            shape((heads, tokens, 1), F32),
+            shape((heads, 1, tokens), F32),
             shape((size, width), F32),
             shape((size, width), BF16),
             shape((tokens, LANES), F32),
             shape((tokens, LANES), F32),
-            shape((tokens, 1), jnp.int32),
+            shape((1, tokens), jnp.int32),
             shape((tokens, width), BF16),
             shape(w_all_shape, BF16),
         ),
         scratch_shapes=[
             pltpu.VMEM((1, tokens), jnp.int32),
+            pltpu.VMEM((tokens, 1), jnp.int32),
             pltpu.VMEM((tokens, width), BF16),
             pltpu.VMEM(w_all_shape, BF16),
             pltpu.VMEM((count, size, heads * LANES), BF16),
@@ -691,17 +676,17 @@
         name="attend_backward",
     )(
         g_own, w_all, w, cosine, sine, q, k, v,
-        logs.reshape(heads, 1, tokens), starts.reshape(1, tokens), *bulk,
+        logs, starts, *bulk,
     )
 
 
 def doubling_stages(axes):
     stages = []
     for axis in axes:
-        step = 1
-        while step < lax.axis_size(axis):
+        step = lax.axis_size(axis) // 2
+        while step:
             stages.append((axis, step))
-            step *= 2
+            step //= 2
     return stages
 
 
@@ -742,6 +727,67 @@
         return self.held[len(self.stages)]
 
 
+class RingSum:
+    def __init__(self, count, part, out, to_right, to_left, send_sems, recv_sems):
+        place, index_at = ring_places(count)
+        self.count, self.half, self.size = count, count // 2, out.shape[0]
+        self.part, self.out, self.held = part, out, (to_right, to_left)
+        self.send_sems, self.recv_sems = send_sems, recv_sems
+        self.neighbours = (
+            index_at((place + 1) % count), index_at((place + count - 1) % count)
+        )
+
+    def copy(self, step, way):
+        held, middle = self.held[way], self.size // 2
+        if step == 0:
+            source = self.part.at[pl.ds((self.count - 1) * self.size + way * middle, middle)]
+            target = held.at[0, pl.ds(way * middle, middle)]
+        else:
+            source, target = held.at[step - 1], held.at[step]
+        return pltpu.make_async_remote_copy(
+            src_ref=source,
+            dst_ref=target,
+            send_sem=self.send_sems.at[step, way],
+            recv_sem=self.recv_sems.at[step, way],
+            device_id={"ep": self.neighbours[way]},
+            device_id_type=MESH,
+        )
+
+    def start(self):
+        for way in range(2):
+            self.copy(0, way).start()
+
+    def advance(self, step):
+        middle, part = self.size // 2, self.part
+        for way in range(2):
+            held = self.held[way]
+            first = (2 * (self.half - step) - 1 - way) * self.size
+            self.copy(step - 1, way).wait_recv()
+            if step == 1:
+                here = slice(way * middle, (way + 1) * middle)
+                rest = slice((1 - way) * middle, (2 - way) * middle)
+                own = part[first + way * middle : first + (way + 1) * middle, :]
+                held[0, here] = (own.astype(F32) + held[0, here].astype(F32)).astype(BF16)
+                held[0, rest] = part[first + (1 - way) * middle : first + (2 - way) * middle, :]
+            else:
+                own = part[first : first + self.size, :]
+                held[step - 1] = (own.astype(F32) + held[step - 1].astype(F32)).astype(BF16)
+            self.copy(step, way).start()
+
+    def last(self):
+        own = self.part[(self.count - 2) * self.size : (self.count - 1) * self.size, :]
+        total = own.astype(F32)
+        for way in range(2):
+            self.copy(self.half - 1, way).wait_recv()
+            total = total + self.held[way][self.half - 1].astype(F32)
+        self.out[...] = total
+
+    def finish(self):
+        for step in range(self.half):
+            for way in range(2):
+                self.copy(step, way).wait_send()
+
+
 def reduce_kernel(count, grp_count, number, bulk_number, small_axes, *refs):
     refs = list(refs)
 
@@ -758,78 +804,38 @@
     send_sems, recv_sems = take(2)
     small_sems = take(small_number)
     (plane_sems,) = take(1)
-    half = count // 2
-    size = outs[0].shape[0]
-    middle = size // 2
-    place, index_at = ring_places(count)
-    neighbours = (index_at((place + 1) % count), index_at((place + count - 1) % count))
     greet("ep", count)
     greet("grp", grp_count)
     for held, small in zip(small_held, smalls):
         held[0] = small[...]
     pl.semaphore_wait(pltpu.get_barrier_semaphore(), count - 1 + grp_count - 1)
-
-    def copy(a, step, way):
-        held = (to_right, to_left)[way][a]
-        if step == 0:
-            cut = pl.ds(way * middle, middle)
-            source = parts[a].at[pl.ds((count - 1) * size + way * middle, middle)]
-            target = held.at[0, cut]
-        else:
-            source, target = held.at[step - 1], held.at[step]
-        return pltpu.make_async_remote_copy(
-            src_ref=source,
-            dst_ref=target,
-            send_sem=send_sems.at[a, step, way],
-            recv_sem=recv_sems.at[a, step, way],
-            device_id={"ep": neighbours[way]},
-            device_id_type=MESH,
-        )
-
+    rings = [
+        RingSum(
+            count, parts[a], outs[a], to_right[a], to_left[a], send_sems.at[a], recv_sems.at[a]
+        )
+        for a in range(number)
+    ]
     sums = [
         Doubling(held, arrived, doubling_stages(axes), sems)
         for held, arrived, axes, sems in zip(small_held, small_arrived, small_axes, small_sems)
     ]
-    for a in range(number):
-        for way in range(2):
-            copy(a, 0, way).start()
+    for ring in rings:
+        ring.start()
     for item in sums:
         item.start()
     plane_copies = PlaneCopies(bulk, landed, grp_count // 2, plane_sems)
     plane_copies.start()
-    for step in range(1, half):
-        far = half - step
-        for a in range(number):
-            for way in range(2):
-                held = (to_right, to_left)[way][a]
-                first = (2 * far - 1 - way) * size
-                copy(a, step - 1, way).wait_recv()
-                if step == 1:
-                    here = slice(way * middle, (way + 1) * middle)
-                    rest = slice((1 - way) * middle, (2 - way) * middle)
-                    own = parts[a][first + way * middle : first + (way + 1) * middle, :]
-                    held[0, here] = (own.astype(F32) + held[0, here].astype(F32)).astype(BF16)
-                    held[0, rest] = parts[a][
-                        first + (1 - way) * middle : first + (2 - way) * middle, :
-                    ]
-                else:
-                    own = parts[a][first : first + size, :]
-                    held[step - 1] = (own.astype(F32) + held[step - 1].astype(F32)).astype(BF16)
-                copy(a, step, way).start()
+    for step in range(1, count // 2):
+        for ring in rings:
+            ring.advance(step)
             for item in sums:
                 item.advance()
-    for a in range(number):
-        own = parts[a][(count - 2) * size : (count - 1) * size, :].astype(F32)
-        for way in range(2):
-            copy(a, half - 1, way).wait_recv()
-            own = own + (to_right, to_left)[way][a][half - 1].astype(F32)
-        outs[a][...] = own
+    for ring in rings:
+        ring.last()
     for item, out in zip(sums, small_outs):
         out[...] = item.finish()
-    for a in range(number):
-        for step in range(half):
-            for way in range(2):
-                copy(a, step, way).wait_send()
+    for ring in rings:
+        ring.finish()
     plane_copies.finish()
 
 
@@ -866,6 +872,152 @@
         results[number : number + len(smalls)],
         results[number + len(smalls) :],
     )
+
+
+def reduce_and_weights_kernel(
+    count, grp_count, part, x_in, cot_in, grad_e_in, act_e_in, grad_s_in, act_s_in, *refs
+):
+    refs = list(refs)
+
+    def take(amount):
+        taken = refs[:amount]
+        del refs[:amount]
+        return taken
+
+    planes = grp_count // 2
+    (summed,) = take(1)
+    outs = [take(planes) for _ in range(4)]
+    sources = (x_in, grad_e_in, cot_in, act_e_in, grad_s_in, act_s_in)
+    held = take(6)
+    x, grad_e, cot, act_e, grad_s, act_s = held
+    to_right, to_left = take(2)
+    staged, arrived = take(4), take(4)
+    send_sems, recv_sems, load_sems, core_send, core_recv, out_sems = take(6)
+    mine = lax.axis_index("grp")
+    core, plane = mine % 2, mine // 2
+    part_width = x.shape[1] // grp_count
+
+    loads = [
+        pltpu.make_async_copy(source, target, load_sems.at[i])
+        for i, (source, target) in enumerate(zip(sources, held))
+    ]
+    for load in loads:
+        load.start()
+    greet("ep", count)
+    greet("grp", grp_count)
+    pl.semaphore_wait(pltpu.get_barrier_semaphore(), count - 1 + grp_count - 1)
+    ring = RingSum(count, part, summed, to_right, to_left, send_sems, recv_sems)
+    ring.start()
+
+    def columns(order, side):
+        member = 2 * ((plane + order) % planes) + (core if side == 0 else 1 - core)
+        return pl.ds(pl.multiple_of(member * part_width, part_width), part_width)
+
+    def products(kind, cut):
+        if kind == 0:
+            return [dot_tn(x[:, cut], grad_e[k]) for k in range(2)]
+        if kind == 1:
+            return [dot_tn(act_e[...], cot[:, cut])]
+        if kind == 2:
+            return [dot_tn(grad_s[k], x[:, cut]) for k in range(2)]
+        return [dot_tn(act_s[...], cot[:, cut])]
+
+    def to_core(kind, place):
+        return pltpu.make_async_remote_copy(
+            src_ref=staged[kind],
+            dst_ref=arrived[kind].at[place],
+            send_sem=core_send.at[kind, place],
+            recv_sem=core_recv.at[kind, place],
+            device_id={"grp": mine + 1 - 2 * core},
+            device_id_type=MESH,
+        )
+
+    def store(kind, place):
+        return pltpu.make_async_copy(staged[kind], outs[kind][place], out_sems.at[kind, place])
+
+    orders = list(range(1, planes)) + [0]
+    needs = ((0, 1), (2, 3), (4,), (5,))
+    ring_step = 1
+    number = 0
+    for side in (1, 0):
+        for place, order in enumerate(orders):
+            for kind in range(4):
+                if side == 1 and place == 0:
+                    for i in needs[kind]:
+                        loads[i].wait()
+                pieces = products(kind, columns(order, side))
+                if side == 1:
+                    if place:
+                        to_core(kind, place - 1).wait_send()
+                else:
+                    to_core(kind, place).wait_recv()
+                    if place:
+                        store(kind, place - 1).wait()
+                    else:
+                        to_core(kind, planes - 1).wait_send()
+                for k, piece in enumerate(pieces):
+                    whole = (k,) if len(pieces) > 1 else (Ellipsis,)
+                    if side == 0:
+                        piece = piece + arrived[kind][(place, *whole)].astype(F32)
+                    staged[kind][whole] = piece.astype(BF16)
+                if side == 1:
+                    to_core(kind, place).start()
+                else:
+                    store(kind, place).start()
+                number += 1
+                if number % 4 == 2:
+                    if ring_step < count // 2:
+                        ring.advance(ring_step)
+                    elif ring_step == count // 2:
+                        ring.last()
+                    ring_step += 1
+    while ring_step <= count // 2:
+        if ring_step < count // 2:
+            ring.advance(ring_step)
+        else:
+            ring.last()
+        ring_step += 1
+    for kind in range(4):
+        store(kind, planes - 1).wait()
+    ring.finish()
+
+
+def reduce_and_weights(
+    count, grp_count, part, x, cot, grad_e, act_e, grad_s, act_s
+):
+    tokens, width = part.shape
+    size, half, planes = tokens // count, count // 2, grp_count // 2
+    part_width = width // grp_count
+    wide, narrow = act_e.shape[1], act_s.shape[1]
+    shapes = [
+        (2, part_width, wide), (wide, part_width), (2, narrow, part_width), (narrow, part_width)
+    ]
+    anywhere = pl.BlockSpec(memory_space=pl.ANY)
+    whole = pl.BlockSpec(memory_space=pltpu.VMEM)
+    shape = jax.ShapeDtypeStruct
+    dma = pltpu.SemaphoreType.DMA
+    summed, *slices = pl.pallas_call(
+        functools.partial(reduce_and_weights_kernel, count, grp_count),
+        in_specs=[whole] + [anywhere] * 6,
+        out_specs=[whole] + [anywhere] * (4 * planes),
+        out_shape=[shape((size, width), F32)]
+        + [shape(dims, BF16) for dims in shapes for _ in range(planes)],
+        scratch_shapes=[
+            pltpu.VMEM(value.shape, BF16) for value in (x, grad_e, cot, act_e, grad_s, act_s)
+        ]
+        + [pltpu.VMEM((half, size, width), BF16)] * 2
+        + [pltpu.VMEM(dims, BF16) for dims in shapes]
+        + [pltpu.VMEM((planes, *dims), BF16) for dims in shapes]
+        + [dma((half, 2)), dma((half, 2)), dma((6,))]
+        + [dma((4, planes))] * 3,
+        compiler_params=pltpu.CompilerParams(
+            collective_id=3, has_side_effects=True, vmem_limit_bytes=60 * MIB
+        ),
+        cost_estimate=KERNEL_COST,
+        name="reduce_and_weights",
+    )(part, x, cot, grad_e, act_e, grad_s, act_s)
+    groups = [slices[i * planes : (i + 1) * planes] for i in range(4)]
+    return summed, [group[:-1] for group in groups], [group[-1] for group in groups]
 
 
 def tiles_of(width):
@@ -1147,25 +1299,27 @@
     def down_grad(act):
         return lambda rows, member: dot_tn(act, columns_of(rows, member))
 
-    sums = [
-        GrpReduce(group_two, expert_gate_up_grad),
-        GrpReduce(group_cot, down_grad(expert_act)),
-        GrpReduce(group_two, shared_gate_up_grad),
-        GrpReduce(group_cot, down_grad(shared_act)),
-    ]
-    part, aways = flat_tied(part, [item.away() for item in sums])
-    arrived = [[item.to_partner(v) for v in values_] for item, values_ in zip(sums, aways)]
-    (grad_normed_two,), _, _ = reduce_rows(ep_count, grp_count, 3, [part])
     normal_two, factor_two = norm_of(residual)
     grad_y = cotangent.astype(F32)
+    if ep_count == 8:
+        grad_normed_two, passed, sums_own = reduce_and_weights(
+            ep_count, grp_count, part, group_two, group_cot, expert_grad, expert_act,
+            shared_grad, shared_act,
+        )
+    else:
+        sums = [
+            GrpReduce(group_two, expert_gate_up_grad),
+            GrpReduce(group_cot, down_grad(expert_act)),
+            GrpReduce(group_two, shared_gate_up_grad),
+            GrpReduce(group_cot, down_grad(shared_act)),
+        ]
+        arrived = [[item.to_partner(value) for value in item.away()] for item in sums]
+        passed = [item.pass_on(values_) for item, values_ in zip(sums, arrived)]
+        sums_own = [item.own() for item in sums]
+        (grad_normed_two,), _, _ = reduce_rows(ep_count, grp_count, 3, [part])
     grad_residual = grad_y + norm_back(grad_normed_two, normal_two, factor_two, norm2_gain)
     grad_norm2 = jnp.sum(grad_normed_two * normal_two, 0)
-    for item in sums:
-        item.after(grad_normed_two)
-    own_attn, passed = flat_tied(
-        grad_residual.astype(BF16),
-        [item.pass_on(values_) for item, values_ in zip(sums, arrived)],
-    )
+    own_attn = grad_residual.astype(BF16)
     each = grp_count // 2 - 1
 
     grad_qkv, grad_bias, grad_branch, group_attn, *landed = attend_backward(
@@ -1173,15 +1327,14 @@
         logs, starts, scale, passed[0],
     )
     from_planes = [landed]
-    grad_norm1 = jnp.zeros((width,), F32)
+    inners = []
 
     def w_qkv_grad(rows, member):
-        nonlocal grad_norm1
         piece = dot_tn(columns_of(rows, member), grad_qkv)
         start = member * slice_width
         weights = lax.dynamic_slice_in_dim(w_flat, start, slice_width, 0).astype(F32)
-        inner = jnp.sum(weights * piece, -1)
-        grad_norm1 = lax.dynamic_update_slice_in_dim(grad_norm1, inner, start, 0)
+        place = (jnp.arange(grp_count) == member).astype(F32)
+        inners.append(place[:, None] * jnp.sum(weights * piece, -1)[None, :])
         return piece
 
     more = [
@@ -1194,25 +1347,24 @@
     more_own = [item.own() for item in more]
     grad_routes = dot_tn(grad_logits, group_two)
     grad_routes = grad_routes[: expert_count + 1] + grad_routes[LANES : LANES + expert_count + 1]
+    grad_norm1 = sum(inners).reshape(width)
     small = jnp.concatenate([grad_norm2[None], (grad_norm1 / norm1_gain)[None], grad_routes], 0)
     bulk = [value for values_ in passed[1:] for value in values_]
     (grad_normed_one, out_sum), (small, bias_total), landed = reduce_rows(
         ep_count, grp_count, 4, [grad_branch, out_parts], [small, grad_bias],
-        [("ep", "grp"), ("grp",)], bulk + [value for values_ in more_passed for value in values_],
+        [("grp", "ep"), ("grp",)], bulk + [value for values_ in more_passed for value in values_],
     )
     from_planes += [landed[i * each : (i + 1) * each] for i in range(5)]
     layer_out = (residual + out_sum).astype(BF16)
     normal_one, factor_one = norm_of(hidden_in.astype(F32))
     grad_x = grad_residual + norm_back(grad_normed_one, normal_one, factor_one, norm1_gain)
 
-    for item in sums:
-        item.after(grad_normed_one)
     (
         grad_expert_gate_up, grad_expert_down, grad_shared_gate_up, grad_shared_down,
         grad_w_qkv, grad_w_out,
     ) = [
         add_all(own, values_)
-        for own, values_ in zip([item.own() for item in sums] + more_own, from_planes)
+        for own, values_ in zip(sums_own + more_own, from_planes)
     ]
     bias_total = bias_total.reshape(heads, grp_count, qkv_dim // grp_count)
     grad_b = lax.dynamic_index_in_dim(bias_total, lax.axis_index("grp"), 1, keepdims=False)

time: 668 us -> 510 us (0.76)
  Pallas kernels: 499 us -> 434 us
  matrix products: 81.7 us -> 29.6 us
  other arithmetic: 44.6 us -> 23.8 us
  local copies, waits for them, and re-layouts: 30.1 us -> 15.2 us
    pallas_call x2 -> x1, Pallas kernels: 209 us -> 112 us  [reduce_rows(): pl.pallas_call(functools.partial(reduce_kernel, count, grp_count, number,...]
    dot_general x33 -> x9, matrix products: 81.7 us -> 29.6 us  [dot_tn(): lax.dot_general(lhs, rhs, (((0,), (0,)), ((), ())), preferred_element_typ...]
    pallas_call x0 -> x1, Pallas kernels: none -> 51.5 us  [reduce_and_weights(): pl.pallas_call(functools.partial(reduce_and_weights_kernel, count, grp_co...]
    pallas_call x1, Pallas kernels: 107 us -> 88.2 us  [attend_forward(): pl.pallas_call(functools.partial(attend_forward_kernel, count, grp_count,...]
    another operation x4 -> x0, other arithmetic: 8.08 us -> none  [the longest x2 5.59 us: expert_gate_up_grad(): return jnp.stack([dot_tn(columns, expert_grad[k]) for k in range(2)], 0)]
    unnamed x120 -> x81, local copies, waits for them, and re-layouts: 13.4 us -> 7.94 us
  transfers between devices with their start and end apart: 12 -> 4, of which waited for: 0 -> 0; matrix products, arithmetic and copies ran while one was open for 16% -> 10% of each run, Pallas kernels for 32% -> 22%
where the time goes in v3:
time: 510 us; the launch traced here: 504 us
  Pallas kernels  434 us (85%)
  matrix products  29.6 us (6%)
  other arithmetic  23.8 us (5%)
  local copies, waits for them, and re-layouts  15.2 us (3%)
    pallas_call x1, Pallas kernels, reduce_rows(): pl.pallas_call(functools.partial(reduce_kernel, count, grp_count, number,...  112 us
    pallas_call x1, Pallas kernels, experts(): pl.pallas_call(functools.partial(experts_kernel, count, expert_count), in...  109 us
    pallas_call x1, Pallas kernels, attend_forward(): pl.pallas_call(functools.partial(attend_forward_kernel, count, grp_count,...  88.2 us
    pallas_call x1, Pallas kernels, attend_backward(): pl.pallas_call(functools.partial(attend_backward_kernel, count, grp_count...  73.1 us
    pallas_call x1, Pallas kernels, reduce_and_weights(): pl.pallas_call(functools.partial(reduce_and_weights_kernel, count, grp_co...  51.5 us
    dot_general x9, matrix products, dot_tn(): lax.dot_general(lhs, rhs, (((0,), (0,)), ((), ())), preferred_element_typ...  29.6 us
  transfers between devices with their start and end apart: 4, of which 0 were waited for; matrix products, arithmetic and copies ran while one was open for 10% of the time, Pallas kernels for 22%

profile of v3, /device:TPU:0, one launch (start us, length us, event | category | flops | bytes accessed | tf_op | source)
XLA Modules:
  0.0 504.4 jit_solution(12827228843747322131)
XLA Ops:
  0.7 0.0 copy-start.22
  0.7 4.3 copy.34
  5.0 1.0 copy.30.segments
  6.0 0.0 copy-done.27
  6.0 0.6 copy.35
  6.6 0.3 broadcast_in_dim.54
  7.0 0.0 copy-done.21
  7.0 0.3 copy.31
  7.3 1.0 copy.33.routes
  8.3 88.2 %attend_forward.1 = (bf16[2,1024,128]{2,1,0:T(8,128)(2,1)}, bf16[2,1024,128]{2,1,0:T(8,128)(2,1)}, bf16[2,1024,128]{2,1,0:T(8,128)(2,1)}, bf16[1024,256]{1,0:T(8...) custom-call(bf16[128,2048]{1,0:T(8,128)(2,1)} %hidden.1, ...), custom_call_target="tpu_custom_call" | custom-call | flops 1000000 | bytes 100000 | tf_op jit(solution)/shard_map/attend_forward/pallas_call | solution.py:461
  96.5 1.4 multiply_reduce_fusion.6
  97.9 0.1 pad.5.clone
  98.0 1.1 maximum_maximum_fusion.routes_w
  99.1 108.7 %experts.1 = (bf16[1024,1408]{1,0:T(8,128)(2,1)}, bf16[2,1024,1408]{2,1,0:T(8,128)(2,1)}, bf16[1024,704]{1,0:T(8,128)(2,1)}, bf16[2,1024,704]{2,1,0:T(8,128)(2,1...) custom-call(bf16[128,2048]{1,0:T(8,128)(2,1)} %get-tuple-element.58., ...), custom_call_target="tpu_custom_call" | custom-call | flops 1000000 | bytes 100000 | tf_op jit(solution)/shard_map/experts/pallas_call | solution.py:1199
  207.8 0.0 copy-start.19
  207.8 51.5 %reduce_and_weights.1 = (f32[128,2048]{1,0:T(8,128)}, bf16[2,512,1408]{2,1,0:T(8,128)(2,1)}, bf16[2,512,1408]{2,1,0:T(8,128)(2,1)}, bf16[1408,512]{1,0:T(8,128)(...) custom-call(bf16[1024,2048]{1,0:T(8,128)(2,1)} %get-tuple-element.59, ...), custom_call_target="tpu_custom_call" | custom-call | flops 1000000 | bytes 100000 | tf_op jit(solution)/shard_map/reduce_and_weights/pallas_call | solution.py:999
  259.4 0.0 copy-start.5
  259.4 1.7 multiply_reduce_fusion.4
  261.1 1.1 fusion.31.g_own
  262.3 73.1 %attend_backward.1 = (bf16[1024,768]{1,0:T(8,128)(2,1)}, f32[1,768]{1,0:T(1,128)}, bf16[1024,2048]{1,0:T(8,128)(2,1)}, bf16[1024,2048]{1,0:T(8,128)(2,1)}, bf16[2,512,1408]{2,1,0:T(8,128)(2,1)}) custom-call(bf16[128,2048]{1,0:T(8,128)(2,1)} %fusion.31.g_own, bf16[4,2048,512]{2,1,0:T(8,128)(2,1)} %get-tuple-element.67.w_all, bf16[2048,768]{1,0:T(8,128)(2,1)} %bitcast.40, ...), custom_call_target="tpu_custom_call" | custom-call | flops 1000000 | bytes 100000 | tf_op jit(solution)/shard_map/attend_backward/pallas_call | solution.py:646
  335.4 2.4 convolution_convert_fusion.1
  337.8 0.0 collective-permute-start.1
  337.8 4.2 fusion.33
  342.0 0.5 collective-permute-start
  342.5 2.4 convolution_convert_fusion
  344.9 0.0 collective-permute-start.3
  344.9 4.0 fusion.15
  348.8 0.5 compare_convert_fusion.2
  349.4 0.7 fusion.6
  350.1 4.1 fusion.17
  354.1 1.3 fusion.34
  355.4 0.5 copy-done.8
  355.9 0.9 copy-done.9
  356.8 3.1 add_bitcast_fusion
  359.9 0.5 add_rsqrt_fusion
  360.4 0.5 compare_convert_fusion
  360.9 2.0 fusion.8
  362.9 0.0 collective-permute-done.1
  362.9 2.6 add_convert_fusion.2.refs_8_
  365.5 0.0 collective-permute-done
  365.6 0.0 copy-start.33
  365.6 0.0 copy-start.34
  365.6 0.0 copy-start.35
  365.6 0.0 copy-start.20
  365.6 6.8 %multiply_reduce_fusion.3 = (f32[512]{0:T(512)S(1)}, f32[512]{0:T(512)S(1)}, f32[512]{0:T(512)S(1)}, f32[512]{0:T(512)S(1)}, bf16[512,768]{1,0:T(8,128)(2,1)}, /*index=5*/bf16[512,768]{1,0:T(8,128)(2,1)}, f32[512,768]{1,0:T(8,128)}) fusion(f32[512,768]{1,0:T(8,128)} %get-tuple-element.115, bf16[2048,768]{1,0:T(8,128)(2,1)S(1)} %bitcast.41, ...), kind=kOutput, calls=%fused_computation.8 | convolution fusion | flops 811595776 | bytes 14428672 | tf_op jit(solution)/shard_map/dot_general | solution.py:30
  372.5 0.1 add_bitcast_fusion.3
  372.6 0.7 pad_maximum_fusion.refs_2_
  373.2 112.1 %reduce_rows.1 = (f32[128,2048]{1,0:T(8,128)}, f32[128,2048]{1,0:T(8,128)}, f32[11,2048]{1,0:T(8,128)}, f32[1,768]{1,0:T(1,128)}, bf16[1408,512]{1,0:T(8,128)(2,...) custom-call(bf16[1024,2048]{1,0:T(8,128)(2,1)} %get-tuple-element.76, ...), custom_call_target="tpu_custom_call" | custom-call | flops 1000000 | bytes 100000 | tf_op jit(solution)/shard_map/reduce_rows/pallas_call | solution.py:850
  485.4 1.7 slice_bitcast_fusion
  487.1 1.5 fusion.32
  488.6 0.0 collective-permute-start.2
  488.6 1.5 fusion.2
  490.2 3.5 add_bitcast_fusion.2
  493.7 1.6 fusion.5
  495.4 1.3 convert_add_fusion.1
  496.7 0.0 collective-permute-done.3
  496.7 0.9 convert_add_fusion.2
  497.6 0.1 reshape.114
  497.7 0.6 constant_dynamic-slice_fusion
  498.3 2.0 add_bitcast_fusion.1
  500.3 0.0 collective-permute-done.2
  500.3 0.2 copy-done.14
  500.5 1.4 convert_add_fusion
  502.0 2.0 reshape.113
  (72 shorter events, 0.2 us)
Async XLA Ops:
  0.7 4.3 copy-start.22
  0.7 5.4 %copy-start.27 = (f32[2,384]{1,0:T(2,128)S(1)}, f32[2,384]{1,0:T(2,128)}, u32[]{:S(2)}) copy-start(f32[2,384]{1,0:T(2,128)} %param.21) | copy-start | bytes 9220
  0.7 5.9 %copy-start.26 = (bf16[2048]{0:T(1024)(128)(2,1)S(1)}, bf16[2048]{0:T(1024)(128)(2,1)}, u32[]{:S(2)}) copy-start(bf16[2048]{0:T(1024)(128)(2,1)} %param.27) | copy-start | bytes 12292
  0.7 6.3 %copy-start.21 = (bf16[2048,8]{0,1:T(8,128)(2,1)S(1)}, bf16[2048,8]{0,1:T(8,128)(2,1)}, u32[]{:S(2)}) copy-start(bf16[2048,8]{0,1:T(8,128)(2,1)} %param.24) | copy-start | bytes 98308
  0.7 6.5 %copy-start.23 = (s32[1024,4]{0,1:T(4,128)S(1)}, s32[1024,4]{0,1:T(4,128)}, u32[]{:S(2)}) copy-start(s32[1024,4]{0,1:T(4,128)} %param.17) | copy-start | bytes 49156
  97.9 163.2 %copy-start.24 = (f32[128]{0:T(128)}, f32[128]{0:T(128)S(1)}, u32[]{:S(2)}) copy-start(f32[128]{0:T(128)S(1)} %add_rsqrt_fusion.1) | copy-start | bytes 1540
  207.8 51.6 %copy-start.1 = (f32[128,2048]{1,0:T(8,128)S(1)}, f32[128,2048]{1,0:T(8,128)}, u32[]{:S(2)}) copy-start(f32[128,2048]{1,0:T(8,128)} %get-tuple-element.57) | copy-start | bytes 3145732
  207.8 51.6 %copy-start.19 = (f32[2048]{0:T(1024)S(1)}, f32[2048]{0:T(1024)}, u32[]{:S(2)}) copy-start(f32[2048]{0:T(1024)} %param.23) | copy-start | bytes 24580
  259.4 1.7 copy-start.2
  259.4 1.7 copy-start.5
  261.1 74.3 %copy-start.29 = (f32[128]{0:T(128)}, f32[128]{0:T(128)S(1)}, u32[]{:S(2)}) copy-start(f32[128]{0:T(128)S(1)} %broadcast_multiply_fusion.1) | copy-start | bytes 1540
  262.3 73.2 %copy-start.17 = (bf16[1024,256]{1,0:T(8,128)(2,1)S(1)}, bf16[1024,256]{1,0:T(8,128)(2,1)}, u32[]{:S(2)}) copy-start(bf16[1024,256]{1,0:T(8,128)(2,1)} %get-tuple-element.85) | copy-start | bytes 1572868
  337.8 25.1 %collective-permute-start.1 = (bf16[256,512]{1,0:T(8,128)(2,1)}, bf16[256,512]{1,0:T(8,128)(2,1)}, u32[]{:S(2)}, u32[]{:S(2)}) collective-permute-start(bf16[256,512]{1,0:T(8,128)(2,1)} %convolution_convert_fusion.1), channel_id=1, source_target_pairs={{0,8},{8,0},{16,24},{24,16},{1,9},{9,1},{17,25},{25,17},{2,10},{10... | collective-permute-start | bytes 786440 | tf_op jit(solution)/shard_map/ppermute | solution.py:43
  342.0 23.6 %collective-permute-start = (bf16[512,768]{1,0:T(8,128)(2,1)}, bf16[512,768]{1,0:T(8,128)(2,1)}, u32[]{:S(2)}, u32[]{:S(2)}) collective-permute-start(bf16[512,768]{1,0:T(8,128)(2,1)} %get-tuple-element.114), channel_id=1, source_target_pairs={{0,8},{8,0},{16,24},{24,16},{1,9},{9,1},{17,25},{25,17},{2,10},{10... | collective-permute-start | bytes 2359304 | tf_op jit(solution)/shard_map/ppermute | solution.py:43
  344.9 151.9 %collective-permute-start.3 = (bf16[256,512]{1,0:T(8,128)(2,1)}, bf16[256,512]{1,0:T(8,128)(2,1)S(1)}, u32[]{:S(2)}, u32[]{:S(2)}) collective-permute-start(bf16[256,512]{1,0:T(8,128)(2,1)} %convolution_convert_fusion), channel_id=1, source_target_pairs={{0,8},{8,0},{16,24},{24,16},{1,9},{9,1},{17,25},{25,17},{2,10},{10... | collective-permute-start | bytes 786440 | tf_op jit(solution)/shard_map/ppermute | solution.py:43
  344.9 4.5 copy-start.3
  350.1 4.1 copy-start.6
  350.1 4.1 copy-start.37
  354.1 1.8 copy-start.8
  354.1 2.7 copy-start.9
  356.8 3.1 copy-start.36
  360.9 4.6 copy-start
  365.5 6.9 %copy-start.32 = (f32[4]{0:T(128)S(1)}, f32[4]{0:T(128)}, u32[]{:S(2)}) copy-start(f32[4]{0:T(128)} %get-tuple-element.119) | copy-start | bytes 52
  365.6 6.9 %copy-start.33 = (f32[4]{0:T(128)S(1)}, f32[4]{0:T(128)}, u32[]{:S(2)}) copy-start(f32[4]{0:T(128)} %get-tuple-element.120) | copy-start | bytes 52
  365.6 6.9 %copy-start.34 = (f32[4]{0:T(128)S(1)}, f32[4]{0:T(128)}, u32[]{:S(2)}) copy-start(f32[4]{0:T(128)} %get-tuple-element.117) | copy-start | bytes 52
  365.6 6.9 %copy-start.35 = (f32[4]{0:T(128)S(1)}, f32[4]{0:T(128)}, u32[]{:S(2)}) copy-start(f32[4]{0:T(128)} %get-tuple-element.118) | copy-start | bytes 52
  365.6 7.0 %copy-start.20 = (f32[2048]{0:T(1024)S(1)}, f32[2048]{0:T(1024)}, u32[]{:S(2)}) copy-start(f32[2048]{0:T(1024)} %param.19) | copy-start | bytes 24580
  373.2 115.3 %copy-start.31 = (f32[128]{0:T(128)S(1)}, f32[128]{0:T(128)}, u32[]{:S(2)}) copy-start(f32[128]{0:T(128)} %add_rsqrt_fusion) | copy-start | bytes 1540
  485.4 4.7 copy-start.11
  488.6 11.7 %collective-permute-start.2 = (bf16[512,768]{1,0:T(8,128)(2,1)}, bf16[512,768]{1,0:T(8,128)(2,1)}, u32[]{:S(2)}, u32[]{:S(2)}) collective-permute-start(bf16[512,768]{1,0:T(8,128)(2,1)} %get-tuple-element.107), channel_id=1, source_target_pairs={{0,8},{8,0},{16,24},{24,16},{1,9},{9,1},{17,25},{25,17},{2,10},{10... | collective-permute-start | bytes 2359304 | tf_op jit(solution)/shard_map/ppermute | solution.py:43
  490.1 3.6 copy-start.7
  490.1 3.6 copy-start.13
  490.2 3.5 copy-start.25
  490.2 3.5 copy-start.30
  493.7 1.7 copy-start.15
  493.7 1.7 copy-start.16
  495.4 1.4 copy-start.18
  495.4 2.2 copy-start.28
  495.4 2.9 copy-start.10
  495.4 2.9 copy-start.12
  498.3 2.0 copy-start.4
  498.3 2.2 copy-start.14

commit v4 on v3

--- a/solution.py
+++ b/solution.py
@@ -788,7 +788,40 @@
                 self.copy(step, way).wait_send()
 
 
-def reduce_kernel(count, grp_count, number, bulk_number, small_axes, *refs):
+def reduce_kernel(count, part, out, to_right, to_left, send_sems, recv_sems):
+    greet("ep", count)
+    pl.semaphore_wait(pltpu.get_barrier_semaphore(), count - 1)
+    ring = RingSum(count, part, out, to_right, to_left, send_sems, recv_sems)
+    ring.start()
+    for step in range(1, count // 2):
+        ring.advance(step)
+    ring.last()
+    ring.finish()
+
+
+def reduce_rows(count, part):
+    tokens, width = part.shape
+    size, half = tokens // count, count // 2
+    whole = pl.BlockSpec(memory_space=pltpu.VMEM)
+    return pl.pallas_call(
+        functools.partial(reduce_kernel, count),
+        in_specs=[whole],
+        out_specs=whole,
+        out_shape=jax.ShapeDtypeStruct((size, width), F32),
+        scratch_shapes=[pltpu.VMEM((half, size, width), BF16)] * 2
+        + [pltpu.SemaphoreType.DMA((half, 2))] * 2,
+        compiler_params=pltpu.CompilerParams(
+            collective_id=3, has_side_effects=True, vmem_limit_bytes=56 * MIB
+        ),
+        cost_estimate=KERNEL_COST,
+        name="reduce_rows",
+    )(part)
+
+
+def finish_kernel(
+    count, grp_count, bulk_number, branch, out_parts, small, bias, gain, g_qkv, attended, w,
+    x_in, attn_in, *refs
+):
     refs = list(refs)
 
     def take(amount):
@@ -796,35 +829,100 @@
         del refs[:amount]
         return taken
 
-    small_number = len(small_axes)
-    parts, smalls, bulk = take(number), take(small_number), take(bulk_number)
-    outs, small_outs, landed = take(number), take(small_number), take(bulk_number)
-    to_right, to_left = take(number), take(number)
-    small_held, small_arrived = take(small_number), take(small_number)
-    send_sems, recv_sems = take(2)
-    small_sems = take(small_number)
-    (plane_sems,) = take(1)
+    planes = grp_count // 2
+    far_number = planes - 1
+    bulk = take(bulk_number)
+    branch_sum, out_sum, small_sum, bias_sum, own_q, own_o = take(6)
+    landed = take(bulk_number + 2 * far_number)
+    rings_held = take(4)
+    x, attn = take(2)
+    away, arrived, far = take(2), take(2), take(2)
+    small_held, small_arrived, bias_held, bias_arrived = take(4)
+    (
+        send_sems, recv_sems, small_sems, bias_sems, plane_sems, load_sems, core_send, core_recv
+    ) = take(8)
+    mine = lax.axis_index("grp")
+    core, plane = mine % 2, mine // 2
+    part_width = x.shape[2]
+    orders = list(range(1, planes)) + [0]
+    units = [(side, place) for side in (1, 0) for place in range(planes)]
+
+    def columns(unit):
+        side, place = units[unit]
+        member = 2 * ((plane + orders[place]) % planes) + (core if side == 0 else 1 - core)
+        return pl.ds(pl.multiple_of(member * part_width, part_width), part_width)
+
+    def loads(unit):
+        slot = unit % 2
+        return [
+            pltpu.make_async_copy(
+                source.at[:, columns(unit)], target.at[slot], load_sems.at[i, slot]
+            )
+            for i, (source, target) in enumerate(((x_in, x), (attn_in, attn)))
+        ]
+
+    for unit in range(2):
+        for load in loads(unit):
+            load.start()
     greet("ep", count)
     greet("grp", grp_count)
-    for held, small in zip(small_held, smalls):
-        held[0] = small[...]
+    small_held[0] = small[...]
+    bias_held[0] = bias[...]
     pl.semaphore_wait(pltpu.get_barrier_semaphore(), count - 1 + grp_count - 1)
     rings = [
         RingSum(
-            count, parts[a], outs[a], to_right[a], to_left[a], send_sems.at[a], recv_sems.at[a]
-        )
-        for a in range(number)
-    ]
-    sums = [
-        Doubling(held, arrived, doubling_stages(axes), sems)
-        for held, arrived, axes, sems in zip(small_held, small_arrived, small_axes, small_sems)
+            count, part, out, rings_held[2 * a], rings_held[2 * a + 1], send_sems.at[a],
+            recv_sems.at[a],
+        )
+        for a, (part, out) in enumerate(((branch, branch_sum), (out_parts, out_sum)))
     ]
     for ring in rings:
         ring.start()
-    for item in sums:
-        item.start()
-    plane_copies = PlaneCopies(bulk, landed, grp_count // 2, plane_sems)
-    plane_copies.start()
+    sums = [
+        Doubling(small_held, small_arrived, doubling_stages(("grp", "ep")), small_sems),
+        Doubling(bias_held, bias_arrived, doubling_stages(("grp",)), bias_sems),
+    ]
+    sums[1].start()
+
+    def to_core(kind, place):
+        return pltpu.make_async_remote_copy(
+            src_ref=away[kind].at[place],
+            dst_ref=arrived[kind].at[place],
+            send_sem=core_send.at[kind, place],
+            recv_sem=core_recv.at[kind, place],
+            device_id={"grp": mine + 1 - 2 * core},
+            device_id_type=MESH,
+        )
+
+    for unit, (side, place) in enumerate(units):
+        cut, slot = columns(unit), unit % 2
+        for load in loads(unit):
+            load.wait()
+        q_piece = dot_tn(x[slot], g_qkv[...])
+        inner = jnp.sum(q_piece * w[cut, :].astype(F32), -1, keepdims=True)
+        inner = jnp.transpose(jnp.broadcast_to(inner, (part_width, LANES)))[:1, :]
+        small_held[0, 1:2, cut] = inner / gain[:, cut]
+        o_piece = dot_tn(attended[...], attn[slot])
+        for kind, piece in enumerate((q_piece, o_piece)):
+            if side == 1:
+                away[kind][place] = piece.astype(BF16)
+                to_core(kind, place).start()
+            else:
+                to_core(kind, place).wait_recv()
+                piece = piece + arrived[kind][place].astype(F32)
+                if orders[place]:
+                    far[kind][place] = piece.astype(BF16)
+                else:
+                    (own_q, own_o)[kind][...] = piece
+        if unit + 2 < len(units):
+            for load in loads(unit + 2):
+                load.start()
+    sums[0].start()
+    far_copies = PlaneCopies(
+        [far[kind].at[place] for kind in range(2) for place in range(far_number)] + bulk,
+        landed, planes, plane_sems,
+    )
+    far_copies.start()
     for step in range(1, count // 2):
         for ring in rings:
             ring.advance(step)
@@ -832,46 +930,63 @@
                 item.advance()
     for ring in rings:
         ring.last()
-    for item, out in zip(sums, small_outs):
-        out[...] = item.finish()
+    small_sum[...] = sums[0].finish()
+    bias_sum[...] = sums[1].finish()
     for ring in rings:
         ring.finish()
-    plane_copies.finish()
-
-
-def reduce_rows(count, grp_count, call, parts, smalls=(), small_axes=(), bulk=()):
-    tokens, width = parts[0].shape
-    size, number, half = tokens // count, len(parts), count // 2
-    stages = [len(doubling_stages(axes)) for axes in small_axes]
+    for kind in range(2):
+        for place in range(planes):
+            to_core(kind, place).wait_send()
+    far_copies.finish()
+
+
+def finish(
+    count, grp_count, branch, out_parts, small, bias, gain, g_qkv, attended, w, x, attn, bulk
+):
+    tokens, width = branch.shape
+    size, half, planes = tokens // count, count // 2, grp_count // 2
+    part_width = width // grp_count
+    q_shape, o_shape = (part_width, g_qkv.shape[1]), (attended.shape[1], part_width)
+    stages = len(doubling_stages(("grp", "ep"))), len(doubling_stages(("grp",)))
     anywhere = pl.BlockSpec(memory_space=pl.ANY)
     whole = pl.BlockSpec(memory_space=pltpu.VMEM)
     shape = jax.ShapeDtypeStruct
     dma = pltpu.SemaphoreType.DMA
+    landed = [shape(dims, BF16) for dims in (q_shape, o_shape) for _ in range(planes - 1)]
+    landed += [shape(value.shape, value.dtype) for value in bulk]
     results = pl.pallas_call(
-        functools.partial(
-            reduce_kernel, count, grp_count, number, len(bulk), tuple(small_axes)
-        ),
-        in_specs=[whole] * (number + len(smalls)) + [anywhere] * len(bulk),
-        out_specs=[whole] * (number + len(smalls)) + [anywhere] * len(bulk),
-        out_shape=[shape((size, width), F32)] * number
-        + [shape(value.shape, value.dtype) for value in (*smalls, *bulk)],
-        scratch_shapes=[pltpu.VMEM((half, size, width), BF16)] * (2 * number)
-        + [pltpu.VMEM((k + 1, *value.shape), F32) for k, value in zip(stages, smalls)]
-        + [pltpu.VMEM((k, *value.shape), F32) for k, value in zip(stages, smalls)]
-        + [dma((number, half, 2))] * 2
-        + [dma((2, k)) for k in stages]
-        + [dma((2, max(len(bulk), 1)))],
+        functools.partial(finish_kernel, count, grp_count, len(bulk)),
+        in_specs=[whole] * 8 + [anywhere] * (2 + len(bulk)),
+        out_specs=[whole] * 6 + [anywhere] * len(landed),
+        out_shape=[
+            shape((size, width), F32),
+            shape((size, width), F32),
+            shape(small.shape, F32),
+            shape(bias.shape, F32),
+            shape(q_shape, F32),
+            shape(o_shape, F32),
+            *landed,
+        ],
+        scratch_shapes=[pltpu.VMEM((half, size, width), BF16)] * 4
+        + [pltpu.VMEM((2, tokens, part_width), BF16)] * 2
+        + [pltpu.VMEM((planes, *dims), BF16) for dims in (q_shape, o_shape)] * 2
+        + [pltpu.VMEM((max(planes - 1, 1), *dims), BF16) for dims in (q_shape, o_shape)]
+        + [
+            pltpu.VMEM((stages[0] + 1, *small.shape), F32),
+            pltpu.VMEM((stages[0], *small.shape), F32),
+            pltpu.VMEM((stages[1] + 1, *bias.shape), F32),
+            pltpu.VMEM((stages[1], *bias.shape), F32),
+        ]
+        + [dma((2, half, 2))] * 2
+        + [dma((2, stages[0])), dma((2, stages[1])), dma((2, len(landed))), dma((2, 2))]
+        + [dma((2, planes))] * 2,
         compiler_params=pltpu.CompilerParams(
-            collective_id=call, has_side_effects=True, vmem_limit_bytes=56 * MIB
+            collective_id=4, has_side_effects=True, vmem_limit_bytes=60 * MIB
         ),
         cost_estimate=KERNEL_COST,
-        name="reduce_rows",
-    )(*parts, *smalls, *bulk)
-    return (
-        results[:number],
-        results[number : number + len(smalls)],
-        results[number + len(smalls) :],
-    )
+        name="finish",
+    )(branch, out_parts, small, bias, gain, g_qkv, attended, w, x, attn, *bulk)
+    return results[:6], results[6:]
 
 
 def reduce_and_weights_kernel(
@@ -886,13 +1001,14 @@
 
     planes = grp_count // 2
     (summed,) = take(1)
-    outs = [take(planes) for _ in range(4)]
+    outs = [take(planes) for _ in range(5)]
+    landed = take(planes - 1)
     sources = (x_in, grad_e_in, cot_in, act_e_in, grad_s_in, act_s_in)
     held = take(6)
     x, grad_e, cot, act_e, grad_s, act_s = held
     to_right, to_left = take(2)
-    staged, arrived = take(4), take(4)
-    send_sems, recv_sems, load_sems, core_send, core_recv, out_sems = take(6)
+    staged, arrived = take(5), take(5)
+    send_sems, recv_sems, load_sems, core_send, core_recv, out_sems, plane_sems = take(7)
     mine = lax.axis_index("grp")
     core, plane = mine % 2, mine // 2
     part_width = x.shape[1] // grp_count
@@ -914,11 +1030,11 @@
         return pl.ds(pl.multiple_of(member * part_width, part_width), part_width)
 
     def products(kind, cut):
-        if kind == 0:
-            return [dot_tn(x[:, cut], grad_e[k]) for k in range(2)]
-        if kind == 1:
+        if kind < 2:
+            return [dot_tn(x[:, cut], grad_e[kind])]
+        if kind == 2:
             return [dot_tn(act_e[...], cot[:, cut])]
-        if kind == 2:
+        if kind == 3:
             return [dot_tn(grad_s[k], x[:, cut]) for k in range(2)]
         return [dot_tn(act_s[...], cot[:, cut])]
 
@@ -936,25 +1052,23 @@
         return pltpu.make_async_copy(staged[kind], outs[kind][place], out_sems.at[kind, place])
 
     orders = list(range(1, planes)) + [0]
-    needs = ((0, 1), (2, 3), (4,), (5,))
+    needs = ((0, 1), (), (2, 3), (4,), (5,))
+    plane_copies = PlaneCopies(outs[0][: planes - 1], landed, planes, plane_sems)
     ring_step = 1
     number = 0
-    for side in (1, 0):
-        for place, order in enumerate(orders):
-            for kind in range(4):
+    for place, order in enumerate(orders):
+        for side in (1, 0):
+            for kind in range(5):
                 if side == 1 and place == 0:
                     for i in needs[kind]:
                         loads[i].wait()
                 pieces = products(kind, columns(order, side))
                 if side == 1:
-                    if place:
-                        to_core(kind, place - 1).wait_send()
+                    if place and kind:
+                        store(kind, place - 1).wait()
                 else:
                     to_core(kind, place).wait_recv()
-                    if place:
-                        store(kind, place - 1).wait()
-                    else:
-                        to_core(kind, planes - 1).wait_send()
+                    to_core(kind, place).wait_send()
                 for k, piece in enumerate(pieces):
                     whole = (k,) if len(pieces) > 1 else (Ellipsis,)
                     if side == 0:
@@ -964,8 +1078,11 @@
                     to_core(kind, place).start()
                 else:
                     store(kind, place).start()
+                if side == 0 and kind == 1 and order:
+                    store(0, place).wait()
+                    plane_copies.copies[place].start()
                 number += 1
-                if number % 4 == 2:
+                if number % 5 == 2:
                     if ring_step < count // 2:
                         ring.advance(ring_step)
                     elif ring_step == count // 2:
@@ -977,9 +1094,10 @@
         else:
             ring.last()
         ring_step += 1
-    for kind in range(4):
+    for kind in range(5):
         store(kind, planes - 1).wait()
     ring.finish()
+    plane_copies.finish()
 
 
 def reduce_and_weights(
@@ -990,7 +1108,8 @@
     part_width = width // grp_count
     wide, narrow = act_e.shape[1], act_s.shape[1]
     shapes = [
-        (2, part_width, wide), (wide, part_width), (2, narrow, part_width), (narrow, part_width)
+        (part_width, wide), (part_width, wide), (wide, part_width), (2, narrow, part_width),
+        (narrow, part_width),
     ]
     anywhere = pl.BlockSpec(memory_space=pl.ANY)
     whole = pl.BlockSpec(memory_space=pltpu.VMEM)
@@ -999,9 +1118,10 @@
     summed, *slices = pl.pallas_call(
         functools.partial(reduce_and_weights_kernel, count, grp_count),
         in_specs=[whole] + [anywhere] * 6,
-        out_specs=[whole] + [anywhere] * (4 * planes),
+        out_specs=[whole] + [anywhere] * (6 * planes - 1),
         out_shape=[shape((size, width), F32)]
-        + [shape(dims, BF16) for dims in shapes for _ in range(planes)],
+        + [shape(dims, BF16) for dims in shapes for _ in range(planes)]
+        + [shape(shapes[0], BF16)] * (planes - 1),
         scratch_shapes=[
             pltpu.VMEM(value.shape, BF16) for value in (x, grad_e, cot, act_e, grad_s, act_s)
         ]
@@ -1009,15 +1129,17 @@
         + [pltpu.VMEM(dims, BF16) for dims in shapes]
         + [pltpu.VMEM((planes, *dims), BF16) for dims in shapes]
         + [dma((half, 2)), dma((half, 2)), dma((6,))]
-        + [dma((4, planes))] * 3,
+        + [dma((5, planes))] * 3
+        + [dma((2, max(planes - 1, 1)))],
         compiler_params=pltpu.CompilerParams(
             collective_id=3, has_side_effects=True, vmem_limit_bytes=60 * MIB
         ),
         cost_estimate=KERNEL_COST,
         name="reduce_and_weights",
     )(part, x, cot, grad_e, act_e, grad_s, act_s)
-    groups = [slices[i * planes : (i + 1) * planes] for i in range(4)]
-    return summed, [group[:-1] for group in groups], [group[-1] for group in groups]
+    groups = [slices[i * planes : (i + 1) * planes] for i in range(5)]
+    passed, own = [group[:-1] for group in groups], [group[-1] for group in groups]
+    return summed, passed, own, slices[5 * planes :]
 
 
 def tiles_of(width):
@@ -1288,27 +1410,26 @@
         expert_gate_up, expert_down, jnp.swapaxes(shared_gate_up, 1, 2), shared_down,
     )
 
-    def expert_gate_up_grad(rows, member):
-        columns = columns_of(rows, member)
-        return jnp.stack([dot_tn(columns, expert_grad[k]) for k in range(2)], 0)
-
-    def shared_gate_up_grad(rows, member):
-        columns = columns_of(rows, member)
-        return jnp.stack([dot_tn(shared_grad[k], columns) for k in range(2)], 0)
-
-    def down_grad(act):
-        return lambda rows, member: dot_tn(act, columns_of(rows, member))
-
-    normal_two, factor_two = norm_of(residual)
-    grad_y = cotangent.astype(F32)
     if ep_count == 8:
-        grad_normed_two, passed, sums_own = reduce_and_weights(
+        grad_normed_two, passed, sums_own, first_landed = reduce_and_weights(
             ep_count, grp_count, part, group_two, group_cot, expert_grad, expert_act,
             shared_grad, shared_act,
         )
     else:
+
+        def up_grad(k):
+            return lambda rows, member: dot_tn(columns_of(rows, member), expert_grad[k])
+
+        def shared_gate_up_grad(rows, member):
+            columns = columns_of(rows, member)
+            return jnp.stack([dot_tn(shared_grad[k], columns) for k in range(2)], 0)
+
+        def down_grad(act):
+            return lambda rows, member: dot_tn(act, columns_of(rows, member))
+
         sums = [
-            GrpReduce(group_two, expert_gate_up_grad),
+            GrpReduce(group_two, up_grad(0)),
+            GrpReduce(group_two, up_grad(1)),
             GrpReduce(group_cot, down_grad(expert_act)),
             GrpReduce(group_two, shared_gate_up_grad),
             GrpReduce(group_cot, down_grad(shared_act)),
@@ -1316,59 +1437,42 @@
         arrived = [[item.to_partner(value) for value in item.away()] for item in sums]
         passed = [item.pass_on(values_) for item, values_ in zip(sums, arrived)]
         sums_own = [item.own() for item in sums]
-        (grad_normed_two,), _, _ = reduce_rows(ep_count, grp_count, 3, [part])
+        grad_normed_two = reduce_rows(ep_count, part)
+        first_landed = None
+    normal_two, factor_two = norm_of(residual)
+    grad_y = cotangent.astype(F32)
     grad_residual = grad_y + norm_back(grad_normed_two, normal_two, factor_two, norm2_gain)
     grad_norm2 = jnp.sum(grad_normed_two * normal_two, 0)
     own_attn = grad_residual.astype(BF16)
     each = grp_count // 2 - 1
 
+    bulk = passed[1] + passed[4] + (passed[0] if first_landed is None else [])
     grad_qkv, grad_bias, grad_branch, group_attn, *landed = attend_backward(
         ep_count, grp_count, own_attn, w_all, w_flat, cosine, sine, queries, key_rows, values,
-        logs, starts, scale, passed[0],
+        logs, starts, scale, bulk,
     )
-    from_planes = [landed]
-    inners = []
-
-    def w_qkv_grad(rows, member):
-        piece = dot_tn(columns_of(rows, member), grad_qkv)
-        start = member * slice_width
-        weights = lax.dynamic_slice_in_dim(w_flat, start, slice_width, 0).astype(F32)
-        place = (jnp.arange(grp_count) == member).astype(F32)
-        inners.append(place[:, None] * jnp.sum(weights * piece, -1)[None, :])
-        return piece
-
-    more = [
-        GrpReduce(group_one, w_qkv_grad),
-        GrpReduce(group_attn, lambda rows, member: dot_tn(attended, columns_of(rows, member))),
-    ]
-    aways = [item.away() for item in more]
-    arrived = [[item.to_partner(v) for v in values_] for item, values_ in zip(more, aways)]
-    more_passed = [item.pass_on(values_) for item, values_ in zip(more, arrived)]
-    more_own = [item.own() for item in more]
+    from_planes = {1: landed[:each], 4: landed[each : 2 * each]}
+    from_planes[0] = landed[2 * each :] if first_landed is None else first_landed
+
     grad_routes = dot_tn(grad_logits, group_two)
     grad_routes = grad_routes[: expert_count + 1] + grad_routes[LANES : LANES + expert_count + 1]
-    grad_norm1 = sum(inners).reshape(width)
-    small = jnp.concatenate([grad_norm2[None], (grad_norm1 / norm1_gain)[None], grad_routes], 0)
-    bulk = [value for values_ in passed[1:] for value in values_]
-    (grad_normed_one, out_sum), (small, bias_total), landed = reduce_rows(
-        ep_count, grp_count, 4, [grad_branch, out_parts], [small, grad_bias],
-        [("grp", "ep"), ("grp",)], bulk + [value for values_ in more_passed for value in values_],
+    small = jnp.concatenate([grad_norm2[None], jnp.zeros((1, width), F32), grad_routes], 0)
+    (grad_normed_one, out_sum, small, bias_total, own_q, own_o), landed = finish(
+        ep_count, grp_count, grad_branch, out_parts, small, grad_bias, norm1_gain[None, :],
+        grad_qkv, attended, w_flat, group_one, group_attn, passed[2] + passed[3],
     )
-    from_planes += [landed[i * each : (i + 1) * each] for i in range(5)]
+    from_q, from_o, from_planes[2], from_planes[3] = [
+        landed[i * each : (i + 1) * each] for i in range(4)
+    ]
     layer_out = (residual + out_sum).astype(BF16)
     normal_one, factor_one = norm_of(hidden_in.astype(F32))
     grad_x = grad_residual + norm_back(grad_normed_one, normal_one, factor_one, norm1_gain)
-
-    (
-        grad_expert_gate_up, grad_expert_down, grad_shared_gate_up, grad_shared_down,
-        grad_w_qkv, grad_w_out,
-    ) = [
-        add_all(own, values_)
-        for own, values_ in zip(sums_own + more_own, from_planes)
+    grad_gate, grad_up, grad_expert_down, grad_shared_gate_up, grad_shared_down = [
+        add_all(own, from_planes[i]) for i, own in enumerate(sums_own)
     ]
+    grad_w_qkv, grad_w_out = add_all(own_q, from_q), add_all(own_o, from_o)
     bias_total = bias_total.reshape(heads, grp_count, qkv_dim // grp_count)
     grad_b = lax.dynamic_index_in_dim(bias_total, lax.axis_index("grp"), 1, keepdims=False)
-    grad_shared_gate_up = jnp.swapaxes(grad_shared_gate_up, 1, 2)
 
     return (
         layer_out,
@@ -1379,10 +1483,10 @@
         grad_w_out.reshape(heads, head_dim, slice_width),
         small[0],
         small[2 : expert_count + 2].T,
-        grad_shared_gate_up,
+        jnp.swapaxes(grad_shared_gate_up, 1, 2),
         grad_shared_down,
         small[expert_count + 2],
-        grad_expert_gate_up[None],
+        jnp.stack([grad_gate, grad_up], 0)[None],
         grad_expert_down[None],
     )
 

time: 510 us -> 472 us (0.925)
  matrix products: 29.6 us -> 3.58 us
  Pallas kernels: 434 us -> 426 us
    dot_general x9 -> x1, matrix products: 29.6 us -> 3.58 us  [dot_tn(): lax.dot_general(lhs, rhs, (((0,), (0,)), ((), ())), preferred_element_typ...]
    pallas_call x1, Pallas kernels: 73.1 us -> 65 us  [attend_backward(): pl.pallas_call(functools.partial(attend_backward_kernel, count, grp_count...]
  transfers between devices with their start and end apart: 4 -> 0, of which waited for: 0 -> 0; matrix products, arithmetic and copies ran while one was open for 10% -> 0% of each run, Pallas kernels for 22% -> 0%
where the time goes in v4:
time: 472 us; the launch traced here: 467 us
  Pallas kernels  426 us (90%)
  other arithmetic  22.6 us (5%)
  local copies, waits for them, and re-layouts  13.5 us (3%)
    pallas_call x1, Pallas kernels, finish(): pl.pallas_call(functools.partial(finish_kernel, count, grp_count, len(bul...  110 us
    pallas_call x1, Pallas kernels, experts(): pl.pallas_call(functools.partial(experts_kernel, count, expert_count), in...  109 us
    pallas_call x1, Pallas kernels, attend_forward(): pl.pallas_call(functools.partial(attend_forward_kernel, count, grp_count,...  88.2 us
    pallas_call x1, Pallas kernels, attend_backward(): pl.pallas_call(functools.partial(attend_backward_kernel, count, grp_count...  65 us
    pallas_call x1, Pallas kernels, reduce_and_weights(): pl.pallas_call(functools.partial(reduce_and_weights_kernel, count, grp_co...  53.8 us

profile of v4, /device:TPU:0, one launch (start us, length us, event | category | flops | bytes accessed | tf_op | source)
XLA Modules:
  0.0 466.9 jit_solution(12517995547025155488)
XLA Ops:
  0.6 0.0 copy-start.20
  0.7 0.0 copy-start.23
  0.7 4.2 copy.34
  4.9 0.0 copy-done.20
  4.9 1.0 copy.30.segments
  5.9 0.0 copy-done.23
  5.9 0.6 copy.35
  6.5 88.2 %attend_forward.1 = (bf16[2,1024,128]{2,1,0:T(8,128)(2,1)}, bf16[2,1024,128]{2,1,0:T(8,128)(2,1)}, bf16[2,1024,128]{2,1,0:T(8,128)(2,1)}, bf16[1024,256]{1,0:T(8...) custom-call(bf16[128,2048]{1,0:T(8,128)(2,1)} %hidden.1, ...), custom_call_target="tpu_custom_call" | custom-call | flops 1000000 | bytes 100000 | tf_op jit(solution)/shard_map/attend_forward/pallas_call | solution.py:461
  94.7 0.0 copy-done.22
  94.7 0.3 broadcast_in_dim.47
  95.1 0.0 copy-done.19
  95.1 0.3 copy.31
  95.4 0.1 pad.7.clone
  95.4 1.1 maximum_maximum_fusion.routes_w
  96.6 0.0 copy-done.21
  96.6 1.0 copy.33.routes
  97.6 108.7 %experts.1 = (bf16[1024,1408]{1,0:T(8,128)(2,1)}, bf16[2,1024,1408]{2,1,0:T(8,128)(2,1)}, bf16[1024,704]{1,0:T(8,128)(2,1)}, bf16[2,1024,704]{2,1,0:T(8,128)(2,1...) custom-call(bf16[128,2048]{1,0:T(8,128)(2,1)} %get-tuple-element.62., ...), custom_call_target="tpu_custom_call" | custom-call | flops 1000000 | bytes 100000 | tf_op jit(solution)/shard_map/experts/pallas_call | solution.py:1321
  206.3 0.0 copy-start
  206.3 0.0 copy-start.17
  206.3 53.8 %reduce_and_weights.1 = (f32[128,2048]{1,0:T(8,128)}, bf16[512,1408]{1,0:T(8,128)(2,1)}, bf16[512,1408]{1,0:T(8,128)(2,1)}, bf16[512,1408]{1,0:T(8,128)(2,1)}, b...) custom-call(bf16[1024,2048]{1,0:T(8,128)(2,1)} %get-tuple-element.63, ...), custom_call_target="tpu_custom_call" | custom-call | flops 1000000 | bytes 100000 | tf_op jit(solution)/shard_map/reduce_and_weights/pallas_call | solution.py:1118
  260.2 0.0 copy-start.25
  260.2 0.0 copy-done
  260.2 0.2 multiply_reduce_fusion.2
  260.3 0.0 copy-done.17
  260.4 1.6 multiply_reduce_fusion
  261.9 0.0 copy-done.25
  261.9 0.0 copy-start.1
  261.9 0.0 copy-start.3
  262.0 3.6 fusion.9
  265.6 0.1 pad.3.clone
  265.6 0.7 pad_maximum_fusion.small
  266.4 0.0 copy-done.1
  266.4 0.0 copy-done.3
  266.4 1.1 fusion.7.g_own
  267.5 65.0 %attend_backward.1 = (bf16[1024,768]{1,0:T(8,128)(2,1)}, f32[1,768]{1,0:T(1,128)}, bf16[1024,2048]{1,0:T(8,128)(2,1)}, bf16[1024,2048]{1,0:T(8,128)(2,1)}, bf16[...) custom-call(bf16[128,2048]{1,0:T(8,128)(2,1)} %fusion.7.g_own, bf16[4,2048,512]{2,1,0:T(8,128)(2,1)} %get-tuple-element.71.w_all, ...), custom_call_target="tpu_custom_call" | custom-call | flops 1000000 | bytes 100000 | tf_op jit(solution)/shard_map/attend_backward/pallas_call | solution.py:646
  332.6 110.0 %finish.1 = (f32[128,2048]{1,0:T(8,128)}, f32[128,2048]{1,0:T(8,128)}, f32[11,2048]{1,0:T(8,128)}, f32[1,768]{1,0:T(1,128)}, f32[512,768]{1,0:T(8,128)}, /*index...) custom-call(bf16[1024,2048]{1,0:T(8,128)(2,1)} %get-tuple-element.81, ...), custom_call_target="tpu_custom_call" | custom-call | flops 1000000 | bytes 100000 | tf_op jit(solution)/shard_map/finish/pallas_call | solution.py:957
  442.5 0.0 copy-start.6
  442.6 0.0 copy-start.7
  442.6 0.0 copy-start.8
  442.6 0.0 copy-start.9
  442.6 4.0 add_bitcast_fusion
  446.5 0.0 copy-done.6
  446.5 0.0 copy-done.7
  446.6 0.0 copy-done.8
  446.6 0.0 copy-done.9
  446.6 0.6 add_bitcast_fusion.1
  447.1 0.0 copy-start.12
  447.1 0.0 copy-start.13
  447.2 2.9 maximum_bitcast_fusion
  450.1 1.3 convert_add_fusion.1
  451.4 0.5 copy-done.5
  451.9 0.5 copy-done.10
  452.4 2.0 add_bitcast_fusion.3
  454.4 0.0 copy-done.14
  454.4 0.9 convert_add_fusion.2
  455.3 1.3 convert_add_fusion
  456.6 2.9 reshape.73
  459.6 0.2 fusion.6
  459.8 1.5 fusion.2
  461.3 3.2 fusion.5
  464.5 0.6 slice_bitcast_fusion
  465.2 0.6 fusion.8
  465.8 0.1 reshape.74
  465.9 0.6 constant_dynamic-slice_fusion
  (29 shorter events, 0.1 us)
Async XLA Ops:
  0.6 4.2 copy-start.20
  0.7 5.2 %copy-start.23 = (f32[2,384]{1,0:T(2,128)S(1)}, f32[2,384]{1,0:T(2,128)}, u32[]{:S(2)}) copy-start(f32[2,384]{1,0:T(2,128)} %param.21) | copy-start | bytes 9220
  4.9 89.8 %copy-start.22 = (bf16[2048]{0:T(1024)(128)(2,1)S(1)}, bf16[2048]{0:T(1024)(128)(2,1)}, u32[]{:S(2)}) copy-start(bf16[2048]{0:T(1024)(128)(2,1)} %param.27) | copy-start | bytes 12292
  6.5 88.6 %copy-start.19 = (bf16[2048,8]{0,1:T(8,128)(2,1)S(1)}, bf16[2048,8]{0,1:T(8,128)(2,1)}, u32[]{:S(2)}) copy-start(bf16[2048,8]{0,1:T(8,128)(2,1)} %param.24) | copy-start | bytes 98308
  6.5 90.1 %copy-start.21 = (s32[1024,4]{0,1:T(4,128)S(1)}, s32[1024,4]{0,1:T(4,128)}, u32[]{:S(2)}) copy-start(s32[1024,4]{0,1:T(4,128)} %param.17) | copy-start | bytes 49156
  206.3 53.9 %copy-start = (f32[128,2048]{1,0:T(8,128)S(1)}, f32[128,2048]{1,0:T(8,128)}, u32[]{:S(2)}) copy-start(f32[128,2048]{1,0:T(8,128)} %get-tuple-element.61) | copy-start | bytes 3145732
  206.3 54.0 %copy-start.17 = (f32[2048]{0:T(1024)S(1)}, f32[2048]{0:T(1024)}, u32[]{:S(2)}) copy-start(f32[2048]{0:T(1024)} %param.23) | copy-start | bytes 24580
  260.2 1.8 copy-start.25
  261.9 4.4 copy-start.1
  261.9 4.4 copy-start.3
  442.5 4.0 copy-start.6
  442.6 4.0 copy-start.7
  442.6 4.0 copy-start.8
  442.6 4.0 copy-start.9
  447.1 2.9 copy-start.12
  447.1 2.9 copy-start.13
  450.1 1.8 copy-start.5
  450.1 2.3 copy-start.10
  452.4 2.0 copy-start.14
  452.4 2.1 copy-start.15
  452.4 2.9 copy-start.4
  452.4 2.9 copy-start.11
  455.3 4.3 copy-start.2
  455.3 4.5 copy-start.16
  461.3 3.2 copy-start.18
  461.3 4.5 copy-start.24

commit v5 on v4

--- a/solution.py
+++ b/solution.py
@@ -178,8 +178,8 @@
             for copy in self.last_sends():
                 copy.start()
 
-    def finish(self):
-        for step in range(self.half - 1):
+    def finish(self, first=0):
+        for step in range(first, self.half - 1):
             for copy in self.sends(step):
                 copy.wait_send()
         for copy in self.last_sends():
@@ -223,10 +223,10 @@
 
 
 class PlaneCopies:
-    def __init__(self, sources, targets, planes, sems):
+    def __init__(self, pairs, planes, sems):
         mine, size = lax.axis_index("grp"), lax.axis_size("grp")
         self.copies = []
-        for i, (source, target) in enumerate(zip(sources, targets)):
+        for i, (source, target) in enumerate(pairs):
             shift = 2 * (i % (planes - 1) + 1)
             self.copies.append(
                 pltpu.make_async_remote_copy(
@@ -239,8 +239,8 @@
                 )
             )
 
-    def start(self):
-        for copy in self.copies:
+    def start(self, first=0, last=None):
+        for copy in self.copies[first:last]:
             copy.start()
 
     def finish(self):
@@ -262,10 +262,11 @@
 
 
 def attend_forward_kernel(
-    count, grp_count, heads, scale, hidden, first_gain, gain, w, b, segments, row_segments, w_out,
+    count, grp_count, heads, scale, hidden, cot_own, first_gain, gain, w, b, segments,
+    row_segments, w_out,
     q_out, k_out, v_out, attended_out, log_out, residual_out, normed_out, cosine, sine, row_starts,
-    x_out, w_all_out, row_positions, starts, xs, w_all, received, x_send, x_recv, w_send, w_recv, plane_send, plane_recv, core_send,
-    core_recv, hand_send, hand_recv, x_sems, w_sems, own_sem,
+    x_out, w_all_out, near_out, row_positions, starts, near, xs, w_all, received, x_send, x_recv, w_send, w_recv, plane_send, plane_recv, core_send,
+    core_recv, hand_send, hand_recv, near_send, near_recv, x_sems, w_sems, own_sem,
 ):
     size, width = hidden.shape
     half = count // 2
@@ -369,7 +370,19 @@
             v_out[h, here, :] = projected[:, base + 2 * dim : base + 3 * dim].astype(BF16)
         return carry
 
+    def to_neighbour(way):
+        return pltpu.make_async_remote_copy(
+            src_ref=cot_own,
+            dst_ref=near.at[pl.ds(way * size, size)],
+            send_sem=near_send.at[way],
+            recv_sem=near_recv.at[way],
+            device_id={"ep": (ring_x.right, ring_x.left)[way]},
+            device_id_type=MESH,
+        )
+
     lax.fori_loop(0, half, project, 0)
+    for way in range(2):
+        to_neighbour(way).start()
     to_core(0).start()
     store_w(0).start()
 
@@ -421,6 +434,10 @@
     for j in range(planes):
         to_core(j).wait_recv()
         store_w(planes + j).start()
+    store_near = pltpu.make_async_copy(near, near_out, own_sem.at[1])
+    for way in range(2):
+        to_neighbour(way).wait_recv()
+    store_near.start()
     mixed = jnp.concatenate([received[slot] for slot in range(count)], 1)
     square = jnp.zeros((size, 1), F32)
     for j in range(grp_count):
@@ -442,12 +459,15 @@
         to_core(j).wait_send()
     for slot in exchange.others():
         exchange.copy(slot).wait_send()
+    for way in range(2):
+        to_neighbour(way).wait_send()
+    store_near.wait()
     ring_x.finish()
     ring_w.finish()
 
 
 def attend_forward(
-    count, grp_count, hidden, first_gain, gain, w, b, w_out, segments, scale
+    count, grp_count, hidden, cot_own, first_gain, gain, w, b, w_out, segments, scale
 ):
     size, width = hidden.shape
     tokens = size * count
@@ -460,8 +480,8 @@
     dma = pltpu.SemaphoreType.DMA
     return pl.pallas_call(
         functools.partial(attend_forward_kernel, count, grp_count, heads, scale),
-        in_specs=[whole] * 7 + [anywhere],
-        out_specs=[whole] * 10 + [anywhere] * 2,
+        in_specs=[whole] * 8 + [anywhere],
+        out_specs=[whole] * 10 + [anywhere] * 3,
         out_shape=(
             shape((heads, tokens, LANES), BF16),
             shape((heads, tokens, LANES), BF16),
@@ -475,10 +495,12 @@
             shape((1, tokens), jnp.int32),
             shape((tokens, width), BF16),
             shape(w_all_shape, BF16),
+            shape((2 * size, width), BF16),
         ),
         scratch_shapes=[
             pltpu.VMEM((1, tokens), jnp.int32),
             pltpu.VMEM((tokens, 1), jnp.int32),
+            pltpu.VMEM((2 * size, width), BF16),
             pltpu.VMEM((tokens, width), BF16),
             pltpu.VMEM(w_all_shape, BF16),
             pltpu.VMEM((count, size, heads * LANES), BF16),
@@ -492,16 +514,21 @@
             dma((planes,)),
             dma((count,)),
             dma((count,)),
+            dma((2,)),
+            dma((2,)),
             dma((half,)),
             dma((grp_count,)),
-            dma((1,)),
+            dma((2,)),
         ],
         compiler_params=pltpu.CompilerParams(
             collective_id=1, has_side_effects=True, vmem_limit_bytes=56 * MIB
         ),
         cost_estimate=KERNEL_COST,
         name="attend_forward",
-    )(hidden, first_gain[None, :], gain[None, :], w, b, segments[:, None], segments[None, :], w_out)
+    )(
+        hidden, cot_own, first_gain[None, :], gain[None, :], w, b, segments[:, None],
+        segments[None, :], w_out,
+    )
 
 
 def attend_backward_kernel(
@@ -541,8 +568,7 @@
     greet("grp", grp_count)
     gs[ring.own(), :] = g_own[...]
     pl.semaphore_wait(pltpu.get_barrier_semaphore(), count - 1 + grp_count - 1)
-    plane_copies = PlaneCopies(bulk, landed, grp_count // 2, plane_sems)
-    ring.start()
+    plane_copies = PlaneCopies(list(zip(bulk, landed)), grp_count // 2, plane_sems)
     plane_copies.start()
     for slot in range(count):
         first = slot_index(count, slot) * size
@@ -570,6 +596,7 @@
     )
     for slot in exchange.others():
         exchange.copy(slot).start()
+    ring.start()
     g_att[(count - 2) * size : (count - 1) * size, :] = outbox[count - 2]
     dk[...] = jnp.zeros_like(dk)
     dv[...] = jnp.zeros_like(dv)
@@ -596,11 +623,11 @@
             dk[h] += dot(g_scores, query)
             dv[h] += dot(weights.astype(BF16), g_block)
 
-        @pl.when(i == 0)
+        @pl.when(i == 1)
         def _():
             next_pair(0)
 
-        @pl.when(i == 2)
+        @pl.when(i == 3)
         def _():
             next_pair(1)
 
@@ -883,6 +910,18 @@
         Doubling(bias_held, bias_arrived, doubling_stages(("grp",)), bias_sems),
     ]
     sums[1].start()
+    halves = bulk_number // 2
+    sources = [bulk[i].at[0] for i in range(halves)]
+    targets = [landed[2 * far_number + i].at[0] for i in range(halves)]
+    for kind in range(2):
+        for place in range(far_number):
+            sources.append(far[kind].at[place])
+            targets.append(landed[kind * far_number + place])
+    sources += [bulk[i].at[1] for i in range(halves)] + bulk[halves:]
+    targets += [landed[2 * far_number + i].at[1] for i in range(halves)]
+    targets += landed[2 * far_number + halves :]
+    far_copies = PlaneCopies(list(zip(sources, targets)), planes, plane_sems)
+    far_copies.start(0, halves)
 
     def to_core(kind, place):
         return pltpu.make_async_remote_copy(
@@ -901,7 +940,7 @@
         q_piece = dot_tn(x[slot], g_qkv[...])
         inner = jnp.sum(q_piece * w[cut, :].astype(F32), -1, keepdims=True)
         inner = jnp.transpose(jnp.broadcast_to(inner, (part_width, LANES)))[:1, :]
-        small_held[0, 1:2, cut] = inner / gain[:, cut]
+        small_held[0, small.shape[0] - 1 :, cut] = inner / gain[:, cut]
         o_piece = dot_tn(attended[...], attn[slot])
         for kind, piece in enumerate((q_piece, o_piece)):
             if side == 1:
@@ -918,16 +957,13 @@
             for load in loads(unit + 2):
                 load.start()
     sums[0].start()
-    far_copies = PlaneCopies(
-        [far[kind].at[place] for kind in range(2) for place in range(far_number)] + bulk,
-        landed, planes, plane_sems,
-    )
-    far_copies.start()
+    far_copies.start(halves)
     for step in range(1, count // 2):
-        for ring in rings:
+        for a, ring in enumerate(rings):
             ring.advance(step)
-            for item in sums:
-                item.advance()
+            if a or step == 1:
+                for item in sums:
+                    item.advance()
     for ring in rings:
         ring.last()
     small_sum[...] = sums[0].finish()
@@ -978,7 +1014,7 @@
             pltpu.VMEM((stages[1], *bias.shape), F32),
         ]
         + [dma((2, half, 2))] * 2
-        + [dma((2, stages[0])), dma((2, stages[1])), dma((2, len(landed))), dma((2, 2))]
+        + [dma((2, stages[0])), dma((2, stages[1])), dma((2, len(landed) + len(bulk) // 2)), dma((2, 2))]
         + [dma((2, planes))] * 2,
         compiler_params=pltpu.CompilerParams(
             collective_id=4, has_side_effects=True, vmem_limit_bytes=60 * MIB
@@ -990,7 +1026,8 @@
 
 
 def reduce_and_weights_kernel(
-    count, grp_count, part, x_in, cot_in, grad_e_in, act_e_in, grad_s_in, act_s_in, *refs
+    count, grp_count, expert_count, part, residual, cot_own, gain, grad_logits, x_in, cot_in,
+    grad_e_in, act_e_in, grad_s_in, act_s_in, *refs
 ):
     refs = list(refs)
 
@@ -1000,11 +1037,12 @@
         return taken
 
     planes = grp_count // 2
-    (summed,) = take(1)
+    grad_residual, own_attn, small = take(3)
     outs = [take(planes) for _ in range(5)]
     landed = take(planes - 1)
     sources = (x_in, grad_e_in, cot_in, act_e_in, grad_s_in, act_s_in)
     held = take(6)
+    (summed,) = take(1)
     x, grad_e, cot, act_e, grad_s, act_s = held
     to_right, to_left = take(2)
     staged, arrived = take(5), take(5)
@@ -1053,7 +1091,7 @@
 
     orders = list(range(1, planes)) + [0]
     needs = ((0, 1), (), (2, 3), (4,), (5,))
-    plane_copies = PlaneCopies(outs[0][: planes - 1], landed, planes, plane_sems)
+    plane_copies = PlaneCopies(list(zip(outs[0][: planes - 1], landed)), planes, plane_sems)
     ring_step = 1
     number = 0
     for place, order in enumerate(orders):
@@ -1085,15 +1123,22 @@
                 if number % 5 == 2:
                     if ring_step < count // 2:
                         ring.advance(ring_step)
-                    elif ring_step == count // 2:
-                        ring.last()
                     ring_step += 1
-    while ring_step <= count // 2:
-        if ring_step < count // 2:
-            ring.advance(ring_step)
-        else:
-            ring.last()
+                if number == 5:
+                    rows = dot_tn(grad_logits[:, :LANES], x[...])
+                    rows = rows + dot_tn(grad_logits[:, LANES:], x[...])
+                    small[: expert_count + 1, :] = rows[: expert_count + 1, :]
+    while ring_step < count // 2:
+        ring.advance(ring_step)
         ring_step += 1
+    ring.last()
+    normal, factor = norm_of(residual[...])
+    total = summed[...]
+    own = cot_own[...].astype(F32) + norm_back(total, normal, factor, gain[...])
+    grad_residual[...] = own
+    own_attn[...] = own.astype(BF16)
+    small[expert_count + 1 : expert_count + 2, :] = jnp.sum(total * normal, 0, keepdims=True)
+    small[expert_count + 2 :, :] = jnp.zeros((1, small.shape[1]), F32)
     for kind in range(5):
         store(kind, planes - 1).wait()
     ring.finish()
@@ -1101,7 +1146,8 @@
 
 
 def reduce_and_weights(
-    count, grp_count, part, x, cot, grad_e, act_e, grad_s, act_s
+    count, grp_count, expert_count, part, residual, cot_own, gain, grad_logits, x, cot, grad_e,
+    act_e, grad_s, act_s,
 ):
     tokens, width = part.shape
     size, half, planes = tokens // count, count // 2, grp_count // 2
@@ -1115,16 +1161,21 @@
     whole = pl.BlockSpec(memory_space=pltpu.VMEM)
     shape = jax.ShapeDtypeStruct
     dma = pltpu.SemaphoreType.DMA
-    summed, *slices = pl.pallas_call(
-        functools.partial(reduce_and_weights_kernel, count, grp_count),
-        in_specs=[whole] + [anywhere] * 6,
-        out_specs=[whole] + [anywhere] * (6 * planes - 1),
-        out_shape=[shape((size, width), F32)]
+    rows = pl.pallas_call(
+        functools.partial(reduce_and_weights_kernel, count, grp_count, expert_count),
+        in_specs=[whole] * 5 + [anywhere] * 6,
+        out_specs=[whole] * 3 + [anywhere] * (6 * planes - 1),
+        out_shape=[
+            shape((size, width), F32),
+            shape((size, width), BF16),
+            shape((expert_count + 3, width), F32),
+        ]
         + [shape(dims, BF16) for dims in shapes for _ in range(planes)]
         + [shape(shapes[0], BF16)] * (planes - 1),
         scratch_shapes=[
             pltpu.VMEM(value.shape, BF16) for value in (x, grad_e, cot, act_e, grad_s, act_s)
         ]
+        + [pltpu.VMEM((size, width), F32)]
         + [pltpu.VMEM((half, size, width), BF16)] * 2
         + [pltpu.VMEM(dims, BF16) for dims in shapes]
         + [pltpu.VMEM((planes, *dims), BF16) for dims in shapes]
@@ -1136,10 +1187,11 @@
         ),
         cost_estimate=KERNEL_COST,
         name="reduce_and_weights",
-    )(part, x, cot, grad_e, act_e, grad_s, act_s)
+    )(part, residual, cot_own, gain, grad_logits, x, cot, grad_e, act_e, grad_s, act_s)
+    rows, slices = rows[:3], list(rows[3:])
     groups = [slices[i * planes : (i + 1) * planes] for i in range(5)]
     passed, own = [group[:-1] for group in groups], [group[-1] for group in groups]
-    return summed, passed, own, slices[5 * planes :]
+    return (*rows, passed, own, slices[5 * planes :])
 
 
 def tiles_of(width):
@@ -1152,8 +1204,8 @@
 
 
 def experts_kernel(
-    count, expert_count, x_own, cot_own, routes, routes_w, gate_up_e, down_e, gate_up_s, down_s,
-    act_e_out, grad_e_out, act_s_out, grad_s_out, part_out, branch_out, logits_out, x_out,
+    count, expert_count, x_own, cot_own, routes, routes_w, near, gate_up_e, down_e, gate_up_s,
+    down_s, act_e_out, grad_e_out, act_s_out, grad_s_out, part_out, branch_out, logits_out, x_out,
     cot_out,
     xs, cots, gate_e, up_e, held_e, gate_s, up_s, held_s, act_e, grad_e, act_s, grad_s, part,
     branch, logits_held, x_send, x_recv, cot_send, cot_recv, weight_sems, out_sems, x_sems,
@@ -1180,13 +1232,16 @@
             ]
         )
     ]
+    load_near = pltpu.make_async_copy(near, cots.at[pl.ds(0, rows)], weight_sems.at[6])
+    load_near.start()
     for load in loads:
         load.start()
     xs[ring_x.own(), :] = x_own[...]
     cots[ring_x.own(), :] = cot_own[...]
     pl.semaphore_wait(barrier, 2)
     ring_x.start()
-    ring_cot.start()
+    load_near.wait()
+    ring_cot.forward(0)
 
     def stores(i):
         here = rows_at(i, rows)
@@ -1226,8 +1281,12 @@
         here = rows_at(i, rows)
         ring_x.arrive(i)
         ring_x.forward(i)
-        ring_cot.arrive(i)
-        ring_cot.forward(i)
+
+        @pl.when(i > 0)
+        def _():
+            ring_cot.arrive(i)
+            ring_cot.forward(i)
+
         for copy in store_rows(i):
             copy.start()
 
@@ -1305,11 +1364,12 @@
         for copy in stores(i):
             copy.wait()
     ring_x.finish()
-    ring_cot.finish()
+    ring_cot.finish(1)
 
 
 def experts(
-    count, expert_count, x_own, cot_own, routes, routes_w, gate_up_e, down_e, gate_up_s, down_s
+    count, expert_count, x_own, cot_own, routes, routes_w, near, gate_up_e, down_e, gate_up_s,
+    down_s,
 ):
     size, width = x_own.shape
     tokens, rows, half = size * count, 2 * size, count // 2
@@ -1320,7 +1380,7 @@
     dma = pltpu.SemaphoreType.DMA
     return pl.pallas_call(
         functools.partial(experts_kernel, count, expert_count),
-        in_specs=[whole] * 4 + [anywhere] * 4,
+        in_specs=[whole] * 4 + [anywhere] * 5,
         out_specs=[anywhere] * 9,
         out_shape=(
             shape((tokens, wide), BF16),
@@ -1353,7 +1413,7 @@
             dma((half, 2)),
             dma((half, 2)),
             dma((half, 2)),
-            dma((6,)),
+            dma((7,)),
             dma((2, 9)),
             dma((2, half)),
         ],
@@ -1362,7 +1422,7 @@
         ),
         cost_estimate=KERNEL_COST,
         name="experts",
-    )(x_own, cot_own, routes, routes_w, gate_up_e, down_e, gate_up_s, down_s)
+    )(x_own, cot_own, routes, routes_w, near, gate_up_e, down_e, gate_up_s, down_s)
 
 
 def norm_of(values):
@@ -1396,9 +1456,9 @@
 
     (
         queries, key_rows, values, attended, logs, residual, normed_two, cosine, sine, starts,
-        group_one, w_all,
+        group_one, w_all, near_cot,
     ) = attend_forward(
-        ep_count, grp_count, hidden_in, norm1_gain, norm2_gain, w_flat, b_flat, w_out_flat,
+        ep_count, grp_count, hidden_in, cotangent, norm1_gain, norm2_gain, w_flat, b_flat, w_out_flat,
         segments, scale,
     )
 
@@ -1406,14 +1466,14 @@
         expert_act, expert_grad, shared_act, shared_grad, part, out_parts, grad_logits,
         group_two, group_cot,
     ) = experts(
-        ep_count, expert_count, normed_two, cotangent, routes, routes_w,
+        ep_count, expert_count, normed_two, cotangent, routes, routes_w, near_cot,
         expert_gate_up, expert_down, jnp.swapaxes(shared_gate_up, 1, 2), shared_down,
     )
 
     if ep_count == 8:
-        grad_normed_two, passed, sums_own, first_landed = reduce_and_weights(
-            ep_count, grp_count, part, group_two, group_cot, expert_grad, expert_act,
-            shared_grad, shared_act,
+        grad_residual, own_attn, small, passed, sums_own, first_landed = reduce_and_weights(
+            ep_count, grp_count, expert_count, part, residual, cotangent, norm2_gain[None, :],
+            grad_logits, group_two, group_cot, expert_grad, expert_act, shared_grad, shared_act,
         )
     else:
 
@@ -1439,11 +1499,15 @@
         sums_own = [item.own() for item in sums]
         grad_normed_two = reduce_rows(ep_count, part)
         first_landed = None
-    normal_two, factor_two = norm_of(residual)
-    grad_y = cotangent.astype(F32)
-    grad_residual = grad_y + norm_back(grad_normed_two, normal_two, factor_two, norm2_gain)
-    grad_norm2 = jnp.sum(grad_normed_two * normal_two, 0)
-    own_attn = grad_residual.astype(BF16)
+        normal_two, factor_two = norm_of(residual)
+        grad_residual = cotangent.astype(F32) + norm_back(
+            grad_normed_two, normal_two, factor_two, norm2_gain
+        )
+        grad_norm2 = jnp.sum(grad_normed_two * normal_two, 0)
+        own_attn = grad_residual.astype(BF16)
+        rows = dot_tn(grad_logits, group_two)
+        rows = rows[: expert_count + 1] + rows[LANES : LANES + expert_count + 1]
+        small = jnp.concatenate([rows, grad_norm2[None], jnp.zeros((1, width), F32)], 0)
     each = grp_count // 2 - 1
 
     bulk = passed[1] + passed[4] + (passed[0] if first_landed is None else [])
@@ -1454,14 +1518,11 @@
     from_planes = {1: landed[:each], 4: landed[each : 2 * each]}
     from_planes[0] = landed[2 * each :] if first_landed is None else first_landed
 
-    grad_routes = dot_tn(grad_logits, group_two)
-    grad_routes = grad_routes[: expert_count + 1] + grad_routes[LANES : LANES + expert_count + 1]
-    small = jnp.concatenate([grad_norm2[None], jnp.zeros((1, width), F32), grad_routes], 0)
     (grad_normed_one, out_sum, small, bias_total, own_q, own_o), landed = finish(
         ep_count, grp_count, grad_branch, out_parts, small, grad_bias, norm1_gain[None, :],
-        grad_qkv, attended, w_flat, group_one, group_attn, passed[2] + passed[3],
+        grad_qkv, attended, w_flat, group_one, group_attn, passed[3] + passed[2],
     )
-    from_q, from_o, from_planes[2], from_planes[3] = [
+    from_q, from_o, from_planes[3], from_planes[2] = [
         landed[i * each : (i + 1) * each] for i in range(4)
     ]
     layer_out = (residual + out_sum).astype(BF16)
@@ -1477,15 +1538,15 @@
     return (
         layer_out,
         grad_x,
-        small[1],
+        small[expert_count + 2],
         grad_w_qkv.reshape(slice_width, heads, qkv_dim),
         grad_b,
         grad_w_out.reshape(heads, head_dim, slice_width),
-        small[0],
-        small[2 : expert_count + 2].T,
+        small[expert_count + 1],
+        small[:expert_count].T,
         jnp.swapaxes(grad_shared_gate_up, 1, 2),
         grad_shared_down,
-        small[expert_count + 2],
+        small[expert_count],
         jnp.stack([grad_gate, grad_up], 0)[None],
         grad_expert_down[None],
     )

time: 472 us -> 454 us (0.962)
  Pallas kernels: 426 us -> 418 us
  other arithmetic: 22.6 us -> 16.8 us
    pallas_call x1, Pallas kernels: 110 us -> 98.2 us  [finish(): pl.pallas_call(functools.partial(finish_kernel, count, grp_count, len(bul...]
    pallas_call x1, Pallas kernels: 109 us -> 97.9 us  [experts(): pl.pallas_call(functools.partial(experts_kernel, count, expert_count), in...]
    pallas_call x1, Pallas kernels: 88.2 us -> 97.9 us  [attend_forward(): pl.pallas_call(functools.partial(attend_forward_kernel, count, grp_count,...]
where the time goes in v5:
time: 454 us; the launch traced here: 448 us
  Pallas kernels  418 us (92%)
  other arithmetic  16.8 us (4%)
  local copies, waits for them, and re-layouts  12.5 us (3%)
    pallas_call x1, Pallas kernels, finish(): pl.pallas_call(functools.partial(finish_kernel, count, grp_count, len(bul...  98.2 us
    pallas_call x1, Pallas kernels, attend_forward(): pl.pallas_call(functools.partial(attend_forward_kernel, count, grp_count,...  97.9 us
    pallas_call x1, Pallas kernels, experts(): pl.pallas_call(functools.partial(experts_kernel, count, expert_count), in...  97.9 us
    pallas_call x1, Pallas kernels, attend_backward(): pl.pallas_call(functools.partial(attend_backward_kernel, count, grp_count...  66.5 us
    pallas_call x1, Pallas kernels, reduce_and_weights(): pl.pallas_call(functools.partial(reduce_and_weights_kernel, count, grp_co...  57.2 us

profile of v5, /device:TPU:0, one launch (start us, length us, event | category | flops | bytes accessed | tf_op | source)
XLA Modules:
  0.0 448.4 jit_solution(10935939217668224813)
XLA Ops:
  0.6 0.0 copy-start.20
  0.7 0.0 copy-start.23
  0.7 4.2 copy.34
  4.9 0.0 copy-done.20
  4.9 1.0 copy.30.segments
  5.9 0.0 copy-done.23
  5.9 0.6 copy.35
  6.5 0.0 copy-start.22
  6.5 97.9 %attend_forward.1 = (bf16[2,1024,128]{2,1,0:T(8,128)(2,1)}, bf16[2,1024,128]{2,1,0:T(8,128)(2,1)}, bf16[2,1024,128]{2,1,0:T(8,128)(2,1)}, bf16[1024,256]{1,0:T(8...) custom-call(bf16[128,2048]{1,0:T(8,128)(2,1)} %hidden.1, ...), custom_call_target="tpu_custom_call" | custom-call | flops 1000000 | bytes 100000 | tf_op jit(solution)/shard_map/attend_forward/pallas_call | solution.py:481
  104.4 0.0 copy-done.22
  104.4 0.3 broadcast_in_dim.37
  104.8 0.0 copy-done.19
  104.8 0.3 copy.31
  105.1 0.1 pad.4.clone
  105.2 1.1 maximum_maximum_fusion.routes_w
  106.3 0.0 copy-done.21
  106.3 1.0 copy.33.routes
  107.3 97.9 %experts.1 = (bf16[1024,1408]{1,0:T(8,128)(2,1)}, bf16[2,1024,1408]{2,1,0:T(8,128)(2,1)}, bf16[1024,704]{1,0:T(8,128)(2,1)}, bf16[2,1024,704]{2,1,0:T(8,128)(2,1...) custom-call(bf16[128,2048]{1,0:T(8,128)(2,1)} %get-tuple-element.65., ...), custom_call_target="tpu_custom_call" | custom-call | flops 1000000 | bytes 100000 | tf_op jit(solution)/shard_map/experts/pallas_call | solution.py:1381
  205.2 57.2 %reduce_and_weights.1 = (f32[128,2048]{1,0:T(8,128)}, bf16[128,2048]{1,0:T(8,128)(2,1)}, f32[11,2048]{1,0:T(8,128)}, bf16[512,1408]{1,0:T(8,128)(2,1)}, bf16[512...) custom-call(bf16[1024,2048]{1,0:T(8,128)(2,1)} %get-tuple-element.67, ...), custom_call_target="tpu_custom_call" | custom-call | flops 1000000 | bytes 100000 | tf_op jit(solution)/shard_map/reduce_and_weights/pallas_call | solution.py:1164
  262.4 66.5 %attend_backward.1 = (bf16[1024,768]{1,0:T(8,128)(2,1)}, f32[1,768]{1,0:T(1,128)}, bf16[1024,2048]{1,0:T(8,128)(2,1)}, bf16[1024,2048]{1,0:T(8,128)(2,1)}, bf16[...) custom-call(bf16[128,2048]{1,0:T(8,128)(2,1)} %get-tuple-element.75.g_own, bf16[4,2048,512]{2,1,0:T(8,128)(2,1)} %get-tuple-element.76.w_all, ...), custom_call_target="tpu_custom_call" | custom-call | flops 1000000 | bytes 100000 | tf_op jit(solution)/shard_map/attend_backward/pallas_call | solution.py:673
  328.9 0.0 copy-start.8
  328.9 98.2 %finish.1 = (f32[128,2048]{1,0:T(8,128)}, f32[128,2048]{1,0:T(8,128)}, f32[11,2048]{1,0:T(8,128)}, f32[1,768]{1,0:T(1,128)}, f32[512,768]{1,0:T(8,128)}, /*index...) custom-call(bf16[1024,2048]{1,0:T(8,128)(2,1)} %get-tuple-element.86, ...), custom_call_target="tpu_custom_call" | custom-call | flops 1000000 | bytes 100000 | tf_op jit(solution)/shard_map/finish/pallas_call | solution.py:993
  427.1 0.0 copy-done.8
  427.1 0.0 copy-start.5
  427.2 0.0 copy-start.6
  427.2 0.0 copy-start.7
  427.2 0.0 copy-start.9
  427.2 3.5 add_bitcast_fusion
  430.7 0.0 copy-done.5
  430.7 0.0 copy-done.6
  430.7 0.0 copy-done.7
  430.7 0.0 copy-done.9
  430.7 0.6 add_bitcast_fusion.1
  431.3 0.0 copy-start.13
  431.3 0.0 copy-start.14
  431.3 2.9 maximum_bitcast_fusion
  434.2 0.0 copy-done.13
  434.2 0.0 copy-done.14
  434.2 1.3 convert_add_fusion.1
  435.6 0.5 copy-done.4
  436.1 0.5 copy-done.10
  436.6 2.0 add_bitcast_fusion.3
  438.6 0.0 copy-done.15
  438.6 0.0 copy-done.16
  438.6 0.9 convert_add_fusion.2
  439.5 0.0 copy-done.3
  439.5 0.0 copy-done.12
  439.5 0.0 copy-start.17
  439.5 0.1 convert_add_fusion
  439.6 2.0 reshape.60
  441.6 0.0 copy-done
  441.6 0.2 fusion.6
  441.8 0.0 copy-done.1
  441.8 0.0 copy-done.17
  441.8 2.8 fusion.2
  444.6 0.0 copy-done.2
  444.6 0.0 copy-done.11
  444.6 1.4 fusion.5
  446.0 0.0 copy-done.18
  446.0 0.6 slice_bitcast_fusion
  446.6 0.6 fusion.7
  447.2 0.0 copy-done.24
  447.3 0.1 reshape.61
  447.3 0.6 constant_dynamic-slice_fusion
  (18 shorter events, 0.1 us)
Async XLA Ops:
  0.6 4.2 copy-start.20
  0.7 5.2 %copy-start.23 = (f32[2,384]{1,0:T(2,128)S(1)}, f32[2,384]{1,0:T(2,128)}, u32[]{:S(2)}) copy-start(f32[2,384]{1,0:T(2,128)} %param.21) | copy-start | bytes 9220
  6.5 98.0 %copy-start.22 = (bf16[2048]{0:T(1024)(128)(2,1)S(1)}, bf16[2048]{0:T(1024)(128)(2,1)}, u32[]{:S(2)}) copy-start(bf16[2048]{0:T(1024)(128)(2,1)} %param.27) | copy-start | bytes 12292
  6.5 98.3 %copy-start.19 = (bf16[2048,8]{0,1:T(8,128)(2,1)S(1)}, bf16[2048,8]{0,1:T(8,128)(2,1)}, u32[]{:S(2)}) copy-start(bf16[2048,8]{0,1:T(8,128)(2,1)} %param.24) | copy-start | bytes 98308
  6.5 99.8 %copy-start.21 = (s32[1024,4]{0,1:T(4,128)S(1)}, s32[1024,4]{0,1:T(4,128)}, u32[]{:S(2)}) copy-start(s32[1024,4]{0,1:T(4,128)} %param.17) | copy-start | bytes 49156
  328.9 98.2 %copy-start.8 = (bf16[1408,512]{1,0:T(8,128)(2,1)S(1)}, bf16[1408,512]{1,0:T(8,128)(2,1)}, u32[]{:S(2)}) copy-start(bf16[1408,512]{1,0:T(8,128)(2,1)} %get-tuple-element.113) | copy-start | bytes 4325380
  427.1 3.6 copy-start.5
  427.2 3.6 copy-start.6
  427.2 3.6 copy-start.7
  427.2 3.6 copy-start.9
  431.3 2.9 copy-start.13
  431.3 2.9 copy-start.14
  434.2 1.8 copy-start.4
  434.2 2.3 copy-start.10
  436.5 2.0 copy-start.15
  436.5 2.1 copy-start.16
  436.5 2.9 copy-start.3
  436.6 2.9 copy-start.12
  439.5 2.2 copy-start
  439.5 2.3 copy-start.1
  439.5 2.3 copy-start.17
  441.6 3.0 copy-start.2
  441.6 3.0 copy-start.11
  444.6 1.4 copy-start.18
  444.6 2.7 copy-start.24

commit v6 on v5

--- a/solution.py
+++ b/solution.py
@@ -178,8 +178,8 @@
             for copy in self.last_sends():
                 copy.start()
 
-    def finish(self, first=0):
-        for step in range(first, self.half - 1):
+    def finish(self):
+        for step in range(self.half - 1):
             for copy in self.sends(step):
                 copy.wait_send()
         for copy in self.last_sends():
@@ -262,11 +262,10 @@
 
 
 def attend_forward_kernel(
-    count, grp_count, heads, scale, hidden, cot_own, first_gain, gain, w, b, segments,
-    row_segments, w_out,
+    count, grp_count, heads, scale, hidden, first_gain, gain, w, b, segments, row_segments, w_out,
     q_out, k_out, v_out, attended_out, log_out, residual_out, normed_out, cosine, sine, row_starts,
-    x_out, w_all_out, near_out, row_positions, starts, near, xs, w_all, received, x_send, x_recv, w_send, w_recv, plane_send, plane_recv, core_send,
-    core_recv, hand_send, hand_recv, near_send, near_recv, x_sems, w_sems, own_sem,
+    x_out, w_all_out, row_positions, starts, xs, w_all, received, x_send, x_recv, w_send, w_recv, plane_send, plane_recv, core_send,
+    core_recv, hand_send, hand_recv, x_sems, w_sems, own_sem,
 ):
     size, width = hidden.shape
     half = count // 2
@@ -370,19 +369,7 @@
             v_out[h, here, :] = projected[:, base + 2 * dim : base + 3 * dim].astype(BF16)
         return carry
 
-    def to_neighbour(way):
-        return pltpu.make_async_remote_copy(
-            src_ref=cot_own,
-            dst_ref=near.at[pl.ds(way * size, size)],
-            send_sem=near_send.at[way],
-            recv_sem=near_recv.at[way],
-            device_id={"ep": (ring_x.right, ring_x.left)[way]},
-            device_id_type=MESH,
-        )
-
     lax.fori_loop(0, half, project, 0)
-    for way in range(2):
-        to_neighbour(way).start()
     to_core(0).start()
     store_w(0).start()
 
@@ -434,10 +421,6 @@
     for j in range(planes):
         to_core(j).wait_recv()
         store_w(planes + j).start()
-    store_near = pltpu.make_async_copy(near, near_out, own_sem.at[1])
-    for way in range(2):
-        to_neighbour(way).wait_recv()
-    store_near.start()
     mixed = jnp.concatenate([received[slot] for slot in range(count)], 1)
     square = jnp.zeros((size, 1), F32)
     for j in range(grp_count):
@@ -459,15 +442,12 @@
         to_core(j).wait_send()
     for slot in exchange.others():
         exchange.copy(slot).wait_send()
-    for way in range(2):
-        to_neighbour(way).wait_send()
-    store_near.wait()
     ring_x.finish()
     ring_w.finish()
 
 
 def attend_forward(
-    count, grp_count, hidden, cot_own, first_gain, gain, w, b, w_out, segments, scale
+    count, grp_count, hidden, first_gain, gain, w, b, w_out, segments, scale
 ):
     size, width = hidden.shape
     tokens = size * count
@@ -480,8 +460,8 @@
     dma = pltpu.SemaphoreType.DMA
     return pl.pallas_call(
         functools.partial(attend_forward_kernel, count, grp_count, heads, scale),
-        in_specs=[whole] * 8 + [anywhere],
-        out_specs=[whole] * 10 + [anywhere] * 3,
+        in_specs=[whole] * 7 + [anywhere],
+        out_specs=[whole] * 10 + [anywhere] * 2,
         out_shape=(
             shape((heads, tokens, LANES), BF16),
             shape((heads, tokens, LANES), BF16),
@@ -495,12 +475,10 @@
             shape((1, tokens), jnp.int32),
             shape((tokens, width), BF16),
             shape(w_all_shape, BF16),
-            shape((2 * size, width), BF16),
         ),
         scratch_shapes=[
             pltpu.VMEM((1, tokens), jnp.int32),
             pltpu.VMEM((tokens, 1), jnp.int32),
-            pltpu.VMEM((2 * size, width), BF16),
             pltpu.VMEM((tokens, width), BF16),
             pltpu.VMEM(w_all_shape, BF16),
             pltpu.VMEM((count, size, heads * LANES), BF16),
@@ -514,21 +492,16 @@
             dma((planes,)),
             dma((count,)),
             dma((count,)),
-            dma((2,)),
-            dma((2,)),
             dma((half,)),
             dma((grp_count,)),
-            dma((2,)),
+            dma((1,)),
         ],
         compiler_params=pltpu.CompilerParams(
             collective_id=1, has_side_effects=True, vmem_limit_bytes=56 * MIB
         ),
         cost_estimate=KERNEL_COST,
         name="attend_forward",
-    )(
-        hidden, cot_own, first_gain[None, :], gain[None, :], w, b, segments[:, None],
-        segments[None, :], w_out,
-    )
+    )(hidden, first_gain[None, :], gain[None, :], w, b, segments[:, None], segments[None, :], w_out)
 
 
 def attend_backward_kernel(
@@ -569,6 +542,7 @@
     gs[ring.own(), :] = g_own[...]
     pl.semaphore_wait(pltpu.get_barrier_semaphore(), count - 1 + grp_count - 1)
     plane_copies = PlaneCopies(list(zip(bulk, landed)), grp_count // 2, plane_sems)
+    ring.start()
     plane_copies.start()
     for slot in range(count):
         first = slot_index(count, slot) * size
@@ -596,10 +570,10 @@
     )
     for slot in exchange.others():
         exchange.copy(slot).start()
-    ring.start()
     g_att[(count - 2) * size : (count - 1) * size, :] = outbox[count - 2]
     dk[...] = jnp.zeros_like(dk)
     dv[...] = jnp.zeros_like(dv)
+    next_pair(0)
     for slot in exchange.others():
         exchange.arrived(slot).wait_recv()
 
@@ -624,10 +598,6 @@
             dv[h] += dot(weights.astype(BF16), g_block)
 
         @pl.when(i == 1)
-        def _():
-            next_pair(0)
-
-        @pl.when(i == 3)
         def _():
             next_pair(1)
 
@@ -1204,8 +1174,8 @@
 
 
 def experts_kernel(
-    count, expert_count, x_own, cot_own, routes, routes_w, near, gate_up_e, down_e, gate_up_s,
-    down_s, act_e_out, grad_e_out, act_s_out, grad_s_out, part_out, branch_out, logits_out, x_out,
+    count, expert_count, x_own, cot_own, routes, routes_w, gate_up_e, down_e, gate_up_s, down_s,
+    act_e_out, grad_e_out, act_s_out, grad_s_out, part_out, branch_out, logits_out, x_out,
     cot_out,
     xs, cots, gate_e, up_e, held_e, gate_s, up_s, held_s, act_e, grad_e, act_s, grad_s, part,
     branch, logits_held, x_send, x_recv, cot_send, cot_recv, weight_sems, out_sems, x_sems,
@@ -1232,41 +1202,42 @@
             ]
         )
     ]
-    load_near = pltpu.make_async_copy(near, cots.at[pl.ds(0, rows)], weight_sems.at[6])
-    load_near.start()
     for load in loads:
         load.start()
     xs[ring_x.own(), :] = x_own[...]
     cots[ring_x.own(), :] = cot_own[...]
     pl.semaphore_wait(barrier, 2)
     ring_x.start()
-    load_near.wait()
-    ring_cot.forward(0)
-
-    def stores(i):
-        here = rows_at(i, rows)
-        slot = lax.rem(i, 2)
+    ring_cot.start()
+
+    def stores(slot, length, here):
+        cut = pl.ds(0, length)
         pieces = [
-            (act_e.at[slot], act_e_out.at[here]),
-            (grad_e.at[slot, 0], grad_e_out.at[0, here]),
-            (grad_e.at[slot, 1], grad_e_out.at[1, here]),
-            (act_s.at[slot], act_s_out.at[here]),
-            (grad_s.at[slot, 0], grad_s_out.at[0, here]),
-            (grad_s.at[slot, 1], grad_s_out.at[1, here]),
-            (part.at[slot], part_out.at[here]),
-            (branch.at[slot], branch_out.at[here]),
-            (logits_held.at[slot], logits_out.at[here]),
+            (act_e.at[slot, cut], act_e_out.at[here]),
+            (grad_e.at[slot, 0, cut], grad_e_out.at[0, here]),
+            (grad_e.at[slot, 1, cut], grad_e_out.at[1, here]),
+            (act_s.at[slot, cut], act_s_out.at[here]),
+            (grad_s.at[slot, 0, cut], grad_s_out.at[0, here]),
+            (grad_s.at[slot, 1, cut], grad_s_out.at[1, here]),
+            (part.at[slot, cut], part_out.at[here]),
+            (branch.at[slot, cut], branch_out.at[here]),
+            (logits_held.at[slot, cut], logits_out.at[here]),
         ]
         return [
             pltpu.make_async_copy(source, target, out_sems.at[slot, k])
             for k, (source, target) in enumerate(pieces)
         ]
 
-    def store_rows(i):
-        here = rows_at(i, rows)
+    def pair_stores(i):
+        return stores(lax.rem(i, 2), rows, rows_at(i, rows))
+
+    own_rows = pl.ds((count - 2) * size, size)
+    far_rows = pl.ds((count - 1) * size, size)
+
+    def store_rows(here, number):
         return [
-            pltpu.make_async_copy(xs.at[here], x_out.at[here], x_sems.at[0, i]),
-            pltpu.make_async_copy(cots.at[here], cot_out.at[here], x_sems.at[1, i]),
+            pltpu.make_async_copy(xs.at[here], x_out.at[here], x_sems.at[0, number]),
+            pltpu.make_async_copy(cots.at[here], cot_out.at[here], x_sems.at[1, number]),
         ]
 
     sections = (
@@ -1276,38 +1247,15 @@
     mine = lax.axis_index("ep")
     onehot = (lax.broadcasted_iota(jnp.int32, (1, LANES), 1) == mine).astype(F32)
 
-    def one_pair(i, carry):
-        slot = lax.rem(i, 2)
-        here = rows_at(i, rows)
-        ring_x.arrive(i)
-        ring_x.forward(i)
-
-        @pl.when(i > 0)
-        def _():
-            ring_cot.arrive(i)
-            ring_cot.forward(i)
-
-        for copy in store_rows(i):
-            copy.start()
-
-        @pl.when(i == 0)
-        def _():
-            for load in loads:
-                load.wait()
-
-        @pl.when(i >= 2)
-        def _():
-            for copy in stores(i - 2):
-                copy.wait()
-
-        lane = lax.broadcasted_iota(jnp.int32, (rows, LANES), 1)
+    def compute(here, length, slot, blocks):
+        lane = lax.broadcasted_iota(jnp.int32, (length, LANES), 1)
         inputs, cotangent = xs[here, :], cots[here, :]
         logits = dot(inputs, routes_w[...])
         routed = jnp.where(lane < expert_count, logits, NEGATIVE)
         expo = jnp.exp(routed - jnp.max(routed, -1, keepdims=True))
         probs = expo * (1.0 / jnp.sum(expo, -1, keepdims=True))
         named = jnp.concatenate(
-            [routes[rows_at(slot_index(count, 2 * i + k), size), :] for k in range(2)], 0
+            [routes[rows_at(slot_index(count, block), size), :] for block in blocks], 0
         )
         hits = jnp.sum(jnp.where(named == mine, 1.0, 0.0), -1, keepdims=True)
         own_prob = jnp.sum(probs * onehot, -1, keepdims=True) * hits
@@ -1318,7 +1266,7 @@
         total, out_total = None, None
         for s, (gate_w, up_w, down_w, act_out, grad_out, ahead, back_dot) in enumerate(sections):
             factor = own_prob if s == 0 else share
-            dots = jnp.zeros((rows, 1), F32)
+            dots = jnp.zeros((length, 1), F32)
             for start, width in tiles_of(down_w.shape[0]):
                 cut = pl.ds(start, width)
                 piece = (slice(None), cut) if s == 0 else (cut, slice(None))
@@ -1330,46 +1278,83 @@
                 act = (silu * up).astype(BF16).astype(F32)
                 dots = dots + jnp.sum(grad * act, -1, keepdims=True)
                 scaled = grad * factor
-                act_out[slot, :, cut] = (act * factor).astype(BF16)
-                grad_out[slot, 0, :, cut] = (
+                act_out[slot, :length, cut] = (act * factor).astype(BF16)
+                grad_out[slot, 0, :length, cut] = (
                     scaled * up * (sigma + silu * (1.0 - sigma))
                 ).astype(BF16)
-                grad_out[slot, 1, :, cut] = (scaled * silu).astype(BF16)
+                grad_out[slot, 1, :length, cut] = (scaled * silu).astype(BF16)
             inner.append(dots)
-            back = back_dot(grad_out[slot, 0], gate_w[...]) + back_dot(
-                grad_out[slot, 1], up_w[...]
+            back = back_dot(grad_out[slot, 0, :length], gate_w[...]) + back_dot(
+                grad_out[slot, 1, :length], up_w[...]
             )
             total = back if total is None else total + back
-            out_piece = dot(act_out[slot], down_w[...])
+            out_piece = dot(act_out[slot, :length], down_w[...])
             out_total = out_piece if out_total is None else out_total + out_piece
-        branch[slot] = out_total.astype(BF16)
+        branch[slot, :length] = out_total.astype(BF16)
         grad_logits = own_prob * inner[0] * (onehot - probs)
         grad_share = share * (1.0 - share) * inner[1]
         grad_logits = grad_logits + jnp.where(lane == expert_count, grad_share, 0.0)
         high = grad_logits.astype(BF16)
         low = (grad_logits - high.astype(F32)).astype(BF16)
         total = total + dot_nt(high, routes_w[...]) + dot_nt(low, routes_w[...])
-        logits_held[slot, :, :LANES] = high
-        logits_held[slot, :, LANES:] = low
-        part[slot] = total.astype(BF16)
-        for copy in stores(i):
+        logits_held[slot, :length, :LANES] = high
+        logits_held[slot, :length, LANES:] = low
+        part[slot, :length] = total.astype(BF16)
+        for copy in stores(slot, length, here):
             copy.start()
+
+    def one_pair(i, carry):
+        here = rows_at(i, rows)
+        ring_x.arrive(i)
+        ring_x.forward(i)
+        ring_cot.arrive(i)
+        ring_cot.forward(i)
+        for copy in store_rows(here, i):
+            copy.start()
+
+        @pl.when(i == 1)
+        def _():
+            for copy in stores(1, size, own_rows):
+                copy.wait()
+
+        @pl.when(i >= 2)
+        def _():
+            for copy in pair_stores(i - 2):
+                copy.wait()
+
+        compute(here, rows, lax.rem(i, 2), [2 * i, 2 * i + 1])
         return carry
 
-    lax.fori_loop(0, half, one_pair, 0)
-    for i in range(half):
-        for copy in store_rows(i):
+    for copy in store_rows(own_rows, half - 1):
+        copy.start()
+    for load in loads:
+        load.wait()
+    compute(own_rows, size, 1, [count - 2])
+    lax.fori_loop(0, half - 1, one_pair, 0)
+    ring_x.arrive(half - 1)
+    ring_cot.arrive(half - 1)
+    for copy in store_rows(far_rows, half):
+        copy.start()
+    last = (half - 1) % 2
+    for copy in stores(last, rows, rows_at(half - 3, rows)):
+        copy.wait()
+    compute(far_rows, size, last, [count - 1])
+    for i in range(half - 1):
+        for copy in store_rows(rows_at(i, rows), i):
             copy.wait()
-    for i in range(max(half - 2, 0), half):
-        for copy in stores(i):
+    for number, here in ((half - 1, own_rows), (half, far_rows)):
+        for copy in store_rows(here, number):
             copy.wait()
+    for copy in stores(1 - last, rows, rows_at(half - 2, rows)):
+        copy.wait()
+    for copy in stores(last, size, far_rows):
+        copy.wait()
     ring_x.finish()
-    ring_cot.finish(1)
+    ring_cot.finish()
 
 
 def experts(
-    count, expert_count, x_own, cot_own, routes, routes_w, near, gate_up_e, down_e, gate_up_s,
-    down_s,
+    count, expert_count, x_own, cot_own, routes, routes_w, gate_up_e, down_e, gate_up_s, down_s
 ):
     size, width = x_own.shape
     tokens, rows, half = size * count, 2 * size, count // 2
@@ -1380,7 +1365,7 @@
     dma = pltpu.SemaphoreType.DMA
     return pl.pallas_call(
         functools.partial(experts_kernel, count, expert_count),
-        in_specs=[whole] * 4 + [anywhere] * 5,
+        in_specs=[whole] * 4 + [anywhere] * 4,
         out_specs=[anywhere] * 9,
         out_shape=(
             shape((tokens, wide), BF16),
@@ -1413,16 +1398,16 @@
             dma((half, 2)),
             dma((half, 2)),
             dma((half, 2)),
-            dma((7,)),
+            dma((6,)),
             dma((2, 9)),
-            dma((2, half)),
+            dma((2, half + 1)),
         ],
         compiler_params=pltpu.CompilerParams(
             collective_id=0, has_side_effects=True, vmem_limit_bytes=60 * MIB
         ),
         cost_estimate=KERNEL_COST,
         name="experts",
-    )(x_own, cot_own, routes, routes_w, near, gate_up_e, down_e, gate_up_s, down_s)
+    )(x_own, cot_own, routes, routes_w, gate_up_e, down_e, gate_up_s, down_s)
 
 
 def norm_of(values):
@@ -1456,9 +1441,9 @@
 
     (
         queries, key_rows, values, attended, logs, residual, normed_two, cosine, sine, starts,
-        group_one, w_all, near_cot,
+        group_one, w_all,
     ) = attend_forward(
-        ep_count, grp_count, hidden_in, cotangent, norm1_gain, norm2_gain, w_flat, b_flat, w_out_flat,
+        ep_count, grp_count, hidden_in, norm1_gain, norm2_gain, w_flat, b_flat, w_out_flat,
         segments, scale,
     )
 
@@ -1466,7 +1451,7 @@
         expert_act, expert_grad, shared_act, shared_grad, part, out_parts, grad_logits,
         group_two, group_cot,
     ) = experts(
-        ep_count, expert_count, normed_two, cotangent, routes, routes_w, near_cot,
+        ep_count, expert_count, normed_two, cotangent, routes, routes_w,
         expert_gate_up, expert_down, jnp.swapaxes(shared_gate_up, 1, 2), shared_down,
     )
 

time: 454 us -> 446 us (0.982)
  Pallas kernels: 418 us -> 411 us
    pallas_call x1, Pallas kernels: 97.9 us -> 88.2 us  [attend_forward(): pl.pallas_call(functools.partial(attend_forward_kernel, count, grp_count,...]
    pallas_call x1, Pallas kernels: 97.9 us -> 104 us  [experts(): pl.pallas_call(functools.partial(experts_kernel, count, expert_count), in...]
where the time goes in v6:
time: 446 us; the launch traced here: 442 us
  Pallas kernels  411 us (92%)
  other arithmetic  16.8 us (4%)
  local copies, waits for them, and re-layouts  12.5 us (3%)
    pallas_call x1, Pallas kernels, experts(): pl.pallas_call(functools.partial(experts_kernel, count, expert_count), in...  104 us
    pallas_call x1, Pallas kernels, finish(): pl.pallas_call(functools.partial(finish_kernel, count, grp_count, len(bul...  98.2 us
    pallas_call x1, Pallas kernels, attend_forward(): pl.pallas_call(functools.partial(attend_forward_kernel, count, grp_count,...  88.2 us
    pallas_call x1, Pallas kernels, attend_backward(): pl.pallas_call(functools.partial(attend_backward_kernel, count, grp_count...  66.5 us
    pallas_call x1, Pallas kernels, reduce_and_weights(): pl.pallas_call(functools.partial(reduce_and_weights_kernel, count, grp_co...  54.4 us

profile of v6, /device:TPU:0, one launch (start us, length us, event | category | flops | bytes accessed | tf_op | source)
XLA Modules:
  0.0 441.8 jit_solution(13444874263078658728)
XLA Ops:
  0.6 0.0 copy-start.20
  0.7 0.0 copy-start.23
  0.7 4.2 copy.34
  4.9 0.0 copy-done.20
  4.9 0.0 copy-start.22
  4.9 1.0 copy.30.segments
  5.9 0.0 copy-done.23
  5.9 0.6 copy.35
  6.5 88.2 %attend_forward.1 = (bf16[2,1024,128]{2,1,0:T(8,128)(2,1)}, bf16[2,1024,128]{2,1,0:T(8,128)(2,1)}, bf16[2,1024,128]{2,1,0:T(8,128)(2,1)}, bf16[1024,256]{1,0:T(8...) custom-call(bf16[128,2048]{1,0:T(8,128)(2,1)} %hidden.1, ...), custom_call_target="tpu_custom_call" | custom-call | flops 1000000 | bytes 100000 | tf_op jit(solution)/shard_map/attend_forward/pallas_call | solution.py:461
  94.7 0.0 copy-done.22
  94.7 0.3 broadcast_in_dim.37
  95.0 0.0 copy-done.19
  95.0 0.3 copy.31
  95.3 0.1 pad.4.clone
  95.4 1.1 maximum_maximum_fusion.routes_w
  96.5 0.0 copy-done.21
  96.5 1.0 copy.33.routes
  97.5 104.0 %experts.1 = (bf16[1024,1408]{1,0:T(8,128)(2,1)}, bf16[2,1024,1408]{2,1,0:T(8,128)(2,1)}, bf16[1024,704]{1,0:T(8,128)(2,1)}, bf16[2,1024,704]{2,1,0:T(8,128)(2,1...) custom-call(bf16[128,2048]{1,0:T(8,128)(2,1)} %get-tuple-element.64., ...), custom_call_target="tpu_custom_call" | custom-call | flops 1000000 | bytes 100000 | tf_op jit(solution)/shard_map/experts/pallas_call | solution.py:1366
  201.6 54.4 %reduce_and_weights.1 = (f32[128,2048]{1,0:T(8,128)}, bf16[128,2048]{1,0:T(8,128)(2,1)}, f32[11,2048]{1,0:T(8,128)}, bf16[512,1408]{1,0:T(8,128)(2,1)}, bf16[512...) custom-call(bf16[1024,2048]{1,0:T(8,128)(2,1)} %get-tuple-element.65, ...), custom_call_target="tpu_custom_call" | custom-call | flops 1000000 | bytes 100000 | tf_op jit(solution)/shard_map/reduce_and_weights/pallas_call | solution.py:1134
  256.0 66.5 %attend_backward.1 = (bf16[1024,768]{1,0:T(8,128)(2,1)}, f32[1,768]{1,0:T(1,128)}, bf16[1024,2048]{1,0:T(8,128)(2,1)}, bf16[1024,2048]{1,0:T(8,128)(2,1)}, bf16[...) custom-call(bf16[128,2048]{1,0:T(8,128)(2,1)} %get-tuple-element.73.g_own, bf16[4,2048,512]{2,1,0:T(8,128)(2,1)} %get-tuple-element.74.w_all, ...), custom_call_target="tpu_custom_call" | custom-call | flops 1000000 | bytes 100000 | tf_op jit(solution)/shard_map/attend_backward/pallas_call | solution.py:643
  322.5 0.0 copy-start.8
  322.5 98.2 %finish.1 = (f32[128,2048]{1,0:T(8,128)}, f32[128,2048]{1,0:T(8,128)}, f32[11,2048]{1,0:T(8,128)}, f32[1,768]{1,0:T(1,128)}, f32[512,768]{1,0:T(8,128)}, /*index...) custom-call(bf16[1024,2048]{1,0:T(8,128)(2,1)} %get-tuple-element.84, ...), custom_call_target="tpu_custom_call" | custom-call | flops 1000000 | bytes 100000 | tf_op jit(solution)/shard_map/finish/pallas_call | solution.py:963
  420.8 0.0 copy-done.8
  420.8 0.0 copy-start.5
  420.8 0.0 copy-start.6
  420.8 0.0 copy-start.7
  420.8 0.0 copy-start.9
  420.8 3.5 add_bitcast_fusion
  424.4 0.0 copy-done.5
  424.4 0.0 copy-done.6
  424.4 0.0 copy-done.7
  424.4 0.0 copy-done.9
  424.4 0.6 add_bitcast_fusion.1
  424.9 0.0 copy-start.13
  425.0 0.0 copy-start.14
  425.0 2.9 maximum_bitcast_fusion
  427.9 0.0 copy-done.13
  427.9 0.0 copy-done.14
  427.9 1.3 convert_add_fusion.1
  429.2 0.5 copy-done.4
  429.7 0.5 copy-done.10
  430.2 2.0 add_bitcast_fusion.3
  432.2 0.0 copy-done.15
  432.2 0.0 copy-done.16
  432.2 0.9 convert_add_fusion.2
  433.1 0.0 copy-done.3
  433.1 0.0 copy-done.12
  433.1 0.0 copy-start.17
  433.1 0.1 convert_add_fusion
  433.3 2.0 reshape.60
  435.3 0.0 copy-done
  435.3 0.2 fusion.6
  435.5 0.0 copy-done.1
  435.5 0.0 copy-done.17
  435.5 2.8 fusion.2
  438.2 0.0 copy-done.2
  438.3 0.0 copy-done.11
  438.3 1.4 fusion.5
  439.6 0.0 copy-done.18
  439.6 0.6 slice_bitcast_fusion
  440.3 0.6 fusion.7
  440.9 0.0 copy-done.24
  440.9 0.1 reshape.61
  441.0 0.6 constant_dynamic-slice_fusion
  (18 shorter events, 0.1 us)
Async XLA Ops:
  0.6 4.2 copy-start.20
  0.7 5.2 %copy-start.23 = (f32[2,384]{1,0:T(2,128)S(1)}, f32[2,384]{1,0:T(2,128)}, u32[]{:S(2)}) copy-start(f32[2,384]{1,0:T(2,128)} %param.21) | copy-start | bytes 9220
  4.9 89.8 %copy-start.22 = (bf16[2048]{0:T(1024)(128)(2,1)S(1)}, bf16[2048]{0:T(1024)(128)(2,1)}, u32[]{:S(2)}) copy-start(bf16[2048]{0:T(1024)(128)(2,1)} %param.27) | copy-start | bytes 12292
  6.5 88.5 %copy-start.19 = (bf16[2048,8]{0,1:T(8,128)(2,1)S(1)}, bf16[2048,8]{0,1:T(8,128)(2,1)}, u32[]{:S(2)}) copy-start(bf16[2048,8]{0,1:T(8,128)(2,1)} %param.24) | copy-start | bytes 98308
  6.5 90.0 %copy-start.21 = (s32[1024,4]{0,1:T(4,128)S(1)}, s32[1024,4]{0,1:T(4,128)}, u32[]{:S(2)}) copy-start(s32[1024,4]{0,1:T(4,128)} %param.17) | copy-start | bytes 49156
  322.5 98.2 %copy-start.8 = (bf16[1408,512]{1,0:T(8,128)(2,1)S(1)}, bf16[1408,512]{1,0:T(8,128)(2,1)}, u32[]{:S(2)}) copy-start(bf16[1408,512]{1,0:T(8,128)(2,1)} %get-tuple-element.111) | copy-start | bytes 4325380
  420.8 3.6 copy-start.5
  420.8 3.6 copy-start.6
  420.8 3.6 copy-start.7
  420.8 3.6 copy-start.9
  424.9 2.9 copy-start.13
  425.0 2.9 copy-start.14
  427.9 1.8 copy-start.4
  427.9 2.3 copy-start.10
  430.2 2.0 copy-start.15
  430.2 2.1 copy-start.16
  430.2 2.9 copy-start.3
  430.2 2.9 copy-start.12
  433.1 2.2 copy-start
  433.1 2.3 copy-start.1
  433.1 2.3 copy-start.17
  435.3 3.0 copy-start.2
  435.3 3.0 copy-start.11
  438.2 1.4 copy-start.18
  438.2 2.7 copy-start.24

commit v7 on v6

--- a/solution.py
+++ b/solution.py
@@ -505,16 +505,16 @@
 
 
 def attend_backward_kernel(
-    count, grp_count, heads, scale, g_own, w_all, w, cosine, sine, q, k, v, row_logs, row_starts,
-    *refs,
+    count, grp_count, heads, scale, g_own, cosine, sine, q, k, v, row_logs, row_starts, w_all_in,
+    w_in, *refs,
 ):
-    number = (len(refs) - 17) // 2
+    number = (len(refs) - 20) // 2
     bulk, refs = refs[:number], refs[number:]
     g_out, bias_out, branch_out, group_out = refs[:4]
     landed = refs[4 : 4 + number]
     (
         row_positions, positions, g_att, dk, dv, outbox, gs, send_sems, recv_sems, ring_send,
-        ring_recv, store_sems, plane_sems,
+        ring_recv, store_sems, plane_sems, w_all, w, w_sems,
     ) = refs[4 + number :]
     size, width = g_own.shape
     tokens = size * count
@@ -527,6 +527,11 @@
     part_width = width // grp_count
 
     ring = KernelRing(gs, count, size, ring_send, ring_recv)
+
+    load_all = pltpu.make_async_copy(w_all_in, w_all, w_sems.at[0])
+    load_w = pltpu.make_async_copy(w_in, w, w_sems.at[1])
+    load_all.start()
+    load_w.start()
 
     def store(i):
         here = rows_at(i, 2 * size)
@@ -552,6 +557,7 @@
         positions[slot * size : (slot + 1) * size, :] = first + lax.broadcasted_iota(
             jnp.int32, (size, 1), 0
         )
+    load_all.wait()
     own_rows = None
     for j in range(grp_count):
         member = 2 * ((plane + j % planes) % planes) + (core if j < planes else 1 - core)
@@ -604,6 +610,7 @@
         return carry
 
     lax.fori_loop(0, tokens // rows, scores_back, 0)
+    load_w.wait()
     bias_out[...] = jnp.zeros_like(bias_out)
 
     def finish(i, carry):
@@ -642,7 +649,7 @@
     dma = pltpu.SemaphoreType.DMA
     return pl.pallas_call(
         functools.partial(attend_backward_kernel, count, grp_count, heads, scale),
-        in_specs=[whole] * 10 + [anywhere] * len(bulk),
+        in_specs=[whole] * 8 + [anywhere] * (2 + len(bulk)),
         out_specs=[whole] * 3 + [anywhere] * (1 + len(bulk)),
         out_shape=(
             shape((tokens, 3 * LANES * heads), BF16),
@@ -665,6 +672,9 @@
             dma((count // 2, 2)),
             dma((count // 2,)),
             dma((2, max(len(bulk), 1))),
+            pltpu.VMEM(w_all.shape, BF16),
+            pltpu.VMEM(w.shape, BF16),
+            dma((2,)),
         ],
         compiler_params=pltpu.CompilerParams(
             collective_id=2, has_side_effects=True, vmem_limit_bytes=56 * MIB
@@ -672,8 +682,7 @@
         cost_estimate=KERNEL_COST,
         name="attend_backward",
     )(
-        g_own, w_all, w, cosine, sine, q, k, v,
-        logs, starts, *bulk,
+        g_own, cosine, sine, q, k, v, logs, starts, w_all, w, *bulk,
     )
 
 
@@ -725,8 +734,9 @@
 
 
 class RingSum:
-    def __init__(self, count, part, out, to_right, to_left, send_sems, recv_sems):
+    def __init__(self, count, part, out, to_right, to_left, send_sems, recv_sems, near=None):
         place, index_at = ring_places(count)
+        self.near = near
         self.count, self.half, self.size = count, count // 2, out.shape[0]
         self.part, self.out, self.held = part, out, (to_right, to_left)
         self.send_sems, self.recv_sems = send_sems, recv_sems
@@ -751,20 +761,25 @@
         )
 
     def start(self):
-        for way in range(2):
-            self.copy(0, way).start()
+        if self.near is None:
+            for way in range(2):
+                self.copy(0, way).start()
+        else:
+            self.advance(1)
 
     def advance(self, step):
         middle, part = self.size // 2, self.part
         for way in range(2):
             held = self.held[way]
             first = (2 * (self.half - step) - 1 - way) * self.size
-            self.copy(step - 1, way).wait_recv()
+            if step > 1 or self.near is None:
+                self.copy(step - 1, way).wait_recv()
             if step == 1:
                 here = slice(way * middle, (way + 1) * middle)
                 rest = slice((1 - way) * middle, (2 - way) * middle)
                 own = part[first + way * middle : first + (way + 1) * middle, :]
-                held[0, here] = (own.astype(F32) + held[0, here].astype(F32)).astype(BF16)
+                before = held[0, here] if self.near is None else self.near[here, :]
+                held[0, here] = (own.astype(F32) + before.astype(F32)).astype(BF16)
                 held[0, rest] = part[first + (1 - way) * middle : first + (2 - way) * middle, :]
             else:
                 own = part[first : first + self.size, :]
@@ -780,7 +795,7 @@
         self.out[...] = total
 
     def finish(self):
-        for step in range(self.half):
+        for step in range(0 if self.near is None else 1, self.half):
             for way in range(2):
                 self.copy(step, way).wait_send()
 
@@ -816,8 +831,7 @@
 
 
 def finish_kernel(
-    count, grp_count, bulk_number, branch, out_parts, small, bias, gain, g_qkv, attended, w,
-    x_in, attn_in, *refs
+    count, grp_count, bulk_number, has_near, branch, small, bias, gain, g_qkv, attended, *refs
 ):
     refs = list(refs)
 
@@ -828,10 +842,13 @@
 
     planes = grp_count // 2
     far_number = planes - 1
+    near = take(1)[0] if has_near else None
+    out_in, w_in, x_in, attn_in = take(4)
     bulk = take(bulk_number)
     branch_sum, out_sum, small_sum, bias_sum, own_q, own_o = take(6)
     landed = take(bulk_number + 2 * far_number)
     rings_held = take(4)
+    out_parts, w = take(2)
     x, attn = take(2)
     away, arrived, far = take(2), take(2), take(2)
     small_held, small_arrived, bias_held, bias_arrived = take(4)
@@ -858,9 +875,13 @@
             for i, (source, target) in enumerate(((x_in, x), (attn_in, attn)))
         ]
 
+    load_out = pltpu.make_async_copy(out_in, out_parts, load_sems.at[2, 0])
+    load_w = pltpu.make_async_copy(w_in, w, load_sems.at[2, 1])
+    load_out.start()
     for unit in range(2):
         for load in loads(unit):
             load.start()
+    load_w.start()
     greet("ep", count)
     greet("grp", grp_count)
     small_held[0] = small[...]
@@ -869,12 +890,15 @@
     rings = [
         RingSum(
             count, part, out, rings_held[2 * a], rings_held[2 * a + 1], send_sems.at[a],
-            recv_sems.at[a],
-        )
-        for a, (part, out) in enumerate(((branch, branch_sum), (out_parts, out_sum)))
+            recv_sems.at[a], first,
+        )
+        for a, (part, out, first) in enumerate(
+            ((branch, branch_sum, None), (out_parts, out_sum, near))
+        )
     ]
-    for ring in rings:
-        ring.start()
+    rings[0].start()
+    load_out.wait()
+    rings[1].start()
     sums = [
         Doubling(small_held, small_arrived, doubling_stages(("grp", "ep")), small_sems),
         Doubling(bias_held, bias_arrived, doubling_stages(("grp",)), bias_sems),
@@ -903,6 +927,7 @@
             device_id_type=MESH,
         )
 
+    load_w.wait()
     for unit, (side, place) in enumerate(units):
         cut, slot = columns(unit), unit % 2
         for load in loads(unit):
@@ -930,7 +955,8 @@
     far_copies.start(halves)
     for step in range(1, count // 2):
         for a, ring in enumerate(rings):
-            ring.advance(step)
+            if step > 1 or ring.near is None:
+                ring.advance(step)
             if a or step == 1:
                 for item in sums:
                     item.advance()
@@ -947,7 +973,8 @@
 
 
 def finish(
-    count, grp_count, branch, out_parts, small, bias, gain, g_qkv, attended, w, x, attn, bulk
+    count, grp_count, branch, out_parts, small, bias, gain, g_qkv, attended, w, x, attn, bulk,
+    near,
 ):
     tokens, width = branch.shape
     size, half, planes = tokens // count, count // 2, grp_count // 2
@@ -958,11 +985,12 @@
     whole = pl.BlockSpec(memory_space=pltpu.VMEM)
     shape = jax.ShapeDtypeStruct
     dma = pltpu.SemaphoreType.DMA
+    first = [] if near is None else [near]
     landed = [shape(dims, BF16) for dims in (q_shape, o_shape) for _ in range(planes - 1)]
     landed += [shape(value.shape, value.dtype) for value in bulk]
     results = pl.pallas_call(
-        functools.partial(finish_kernel, count, grp_count, len(bulk)),
-        in_specs=[whole] * 8 + [anywhere] * (2 + len(bulk)),
+        functools.partial(finish_kernel, count, grp_count, len(bulk), bool(first)),
+        in_specs=[whole] * (6 + len(first)) + [anywhere] * (4 + len(bulk)),
         out_specs=[whole] * 6 + [anywhere] * len(landed),
         out_shape=[
             shape((size, width), F32),
@@ -974,6 +1002,7 @@
             *landed,
         ],
         scratch_shapes=[pltpu.VMEM((half, size, width), BF16)] * 4
+        + [pltpu.VMEM((tokens, width), BF16), pltpu.VMEM(w.shape, BF16)]
         + [pltpu.VMEM((2, tokens, part_width), BF16)] * 2
         + [pltpu.VMEM((planes, *dims), BF16) for dims in (q_shape, o_shape)] * 2
         + [pltpu.VMEM((max(planes - 1, 1), *dims), BF16) for dims in (q_shape, o_shape)]
@@ -984,20 +1013,20 @@
             pltpu.VMEM((stages[1], *bias.shape), F32),
         ]
         + [dma((2, half, 2))] * 2
-        + [dma((2, stages[0])), dma((2, stages[1])), dma((2, len(landed) + len(bulk) // 2)), dma((2, 2))]
+        + [dma((2, stages[0])), dma((2, stages[1])), dma((2, len(landed) + len(bulk) // 2)), dma((3, 2))]
         + [dma((2, planes))] * 2,
         compiler_params=pltpu.CompilerParams(
             collective_id=4, has_side_effects=True, vmem_limit_bytes=60 * MIB
         ),
         cost_estimate=KERNEL_COST,
         name="finish",
-    )(branch, out_parts, small, bias, gain, g_qkv, attended, w, x, attn, *bulk)
+    )(branch, small, bias, gain, g_qkv, attended, *first, out_parts, w, x, attn, *bulk)
     return results[:6], results[6:]
 
 
 def reduce_and_weights_kernel(
     count, grp_count, expert_count, part, residual, cot_own, gain, grad_logits, x_in, cot_in,
-    grad_e_in, act_e_in, grad_s_in, act_s_in, *refs
+    grad_e_in, act_e_in, grad_s_in, act_s_in, out_parts, *refs
 ):
     refs = list(refs)
 
@@ -1007,16 +1036,18 @@
         return taken
 
     planes = grp_count // 2
-    grad_residual, own_attn, small = take(3)
+    grad_residual, own_attn, small, out_near = take(4)
     outs = [take(planes) for _ in range(5)]
     landed = take(planes - 1)
     sources = (x_in, grad_e_in, cot_in, act_e_in, grad_s_in, act_s_in)
     held = take(6)
-    (summed,) = take(1)
+    summed, out_far, landing = take(3)
     x, grad_e, cot, act_e, grad_s, act_s = held
     to_right, to_left = take(2)
     staged, arrived = take(5), take(5)
-    send_sems, recv_sems, load_sems, core_send, core_recv, out_sems, plane_sems = take(7)
+    (
+        send_sems, recv_sems, load_sems, core_send, core_recv, out_sems, plane_sems, near_sems
+    ) = take(8)
     mine = lax.axis_index("grp")
     core, plane = mine % 2, mine // 2
     part_width = x.shape[1] // grp_count
@@ -1027,11 +1058,27 @@
     ]
     for load in loads:
         load.start()
+    size = out_far.shape[0]
+    load_far = pltpu.make_async_copy(
+        out_parts.at[pl.ds((count - 1) * size, size)], out_far, load_sems.at[6]
+    )
+    load_far.start()
     greet("ep", count)
     greet("grp", grp_count)
     pl.semaphore_wait(pltpu.get_barrier_semaphore(), count - 1 + grp_count - 1)
     ring = RingSum(count, part, summed, to_right, to_left, send_sems, recv_sems)
     ring.start()
+
+    def near_copy(way):
+        half_rows = pl.ds(way * (size // 2), size // 2)
+        return pltpu.make_async_remote_copy(
+            src_ref=out_far.at[half_rows],
+            dst_ref=landing.at[half_rows],
+            send_sem=near_sems.at[0, way],
+            recv_sem=near_sems.at[1, way],
+            device_id={"ep": ring.neighbours[way]},
+            device_id_type=MESH,
+        )
 
     def columns(order, side):
         member = 2 * ((plane + order) % planes) + (core if side == 0 else 1 - core)
@@ -1093,14 +1140,15 @@
                 if number % 5 == 2:
                     if ring_step < count // 2:
                         ring.advance(ring_step)
+                    if ring_step == count // 2 - 1:
+                        load_far.wait()
+                        near_copy(0).start()
+                        near_copy(1).start()
                     ring_step += 1
                 if number == 5:
                     rows = dot_tn(grad_logits[:, :LANES], x[...])
                     rows = rows + dot_tn(grad_logits[:, LANES:], x[...])
                     small[: expert_count + 1, :] = rows[: expert_count + 1, :]
-    while ring_step < count // 2:
-        ring.advance(ring_step)
-        ring_step += 1
     ring.last()
     normal, factor = norm_of(residual[...])
     total = summed[...]
@@ -1109,6 +1157,9 @@
     own_attn[...] = own.astype(BF16)
     small[expert_count + 1 : expert_count + 2, :] = jnp.sum(total * normal, 0, keepdims=True)
     small[expert_count + 2 :, :] = jnp.zeros((1, small.shape[1]), F32)
+    for way in range(2):
+        near_copy(way).wait()
+    out_near[...] = landing[...]
     for kind in range(5):
         store(kind, planes - 1).wait()
     ring.finish()
@@ -1117,7 +1168,7 @@
 
 def reduce_and_weights(
     count, grp_count, expert_count, part, residual, cot_own, gain, grad_logits, x, cot, grad_e,
-    act_e, grad_s, act_s,
+    act_e, grad_s, act_s, out_parts,
 ):
     tokens, width = part.shape
     size, half, planes = tokens // count, count // 2, grp_count // 2
@@ -1133,12 +1184,13 @@
     dma = pltpu.SemaphoreType.DMA
     rows = pl.pallas_call(
         functools.partial(reduce_and_weights_kernel, count, grp_count, expert_count),
-        in_specs=[whole] * 5 + [anywhere] * 6,
-        out_specs=[whole] * 3 + [anywhere] * (6 * planes - 1),
+        in_specs=[whole] * 5 + [anywhere] * 7,
+        out_specs=[whole] * 4 + [anywhere] * (6 * planes - 1),
         out_shape=[
             shape((size, width), F32),
             shape((size, width), BF16),
             shape((expert_count + 3, width), F32),
+            shape((size, width), BF16),
         ]
         + [shape(dims, BF16) for dims in shapes for _ in range(planes)]
         + [shape(shapes[0], BF16)] * (planes - 1),
@@ -1146,19 +1198,20 @@
             pltpu.VMEM(value.shape, BF16) for value in (x, grad_e, cot, act_e, grad_s, act_s)
         ]
         + [pltpu.VMEM((size, width), F32)]
+        + [pltpu.VMEM((size, width), BF16)] * 2
         + [pltpu.VMEM((half, size, width), BF16)] * 2
         + [pltpu.VMEM(dims, BF16) for dims in shapes]
         + [pltpu.VMEM((planes, *dims), BF16) for dims in shapes]
-        + [dma((half, 2)), dma((half, 2)), dma((6,))]
+        + [dma((half, 2)), dma((half, 2)), dma((7,))]
         + [dma((5, planes))] * 3
-        + [dma((2, max(planes - 1, 1)))],
+        + [dma((2, max(planes - 1, 1))), dma((2, 2))],
         compiler_params=pltpu.CompilerParams(
-            collective_id=3, has_side_effects=True, vmem_limit_bytes=60 * MIB
+            collective_id=3, has_side_effects=True, vmem_limit_bytes=62 * MIB
         ),
         cost_estimate=KERNEL_COST,
         name="reduce_and_weights",
-    )(part, residual, cot_own, gain, grad_logits, x, cot, grad_e, act_e, grad_s, act_s)
-    rows, slices = rows[:3], list(rows[3:])
+    )(part, residual, cot_own, gain, grad_logits, x, cot, grad_e, act_e, grad_s, act_s, out_parts)
+    rows, slices = rows[:4], list(rows[4:])
     groups = [slices[i * planes : (i + 1) * planes] for i in range(5)]
     passed, own = [group[:-1] for group in groups], [group[-1] for group in groups]
     return (*rows, passed, own, slices[5 * planes :])
@@ -1456,9 +1509,12 @@
     )
 
     if ep_count == 8:
-        grad_residual, own_attn, small, passed, sums_own, first_landed = reduce_and_weights(
+        (
+            grad_residual, own_attn, small, out_near, passed, sums_own, first_landed
+        ) = reduce_and_weights(
             ep_count, grp_count, expert_count, part, residual, cotangent, norm2_gain[None, :],
             grad_logits, group_two, group_cot, expert_grad, expert_act, shared_grad, shared_act,
+            out_parts,
         )
     else:
 
@@ -1483,7 +1539,7 @@
         passed = [item.pass_on(values_) for item, values_ in zip(sums, arrived)]
         sums_own = [item.own() for item in sums]
         grad_normed_two = reduce_rows(ep_count, part)
-        first_landed = None
+        first_landed = out_near = None
         normal_two, factor_two = norm_of(residual)
         grad_residual = cotangent.astype(F32) + norm_back(
             grad_normed_two, normal_two, factor_two, norm2_gain
@@ -1505,7 +1561,7 @@
 
     (grad_normed_one, out_sum, small, bias_total, own_q, own_o), landed = finish(
         ep_count, grp_count, grad_branch, out_parts, small, grad_bias, norm1_gain[None, :],
-        grad_qkv, attended, w_flat, group_one, group_attn, passed[3] + passed[2],
+        grad_qkv, attended, w_flat, group_one, group_attn, passed[3] + passed[2], out_near,
     )
     from_q, from_o, from_planes[3], from_planes[2] = [
         landed[i * each : (i + 1) * each] for i in range(4)

time: 446 us -> 441 us (0.989)
  no operation moved by 1% of the time
where the time goes in v7:
time: 441 us; the launch traced here: 437 us
  Pallas kernels  407 us (92%)
  other arithmetic  16.8 us (4%)
  local copies, waits for them, and re-layouts  12.5 us (3%)
    pallas_call x1, Pallas kernels, experts(): pl.pallas_call(functools.partial(experts_kernel, count, expert_count), in...  104 us
    pallas_call x1, Pallas kernels, finish(): pl.pallas_call(functools.partial(finish_kernel, count, grp_count, len(bul...  96.4 us
    pallas_call x1, Pallas kernels, attend_forward(): pl.pallas_call(functools.partial(attend_forward_kernel, count, grp_count,...  88.2 us
    pallas_call x1, Pallas kernels, attend_backward(): pl.pallas_call(functools.partial(attend_backward_kernel, count, grp_count...  63.3 us
    pallas_call x1, Pallas kernels, reduce_and_weights(): pl.pallas_call(functools.partial(reduce_and_weights_kernel, count, grp_co...  54.6 us

profile of v7, /device:TPU:0, one launch (start us, length us, event | category | flops | bytes accessed | tf_op | source)
XLA Modules:
  0.0 436.9 jit_solution(13264020848122961757)
XLA Ops:
  0.6 0.0 copy-start.20
  0.7 0.0 copy-start.23
  0.7 4.2 copy.34
  4.9 0.0 copy-done.20
  4.9 0.0 copy-start.22
  4.9 1.0 copy.30.segments
  5.9 0.0 copy-done.23
  5.9 0.6 copy.35
  6.5 88.2 %attend_forward.1 = (bf16[2,1024,128]{2,1,0:T(8,128)(2,1)}, bf16[2,1024,128]{2,1,0:T(8,128)(2,1)}, bf16[2,1024,128]{2,1,0:T(8,128)(2,1)}, bf16[1024,256]{1,0:T(8...) custom-call(bf16[128,2048]{1,0:T(8,128)(2,1)} %hidden.1, ...), custom_call_target="tpu_custom_call" | custom-call | flops 1000000 | bytes 100000 | tf_op jit(solution)/shard_map/attend_forward/pallas_call | solution.py:461
  94.7 0.0 copy-done.22
  94.7 0.3 broadcast_in_dim.37
  95.0 0.0 copy-done.19
  95.0 0.3 copy.31
  95.3 0.1 pad.4.clone
  95.4 1.1 maximum_maximum_fusion.routes_w
  96.5 0.0 copy-done.21
  96.5 1.0 copy.33.routes
  97.6 104.0 %experts.1 = (bf16[1024,1408]{1,0:T(8,128)(2,1)}, bf16[2,1024,1408]{2,1,0:T(8,128)(2,1)}, bf16[1024,704]{1,0:T(8,128)(2,1)}, bf16[2,1024,704]{2,1,0:T(8,128)(2,1...) custom-call(bf16[128,2048]{1,0:T(8,128)(2,1)} %get-tuple-element.65., ...), custom_call_target="tpu_custom_call" | custom-call | flops 1000000 | bytes 100000 | tf_op jit(solution)/shard_map/experts/pallas_call | solution.py:1419
  201.6 54.6 %reduce_and_weights.1 = (f32[128,2048]{1,0:T(8,128)}, bf16[128,2048]{1,0:T(8,128)(2,1)}, f32[11,2048]{1,0:T(8,128)}, bf16[128,2048]{1,0:T(8,128)(2,1)}, bf16[512...) custom-call(bf16[1024,2048]{1,0:T(8,128)(2,1)} %get-tuple-element.66, ...), custom_call_target="tpu_custom_call" | custom-call | flops 1000000 | bytes 100000 | tf_op jit(solution)/shard_map/reduce_and_weights/pallas_call | solution.py:1185
  256.2 63.3 %attend_backward.1 = (bf16[1024,768]{1,0:T(8,128)(2,1)}, f32[1,768]{1,0:T(1,128)}, bf16[1024,2048]{1,0:T(8,128)(2,1)}, bf16[1024,2048]{1,0:T(8,128)(2,1)}, bf16[...) custom-call(bf16[128,2048]{1,0:T(8,128)(2,1)} %get-tuple-element.75.g_own, f32[1024,128]{1,0:T(8,128)} %get-tuple-element.76.cosine, ...), custom_call_target="tpu_custom_call" | custom-call | flops 1000000 | bytes 100000 | tf_op jit(solution)/shard_map/attend_backward/pallas_call | solution.py:650
  319.5 0.0 copy-start.8
  319.5 96.4 %finish.1 = (f32[128,2048]{1,0:T(8,128)}, f32[128,2048]{1,0:T(8,128)}, f32[11,2048]{1,0:T(8,128)}, f32[1,768]{1,0:T(1,128)}, f32[512,768]{1,0:T(8,128)}, /*index...) custom-call(bf16[1024,2048]{1,0:T(8,128)(2,1)} %get-tuple-element.86, ...), custom_call_target="tpu_custom_call" | custom-call | flops 1000000 | bytes 100000 | tf_op jit(solution)/shard_map/finish/pallas_call | solution.py:991
  415.9 0.0 copy-done.8
  415.9 0.0 copy-start.5
  415.9 0.0 copy-start.6
  415.9 0.0 copy-start.7
  416.0 0.0 copy-start.9
  416.0 3.5 add_bitcast_fusion
  419.5 0.0 copy-done.5
  419.5 0.0 copy-done.6
  419.5 0.0 copy-done.7
  419.5 0.0 copy-done.9
  419.5 0.6 add_bitcast_fusion.1
  420.1 0.0 copy-start.13
  420.1 0.0 copy-start.14
  420.1 2.9 maximum_bitcast_fusion
  423.0 0.0 copy-done.13
  423.0 0.0 copy-done.14
  423.0 1.3 convert_add_fusion.1
  424.3 0.5 copy-done.4
  424.8 0.5 copy-done.10
  425.3 2.0 add_bitcast_fusion.3
  427.4 0.0 copy-done.15
  427.4 0.0 copy-done.16
  427.4 0.9 convert_add_fusion.2
  428.2 0.0 copy-done.3
  428.3 0.0 copy-done.12
  428.3 0.0 copy-start.17
  428.3 0.1 convert_add_fusion
  428.4 2.0 reshape.60
  430.4 0.0 copy-done
  430.4 0.2 fusion.6
  430.6 0.0 copy-done.1
  430.6 0.0 copy-done.17
  430.6 2.8 fusion.2
  433.4 0.0 copy-done.2
  433.4 0.0 copy-done.11
  433.4 1.4 fusion.5
  434.8 0.0 copy-done.18
  434.8 0.6 slice_bitcast_fusion
  435.4 0.6 fusion.7
  436.0 0.0 copy-done.24
  436.1 0.1 reshape.61
  436.1 0.6 constant_dynamic-slice_fusion
  (18 shorter events, 0.1 us)
Async XLA Ops:
  0.6 4.2 copy-start.20
  0.7 5.2 %copy-start.23 = (f32[2,384]{1,0:T(2,128)S(1)}, f32[2,384]{1,0:T(2,128)}, u32[]{:S(2)}) copy-start(f32[2,384]{1,0:T(2,128)} %param.21) | copy-start | bytes 9220
  4.9 89.8 %copy-start.22 = (bf16[2048]{0:T(1024)(128)(2,1)S(1)}, bf16[2048]{0:T(1024)(128)(2,1)}, u32[]{:S(2)}) copy-start(bf16[2048]{0:T(1024)(128)(2,1)} %param.27) | copy-start | bytes 12292
  6.5 88.5 %copy-start.19 = (bf16[2048,8]{0,1:T(8,128)(2,1)S(1)}, bf16[2048,8]{0,1:T(8,128)(2,1)}, u32[]{:S(2)}) copy-start(bf16[2048,8]{0,1:T(8,128)(2,1)} %param.24) | copy-start | bytes 98308
  6.5 90.0 %copy-start.21 = (s32[1024,4]{0,1:T(4,128)S(1)}, s32[1024,4]{0,1:T(4,128)}, u32[]{:S(2)}) copy-start(s32[1024,4]{0,1:T(4,128)} %param.17) | copy-start | bytes 49156
  319.5 96.4 %copy-start.8 = (bf16[1408,512]{1,0:T(8,128)(2,1)S(1)}, bf16[1408,512]{1,0:T(8,128)(2,1)}, u32[]{:S(2)}) copy-start(bf16[1408,512]{1,0:T(8,128)(2,1)} %get-tuple-element.113) | copy-start | bytes 4325380
  415.9 3.6 copy-start.5
  415.9 3.6 copy-start.6
  415.9 3.6 copy-start.7
  416.0 3.6 copy-start.9
  420.1 2.9 copy-start.13
  420.1 2.9 copy-start.14
  423.0 1.8 copy-start.4
  423.0 2.3 copy-start.10
  425.3 2.0 copy-start.15
  425.3 2.1 copy-start.16
  425.3 2.9 copy-start.3
  425.3 2.9 copy-start.12
  428.3 2.2 copy-start
  428.3 2.3 copy-start.1
  428.3 2.3 copy-start.17
  430.4 3.0 copy-start.2
  430.4 3.0 copy-start.11
  433.4 1.4 copy-start.18
  433.4 2.7 copy-start.24

commit v8 on v7

--- a/solution.py
+++ b/solution.py
@@ -246,6 +246,10 @@
     def finish(self):
         for copy in self.copies:
             copy.wait()
+
+
+def rows_ahead(length):
+    return length * 2 // 3 // 16 * 16
 
 
 def greet(axis, count):
@@ -546,7 +550,11 @@
     greet("grp", grp_count)
     gs[ring.own(), :] = g_own[...]
     pl.semaphore_wait(pltpu.get_barrier_semaphore(), count - 1 + grp_count - 1)
-    plane_copies = PlaneCopies(list(zip(bulk, landed)), grp_count // 2, plane_sems)
+    pairs = list(zip(bulk, landed))
+    for i in range(number - (grp_count // 2 - 1), number):
+        cut = pl.ds(0, rows_ahead(bulk[i].shape[1]))
+        pairs[i] = bulk[i].at[0, cut], landed[i].at[0, cut]
+    plane_copies = PlaneCopies(pairs, grp_count // 2, plane_sems)
     ring.start()
     plane_copies.start()
     for slot in range(count):
@@ -905,14 +913,17 @@
     ]
     sums[1].start()
     halves = bulk_number // 2
-    sources = [bulk[i].at[0] for i in range(halves)]
-    targets = [landed[2 * far_number + i].at[0] for i in range(halves)]
+    sources = [bulk[i].at[1] for i in range(halves)]
+    targets = [landed[2 * far_number + i].at[1] for i in range(halves)]
     for kind in range(2):
         for place in range(far_number):
             sources.append(far[kind].at[place])
             targets.append(landed[kind * far_number + place])
-    sources += [bulk[i].at[1] for i in range(halves)] + bulk[halves:]
-    targets += [landed[2 * far_number + i].at[1] for i in range(halves)]
+    length = bulk[0].shape[1]
+    ahead = rows_ahead(length)
+    rest = pl.ds(ahead, length - ahead)
+    sources += [bulk[i].at[0, rest] for i in range(halves)] + bulk[halves:]
+    targets += [landed[2 * far_number + i].at[0, rest] for i in range(halves)]
     targets += landed[2 * far_number + halves :]
     far_copies = PlaneCopies(list(zip(sources, targets)), planes, plane_sems)
     far_copies.start(0, halves)
@@ -1551,13 +1562,14 @@
         small = jnp.concatenate([rows, grad_norm2[None], jnp.zeros((1, width), F32)], 0)
     each = grp_count // 2 - 1
 
-    bulk = passed[1] + passed[4] + (passed[0] if first_landed is None else [])
+    bulk = passed[1] + passed[4] + (passed[0] if first_landed is None else []) + passed[3]
     grad_qkv, grad_bias, grad_branch, group_attn, *landed = attend_backward(
         ep_count, grp_count, own_attn, w_all, w_flat, cosine, sine, queries, key_rows, values,
         logs, starts, scale, bulk,
     )
     from_planes = {1: landed[:each], 4: landed[each : 2 * each]}
-    from_planes[0] = landed[2 * each :] if first_landed is None else first_landed
+    from_planes[0] = landed[2 * each : 3 * each] if first_landed is None else first_landed
+    early = landed[-each:]
 
     (grad_normed_one, out_sum, small, bias_total, own_q, own_o), landed = finish(
         ep_count, grp_count, grad_branch, out_parts, small, grad_bias, norm1_gain[None, :],
@@ -1565,6 +1577,13 @@
     )
     from_q, from_o, from_planes[3], from_planes[2] = [
         landed[i * each : (i + 1) * each] for i in range(4)
+    ]
+    narrow = shared_down.shape[0]
+    went = (jnp.arange(2) == 0)[:, None, None] & (
+        jnp.arange(narrow) < rows_ahead(narrow)
+    )[None, :, None]
+    from_planes[3] = [
+        jnp.where(went, before, value) for before, value in zip(early, from_planes[3])
     ]
     layer_out = (residual + out_sum).astype(BF16)
     normal_one, factor_one = norm_of(hidden_in.astype(F32))

time: 441 us -> 435 us (0.986)
  Pallas kernels: 407 us -> 400 us
    pallas_call x1, Pallas kernels: 96.4 us -> 88.7 us  [finish(): pl.pallas_call(functools.partial(finish_kernel, count, grp_count, len(bul...]
where the time goes in v8:
time: 435 us; the launch traced here: 431 us
  Pallas kernels  400 us (92%)
  other arithmetic  17.1 us (4%)
  local copies, waits for them, and re-layouts  12.4 us (3%)
    pallas_call x1, Pallas kernels, experts(): pl.pallas_call(functools.partial(experts_kernel, count, expert_count), in...  104 us
    pallas_call x1, Pallas kernels, finish(): pl.pallas_call(functools.partial(finish_kernel, count, grp_count, len(bul...  88.7 us
    pallas_call x1, Pallas kernels, attend_forward(): pl.pallas_call(functools.partial(attend_forward_kernel, count, grp_count,...  88.2 us
    pallas_call x1, Pallas kernels, attend_backward(): pl.pallas_call(functools.partial(attend_backward_kernel, count, grp_count...  64.8 us
    pallas_call x1, Pallas kernels, reduce_and_weights(): pl.pallas_call(functools.partial(reduce_and_weights_kernel, count, grp_co...  54.7 us

profile of v8, /device:TPU:0, one launch (start us, length us, event | category | flops | bytes accessed | tf_op | source)
XLA Modules:
  0.0 430.9 jit_solution(11247014132902680991)
XLA Ops:
  0.6 0.0 copy-start.21
  0.7 0.0 copy-start.24
  0.7 4.2 copy.34
  4.9 0.0 copy-done.21
  4.9 1.0 copy.30.segments
  5.9 0.0 copy-done.24
  5.9 0.6 copy.35
  6.5 88.2 %attend_forward.1 = (bf16[2,1024,128]{2,1,0:T(8,128)(2,1)}, bf16[2,1024,128]{2,1,0:T(8,128)(2,1)}, bf16[2,1024,128]{2,1,0:T(8,128)(2,1)}, bf16[1024,256]{1,0:T(8...) custom-call(bf16[128,2048]{1,0:T(8,128)(2,1)} %hidden.1, ...), custom_call_target="tpu_custom_call" | custom-call | flops 1000000 | bytes 100000 | tf_op jit(solution)/shard_map/attend_forward/pallas_call | solution.py:465
  94.7 0.0 copy-done.23
  94.7 0.3 broadcast_in_dim.48
  95.0 0.0 copy-done.20
  95.0 0.3 copy.31
  95.3 0.1 pad.4.clone
  95.4 1.1 maximum_maximum_fusion.routes_w
  96.5 0.0 copy-done.22
  96.5 1.0 copy.33.routes
  97.5 104.0 %experts.1 = (bf16[1024,1408]{1,0:T(8,128)(2,1)}, bf16[2,1024,1408]{2,1,0:T(8,128)(2,1)}, bf16[1024,704]{1,0:T(8,128)(2,1)}, bf16[2,1024,704]{2,1,0:T(8,128)(2,1...) custom-call(bf16[128,2048]{1,0:T(8,128)(2,1)} %get-tuple-element.66., ...), custom_call_target="tpu_custom_call" | custom-call | flops 1000000 | bytes 100000 | tf_op jit(solution)/shard_map/experts/pallas_call | solution.py:1430
  201.5 54.7 %reduce_and_weights.1 = (f32[128,2048]{1,0:T(8,128)}, bf16[128,2048]{1,0:T(8,128)(2,1)}, f32[11,2048]{1,0:T(8,128)}, bf16[128,2048]{1,0:T(8,128)(2,1)}, bf16[512...) custom-call(bf16[1024,2048]{1,0:T(8,128)(2,1)} %get-tuple-element.67, ...), custom_call_target="tpu_custom_call" | custom-call | flops 1000000 | bytes 100000 | tf_op jit(solution)/shard_map/reduce_and_weights/pallas_call | solution.py:1196
  256.2 64.8 %attend_backward.1 = (bf16[1024,768]{1,0:T(8,128)(2,1)}, f32[1,768]{1,0:T(1,128)}, bf16[1024,2048]{1,0:T(8,128)(2,1)}, bf16[1024,2048]{1,0:T(8,128)(2,1)}, bf16[...) custom-call(bf16[128,2048]{1,0:T(8,128)(2,1)} %get-tuple-element.76.g_own, ...), custom_call_target="tpu_custom_call" | custom-call | flops 1000000 | bytes 100000 | tf_op jit(solution)/shard_map/attend_backward/pallas_call | solution.py:658
  321.1 0.0 copy-start.8
  321.1 88.7 %finish.1 = (f32[128,2048]{1,0:T(8,128)}, f32[128,2048]{1,0:T(8,128)}, f32[11,2048]{1,0:T(8,128)}, f32[1,768]{1,0:T(1,128)}, f32[512,768]{1,0:T(8,128)}, /*index...) custom-call(bf16[1024,2048]{1,0:T(8,128)(2,1)} %get-tuple-element.88, ...), custom_call_target="tpu_custom_call" | custom-call | flops 1000000 | bytes 100000 | tf_op jit(solution)/shard_map/finish/pallas_call | solution.py:1002
  409.7 0.0 copy-done.8
  409.8 0.0 copy-start.5
  409.8 0.0 copy-start.6
  409.8 0.0 copy-start.7
  409.8 0.0 copy-start.10
  409.8 3.5 add_bitcast_fusion
  413.3 0.0 copy-done.5
  413.3 0.0 copy-done.6
  413.3 0.0 copy-done.7
  413.3 0.0 copy-done.10
  413.3 0.6 add_bitcast_fusion.1
  413.9 0.0 copy-start.14
  413.9 0.0 copy-start.15
  413.9 0.0 copy-start.11
  413.9 2.9 maximum_bitcast_fusion
  416.9 0.0 copy-done.14
  416.9 0.0 copy-done.15
  416.9 1.3 convert_add_fusion.1
  418.2 0.1 broadcast_and_fusion
  418.3 0.0 copy-done.11
  418.3 0.4 copy-done.4
  418.7 0.5 copy-done.9
  419.2 2.2 add_bitcast_fusion.3
  421.4 0.0 copy-done.16
  421.4 0.0 copy-done.17
  421.4 0.9 convert_add_fusion.2
  422.2 0.0 copy-done.3
  422.2 0.0 copy-done.13
  422.3 0.0 copy-start.18
  422.3 0.1 convert_add_fusion
  422.4 2.0 reshape.100
  424.4 0.0 copy-done
  424.4 0.2 fusion.6
  424.6 0.0 copy-done.1
  424.6 0.0 copy-done.18
  424.6 2.8 fusion.2
  427.4 0.0 copy-done.2
  427.4 0.0 copy-done.12
  427.4 1.4 fusion.5
  428.8 0.6 slice_bitcast_fusion
  429.4 0.6 fusion.7
  430.1 0.1 reshape.101
  430.1 0.6 constant_dynamic-slice_fusion
  (23 shorter events, 0.1 us)
Async XLA Ops:
  0.6 4.2 copy-start.21
  0.7 5.2 %copy-start.24 = (f32[2,384]{1,0:T(2,128)S(1)}, f32[2,384]{1,0:T(2,128)}, u32[]{:S(2)}) copy-start(f32[2,384]{1,0:T(2,128)} %param.21) | copy-start | bytes 9220
  4.9 89.8 %copy-start.23 = (bf16[2048]{0:T(1024)(128)(2,1)S(1)}, bf16[2048]{0:T(1024)(128)(2,1)}, u32[]{:S(2)}) copy-start(bf16[2048]{0:T(1024)(128)(2,1)} %param.27) | copy-start | bytes 12292
  6.5 88.5 %copy-start.20 = (bf16[2048,8]{0,1:T(8,128)(2,1)S(1)}, bf16[2048,8]{0,1:T(8,128)(2,1)}, u32[]{:S(2)}) copy-start(bf16[2048,8]{0,1:T(8,128)(2,1)} %param.24) | copy-start | bytes 98308
  6.5 90.0 %copy-start.22 = (s32[1024,4]{0,1:T(4,128)S(1)}, s32[1024,4]{0,1:T(4,128)}, u32[]{:S(2)}) copy-start(s32[1024,4]{0,1:T(4,128)} %param.17) | copy-start | bytes 49156
  321.1 88.7 %copy-start.8 = (bf16[1408,512]{1,0:T(8,128)(2,1)S(1)}, bf16[1408,512]{1,0:T(8,128)(2,1)}, u32[]{:S(2)}) copy-start(bf16[1408,512]{1,0:T(8,128)(2,1)} %get-tuple-element.115) | copy-start | bytes 4325380
  409.8 3.6 copy-start.5
  409.8 3.6 copy-start.6
  409.8 3.6 copy-start.7
  409.8 3.6 copy-start.10
  413.9 2.9 copy-start.14
  413.9 2.9 copy-start.15
  413.9 4.3 %copy-start.11 = (bf16[2,704,512]{2,1,0:T(8,128)(2,1)S(1)}, bf16[2,704,512]{2,1,0:T(8,128)(2,1)}, u32[]{:S(2)}) copy-start(bf16[2,704,512]{2,1,0:T(8,128)(2,1)} %get-tuple-element.108) | copy-start | bytes 4325380
  416.8 1.8 copy-start.4
  416.9 2.3 copy-start.9
  419.2 2.2 copy-start.16
  419.2 2.2 copy-start.17
  419.2 3.1 copy-start.3
  419.2 3.1 copy-start.13
  422.3 2.2 copy-start
  422.3 2.3 copy-start.1
  422.3 2.3 copy-start.18
  424.4 3.0 copy-start.2
  424.4 3.0 copy-start.12
  427.4 1.4 copy-start.19
  427.4 2.7 copy-start.25
